TPU v7x, 32 devices: a whole 2x2x4 slice. The times are simulated.
32 devices in a mesh: row: 4 (over x, core), col: 4 (over z), panel: 2 (over y).
Axes of the slice: x: 2, y: 2, z: 4, core: 2. Of those that a mesh axis runs over, the one named last changes fastest.
Arguments:
- velocity: bfloat16 [4608, 6, 1024], P(('row', 'col'), None, 'panel'), may hold values from -6 to 6
- panel_weight: float32 [1024], P('panel'), may hold values from -0.21875 to 0.21875
- panel_group: int32 [1024], P('panel'), may hold values from 0 to 3
- tile_map: int32 [4, 4], replicated, may hold values from 0 to 3
- group_gain: float32 [4, 4], replicated, may hold values from 0.25 to 1
Outputs:
- qtf: float32 [4608, 2, 4608], P(('row', 'panel'), None, 'col')
All inputs are finite; a program needn't handle non-finite values.
Results may differ from a plain program's by a relative error of at most 0.0029.
Values may be sent and summed in bfloat16 or wider, within the bound.
No kernel may reach another device: no remote copies, remote signals or barrier semaphores. Data moves between devices by JAX's collectives and lax.ppermute only.
A program may use at most 64 MiB of HBM per device.

v0:
```python
import jax
import jax.numpy as jnp
from jax import lax
from jax.sharding import PartitionSpec as P


def spread(value, axis, source):
    kept = jnp.where(lax.axis_index(axis) == source, value, 0).astype(value.dtype)
    return lax.psum(kept, axis)


def contract(left_side, right_side):
    return lax.dot_general(
        left_side, right_side, (((1,), (1,)), ((), ())), preferred_element_type=jnp.float32
    )


def pair_products(row_piece, right_side, tile_sign, half_depth):
    left_re = row_piece[:, :half_depth]
    left_im = row_piece[:, half_depth:]
    right_re = right_side[:, :half_depth]
    right_im = right_side[:, half_depth:]
    real_part = contract(left_re, right_re) + tile_sign * contract(left_im, right_im)
    imag_part = contract(left_im, right_re) - tile_sign * contract(left_re, right_im)
    return jnp.stack((real_part, imag_part), axis=1)


def local(velocity, panel_weight, panel_group, tile_map, group_gain):
    row_index = lax.axis_index("row")
    col_index = lax.axis_index("col")
    rows_block = lax.all_gather(velocity, "col", axis=0, tiled=True)
    cols_block = spread(rows_block, "row", col_index)
    chosen = (lax.broadcasted_iota(jnp.int32, tile_map.shape, 0) == row_index) & (
        lax.broadcasted_iota(jnp.int32, tile_map.shape, 1) == col_index
    )
    region = jnp.sum(jnp.where(chosen, tile_map, 0))
    group_count = group_gain.shape[0]
    case_cols = lax.broadcasted_iota(jnp.int32, group_gain.shape, 1)
    case_gains = jnp.sum(jnp.where(case_cols == region, group_gain, jnp.float32(0.0)), axis=1)
    group_ids = lax.broadcasted_iota(jnp.int32, (panel_group.shape[0], group_count), 1)
    panel_gain = jnp.sum(
        jnp.where(panel_group[:, None] == group_ids, case_gains[None, :], jnp.float32(0.0)), axis=1
    )
    panel_scale = panel_weight * panel_gain
    weighted = (rows_block.astype(jnp.float32) * panel_scale[None, None, :]).astype(jnp.bfloat16)
    tile_width = weighted.shape[0]
    slab_size = weighted.shape[2]
    left_side = weighted.reshape(tile_width, 6 * slab_size)
    right_side = cols_block.reshape(cols_block.shape[0], 6 * slab_size)
    tile_sign = jnp.where(row_index <= col_index, jnp.float32(1.0), jnp.float32(-1.0))
    half_depth = 3 * slab_size
    partial_tile = pair_products(left_side, right_side, tile_sign, half_depth)
    result = lax.psum_scatter(partial_tile, "panel", scatter_dimension=0, tiled=True)
    return result


def solution(mesh):
    return jax.shard_map(
        local,
        mesh=mesh,
        in_specs=(P(("row", "col"), None, "panel"), P("panel"), P("panel"), P(), P()),
        out_specs=P(("row", "panel"), None, "col"),
        check_vma=False,
    )
```

profile of v0, /device:TPU:24, one launch (start us, length us, event | category | flops | bytes accessed | tf_op | source)
XLA Modules:
  0.0 457.9 jit_solution(10799057426449021860)
XLA Ops:
  6.5 0.0 all-gather.2.cloned.1.call-start
  6.5 0.7 all-gather.2.cloned.1.call-update
  7.3 0.0 all-reduce.2.cloned.1.call-start
  7.3 127.8 %all-gather.2.cloned.1.call-done = bf16[1152,6,512]{2,0,1:T(8,128)(2,1)} async-done(((bf16[288,6,512]{2,0,1:T(8,128)(2,1)}), bf16[1152,6,512]{2,0,1:T(8,128)(2,1)}) %all-gather.2.cloned.1.call-update) | async-done | bytes 7077904 | tf_op jit(solution)/shard_map/all_gather | solution.py:31
  135.1 10.4 %copy.12 = bf16[1152,6,512]{0,2,1:T(8,128)(2,1)} copy(bf16[1152,6,512]{2,0,1:T(8,128)(2,1)} %all-gather.2.cloned.1.call-done) | data formatting | bytes 14155776 | tf_op jit(solution)/shard_map/all_gather | solution.py:31
  145.6 3.4 broadcast_select_fusion
  149.0 0.0 copy-start.2
  149.0 0.0 copy-start.3
  149.0 0.0 copy-start.4
  149.0 0.0 copy-start.1
  149.0 0.0 all-reduce.2.cloned.1.call-update
  149.0 0.0 reduce-scatter.2.cloned.1.call-start
  149.1 0.6 copy-done.2
  149.7 0.7 select_reduce_fusion.2
  150.4 0.6 iota_compare_fusion.3
  151.0 0.0 copy-done.3
  151.0 0.1 select_reduce_fusion.1
  151.1 0.0 copy-done.4
  151.1 0.1 select_reduce_fusion
  151.2 0.0 copy-done.1
  151.2 7.9 %multiply_convert_fusion = bf16[1152,6,512]{0,2,1:T(8,128)(2,1)} fusion(bf16[1152,6,512]{0,2,1:T(8,128)(2,1)} %copy.12, f32[512]{0:T(512)S(1)} %mul.21), kind=kLoop, calls=%fused_computation | loop fusion | flops 10616832 | bytes 14157824 | tf_op jit(solution)/shard_map/convert_element_type | solution.py:45
  159.2 126.6 %all-reduce.2.cloned.1.call-done = bf16[1152,3072]{0,1:T(8,128)(2,1)} async-done(((bf16[1152,3072]{0,1:T(8,128)(2,1)}), bf16[1152,3072]{0,1:T(8,128)(2,1)}) %all-reduce.2.cloned.1.call-update) | async-done | bytes 7077904 | tf_op jit(solution)/shard_map/psum | solution.py:9
  285.7 8.0 %fusion.6 = f32[1152,1152]{1,0:T(8,128)S(1)} fusion(bf16[1152,3072]{0,1:T(8,128)(2,1)} %bitcast.7, bf16[1152,3072]{0,1:T(8,128)(2,1)} %all-reduce.2.cloned.1.call-done), kind=kOutput, calls=%fused_computation.11 | convolution fusion | flops 4076863488 | bytes 12386304 | tf_op jit(solution)/shard_map/dot_general | solution.py:13
  293.8 0.0 copy-done
  293.8 0.0 copy-done.5
  293.8 7.3 %fusion.10 = f32[1152,1152]{1,0:T(8,128)} fusion(bf16[1152,3072]{0,1:T(8,128)(2,1)S(1)} %copy-done.5, bf16[1152,3072]{0,1:T(8,128)(2,1)S(1)} %bitcast.8), kind=kOutput, calls=%fused_computation.15 | convolution fusion | flops 4076863488 | bytes 12386304 | tf_op jit(solution)/shard_map/dot_general | solution.py:13
  301.1 5.2 %fusion.2 = f32[1152,1,1152]{2,0,1:T(8,128)S(1)} fusion(f32[1152,1152]{1,0:T(8,128)S(1)} %fusion.6, bf16[1152,3072]{0,1:T(8,128)(2,1)S(1)} %copy-done.5, bf16[1152,3072]{0,1:T(8,128)(2,1)S(1)} %bitcast.9, f32[]{:T(128)S(6)} %select_n.29), kind=kOutput, calls=%fused_computation.6 | convolution fusion | flops 4079517696 | bytes 17694724 | tf_op jit(solution)/shard_map/dot_general | solution.py:13
  306.3 7.5 %fusion.3 = f32[1152,1,1152]{2,0,1:T(8,128)S(1)} fusion(f32[1152,1152]{1,0:T(8,128)} %fusion.10, bf16[1152,3072]{0,1:T(8,128)(2,1)S(1)} %copy-done.5, bf16[1152,3072]{0,1:T(8,128)(2,1)S(1)} %bitcast.10, f32[]{:T(128)S(6)} %select_n.29), kind=kOutput, calls=%fused_computation.7 | convolution fusion | flops 4079517696 | bytes 17694724 | tf_op jit(solution)/shard_map/dot_general | solution.py:13
  313.8 4.7 %pad_maximum_fusion = f32[1152,2,1152]{2,0,1:T(8,128)} fusion(f32[1152,1,1152]{2,0,1:T(8,128)S(1)} %fusion.2, f32[1152,1,1152]{2,0,1:T(8,128)S(1)} %fusion.3), kind=kLoop, calls=%fused_computation.1 | loop fusion | flops 2654208 | bytes 21233664 | tf_op jit(solution)/shard_map/stack | solution.py:25
  318.5 0.0 reduce-scatter.2.cloned.1.call-update
  318.5 123.7 %reduce-scatter.2.cloned.1.call-done = f32[576,2,1152]{2,0,1:T(8,128)} async-done(((f32[1152,2,1152]{2,0,1:T(8,128)}), f32[576,2,1152]{2,0,1:T(8,128)}) %reduce-scatter.2.cloned.1.call-update) | async-done | bytes 5308432 | tf_op jit(solution)/shard_map/reduce_scatter | solution.py:53
  442.2 9.2 %copy.14 = f32[576,2,1152]{2,1,0:T(2,128)} copy(f32[576,2,1152]{2,0,1:T(8,128)} %reduce-scatter.2.cloned.1.call-done) | data formatting | bytes 10616832 | tf_op jit(solution)/shard_map/reduce_scatter | solution.py:53
  (4 shorter events, 0.0 us)
Async XLA Ops:
  6.5 128.6 %all-gather.2.cloned.1.call-start = ((), (), s32[]{:S(2)}) async-start(), calls=%async_computation.1 | async-start | bytes 8847360 | tf_op jit(solution)/shard_map/all_gather | solution.py:31
  7.3 278.5 %all-reduce.2.cloned.1.call-start = ((), (), s32[]{:S(2)}) async-start(), calls=%async_computation.2 | async-start | bytes 14155776 | tf_op jit(solution)/shard_map/psum | solution.py:9
  149.0 0.7 copy-start.2
  149.0 2.0 copy-start.3
  149.0 2.2 copy-start.4
  149.0 2.2 copy-start.1
  149.0 293.1 %reduce-scatter.2.cloned.1.call-start = ((), (), s32[]{:S(2)}) async-start(), calls=%async_computation.3 | async-start | bytes 15925248 | tf_op jit(solution)/shard_map/reduce_scatter | solution.py:53
  285.7 8.0 %copy-start = (bf16[1152,6,512]{0,2,1:T(8,128)(2,1)S(1)}, bf16[1152,6,512]{0,2,1:T(8,128)(2,1)}, u32[]{:S(2)}) copy-start(bf16[1152,6,512]{0,2,1:T(8,128)(2,1)} %multiply_convert_fusion) | copy-start | bytes 21233668
  285.7 8.0 %copy-start.5 = (bf16[1152,3072]{0,1:T(8,128)(2,1)S(1)}, bf16[1152,3072]{0,1:T(8,128)(2,1)}, u32[]{:S(2)}) copy-start(bf16[1152,3072]{0,1:T(8,128)(2,1)} %all-reduce.2.cloned.1.call-done) | copy-start | bytes 21233668
Sparse Core Ops, SparseCore 0:
  8.9 126.1 all-gather.1
  149.1 136.5 all-reduce.1
  318.6 123.5 reduce-scatter.1
where the time goes:
time: 460 us; the launch traced here: 458 us
  waiting for transfers between devices  379 us (82%)
  matrix products  28 us (6%)
  local copies, waits for them, and re-layouts  20.2 us (4%)
  other arithmetic  17.6 us (4%)
  between operations  13.2 us (3%)
    all_gather x1, waiting for transfers between devices, local(): rows_block = lax.all_gather(velocity, 'col', axis=0, tiled=True)  128 us
    psum x1, waiting for transfers between devices, spread(): return lax.psum(kept, axis)  127 us
    reduce_scatter x1, waiting for transfers between devices, local(): lax.psum_scatter(partial_tile, 'panel', scatter_dimension=0, tiled=True)  124 us
    dot_general x4, matrix products, contract(): lax.dot_general(left_side, right_side, (((1,), (1,)), ((), ())), preferre...  28 us
    all_gather x1, local copies, waits for them, and re-layouts, local(): rows_block = lax.all_gather(velocity, 'col', axis=0, tiled=True)  10.4 us
  transfers between devices with their start and end apart: 3, of which 3 were waited for; matrix products, arithmetic and copies ran while one was open for 2% of the time, Pallas kernels for 0%

commit v1 on v0

v1 whole, which is shorter than its diff:
```python
import functools

import jax
import jax.numpy as jnp
import numpy as np
from jax import lax
from jax.experimental import pallas as pl
from jax.experimental.pallas import tpu as pltpu
from jax.sharding import PartitionSpec as P

LANES = 128
SENDS = ((2, 4), (3, 4), (4, 4), (5, 4), (6, 4))


def route(n):
    step = lambda r: -1 if r % 2 == 0 else 1
    behind = lambda j, d: j if d == 1 else n - 1 - j
    moves = {"own": (0, None, [])}
    holds = {"own": {(r, j): j for r in range(n) for j in range(n)}}

    def add(name, slot, source, pairs):
        moves[name] = (slot, source, pairs)
        holds[name] = {b: holds[source][a] for a, b in pairs}

    def hops(sign, keep):
        return [
            ((r, j), (r, j + sign * step(r)))
            for r in range(n)
            for j in range(n)
            if 0 <= j + sign * step(r) < n and keep(behind(j, sign * step(r)))
        ]

    for t in range(1, n):
        add(f"p{t}", t, "own" if t == 1 else f"p{t - 1}", hops(1, lambda b: b >= t - 1))
    for m in range(1, n):
        for t in range(1, m + 1):
            add(f"q{m}_{t}", m + t, "own" if t == 1 else f"q{m - 1}_{t - 1}", hops(-1, lambda b: b + 1 == m))
    rows = {}
    for name, held in holds.items():
        for device, plane in held.items():
            rows.setdefault(device, {})[plane] = (moves[name][0], name)
    cols = {}
    spreads = {}
    for name, held in holds.items():
        slot = moves[name][0]
        for c in range(n):
            if (c, c) not in held:
                continue
            cols.setdefault((c, c), {})[held[c, c]] = (slot, name)
            for v in range(1, n):
                parent = v & (v - 1)
                source = f"{name}_v{parent}" if parent else name
                late = slot + bin(v >> 1).count("1")
                spreads.setdefault(f"{name}_v{v}", (late, source, []))[2].append(((c ^ parent, c), (c ^ v, c)))
                cols.setdefault((c ^ v, c), {})[held[c, c]] = (late, f"{name}_v{v}")
    return moves, spreads, rows, cols


def share_out(n, rows, cols):
    half = n // 2
    slots = sorted({s for s, _ in SENDS})
    tasks, send_pairs, arrives = {}, [[] for _ in SENDS], {}
    for r in range(n):
        for j in range(n):
            for y in range(2):
                ready = sorted(
                    (max(rows[r, j][kr][0], cols[r, j][kc][0]), kr, kc) for kr in range(n) for kc in range(n)
                )
                left = [b for b in ready if b[1] // half != y]
                for index, (slot, cap) in enumerate(SENDS):
                    able = [b for b in left if b[0] <= slot]
                    if not able or (len(able) < min(cap, len(left)) and index < len(SENDS) - 1):
                        continue
                    for place, b in enumerate(able[:cap]):
                        left.remove(b)
                        tasks.setdefault((r, j, y, slot), []).append((b[1], b[2], 1 + index, place))
                        arrives[r, j, 1 - y, b[1], b[2]] = (index, place)
                    send_pairs[index].append((r, j, y))
                assert not left
                for b in ready:
                    if b[1] // half == y:
                        slot = min(s for s in slots if s >= b[0])
                        place = (b[1] - y * half) * n + b[2]
                        tasks.setdefault((r, j, y, slot), []).append((b[1], b[2], 0, place))
    return slots, tasks, send_pairs, arrives


def rate(w_ref, group_ref, gain_ref, region):
    groups = group_ref[...]
    gain = jnp.zeros(groups.shape, jnp.float32)
    for g in range(gain_ref.shape[0]):
        gain = gain + jnp.where(groups == g, gain_ref[g, region], jnp.float32(0.0))
    return w_ref[...] * gain


def fetch(index, sources, kept, target, sem, h, p, gap):
    def pull(source):
        for c in range(6):
            pltpu.make_async_copy(
                source.at[c], target.at[pl.ds((c // 3) * gap, h), pl.ds((c % 3) * p, p)], sem
            ).start()

    for i, source in enumerate(sources):

        @pl.when(index == i)
        def _():
            pull(source)

    @pl.when(index >= len(sources))
    def _():
        pull(kept.at[index - len(sources)])


def landed(sources, target, sem, h, p, gap):
    for c in range(6):
        pltpu.make_async_copy(
            sources[0].at[c], target.at[pl.ds((c // 3) * gap, h), pl.ds((c % 3) * p, p)], sem
        ).wait()


def pack(stage, real, imag, h):
    tail, quarter = h % LANES, h // 2
    full = h // LANES
    for part, value in ((0, real), (1, imag)):
        for k in range(full):
            stage[pl.ds((part * full + k) * h, h), :] = value[:, k * LANES:(k + 1) * LANES].astype(stage.dtype)
        for fold in range(2):
            lane = (2 * fold + part) * tail
            stage[pl.ds(2 * full * h, quarter), lane:lane + tail] = value[
                fold * quarter:(fold + 1) * quarter, full * LANES:
            ].astype(stage.dtype)


def multiply_blocks(
    first, base, keeps, sources, caps, h, p, gap, table, tile_map, gain_ref, w_ref, group_ref, *refs
):
    srcs = refs[:sources]
    refs = refs[sources:] if first else refs[sources + 2:]
    own, kept = refs[:2]
    outs = refs[2:2 + len(caps)]
    left, right, stage_own, stage_out, l_sem, r_sem, o_sem, k_sem = refs[2 + len(caps):]
    count = table[base]
    copies = table[keeps]

    def keep(t, carry):
        code = table[keeps + 1 + t]
        for i, source in enumerate(srcs):

            @pl.when((code & 63) == i)
            def _():
                pltpu.make_async_copy(source, kept.at[code >> 6], k_sem).start()

        return carry

    lax.fori_loop(0, copies, keep, 0)
    sign = table[2].astype(jnp.float32)
    scale = rate(w_ref, group_ref, gain_ref, tile_map[table[0], table[1]])

    def entry(t):
        code = table[base + 1 + t]
        return code & 63, (code >> 6) & 63, (code >> 12) & 15, code >> 16

    @pl.when(count > 0)
    def _():
        fetch(entry(0)[1], srcs, kept, right.at[0], r_sem.at[0], h, p, gap)

    def task(t, before):
        row, col, kind, place = entry(t)
        slot = lax.rem(t, 2)

        @pl.when(row != before)
        def _():
            fetch(row, srcs, kept, left, l_sem, h, p, h)
            landed(srcs, left, l_sem, h, p, h)
            for c in range(3):
                raw = left[:, c * p:(c + 1) * p].astype(jnp.float32)
                left[:, c * p:(c + 1) * p] = (raw * scale).astype(jnp.bfloat16)

        @pl.when(t + 1 < count)
        def _():
            fetch(entry(t + 1)[1], srcs, kept, right.at[1 - slot], r_sem.at[1 - slot], h, p, gap)

        landed(srcs, right.at[slot], r_sem.at[slot], h, p, gap)
        product = lax.dot_general(
            left[...], right[slot], (((1,), (1,)), ((), ())), preferred_element_type=jnp.float32
        )
        real = product[:h, :h] + sign * product[h:, gap:gap + h]
        imag = product[h:, :h] - sign * product[:h, gap:gap + h]

        @pl.when(kind == 0)
        def _():
            pack(stage_own, real, imag, h)
            copy = pltpu.make_async_copy(stage_own, own.at[place], o_sem)
            copy.start()
            copy.wait()

        for k, out in enumerate(outs):

            @pl.when(kind == k + 1)
            def _():
                pack(stage_out, real, imag, h)
                copy = pltpu.make_async_copy(stage_out, out.at[place], o_sem)
                copy.start()
                copy.wait()

        return row

    lax.fori_loop(0, count, task, jnp.int32(-1))

    def finish(t, carry):
        pltpu.make_async_copy(srcs[0], kept.at[0], k_sem).wait()
        return carry

    lax.fori_loop(0, copies, finish, 0)


def add_up(base, n, h, table, own, *refs):
    recvs = refs[:len(SENDS)]
    out, mine, theirs, real, imag, image, m_sem, t_sem, o_sem = refs[len(SENDS):]
    blocks = (n // 2) * n
    full, tail, quarter = h // LANES, h % LANES, h // 2
    wide = n * h // LANES

    def load(b, slot):
        pltpu.make_async_copy(own.at[b], mine.at[slot], m_sem.at[slot]).start()
        code = table[base + b]
        for k, recv in enumerate(recvs):

            @pl.when((code & 15) == k)
            def _():
                pltpu.make_async_copy(recv.at[code >> 4], theirs.at[slot], t_sem.at[slot]).start()

    def written(chunk, k):
        return pltpu.make_async_copy(
            image.at[chunk % 2, pl.ds(2 * k * h, 2 * h)].reshape(h, 2, LANES),
            out.at[pl.ds(chunk * h, h), :, pl.ds(k * LANES, LANES)],
            o_sem.at[chunk % 2],
        )

    load(0, 0)
    for b in range(blocks):
        slot, chunk, kc = b % 2, b // n, b % n
        if b + 1 < blocks:
            load(b + 1, 1 - slot)
        pltpu.make_async_copy(own.at[0], mine.at[slot], m_sem.at[slot]).wait()
        pltpu.make_async_copy(recvs[0].at[0], theirs.at[slot], t_sem.at[slot]).wait()
        for part, line in ((0, real), (1, imag)):
            for k in range(full):
                at = pl.ds((part * full + k) * h, h)
                line[:, kc * h + k * LANES:kc * h + (k + 1) * LANES] = mine[slot, at, :] + theirs[
                    slot, at, :
                ].astype(jnp.float32)
            at = pl.ds(2 * full * h, quarter)
            rest = mine[slot, at, :] + theirs[slot, at, :].astype(jnp.float32)
            for fold in range(2):
                lane = (2 * fold + part) * tail
                line[
                    fold * quarter:(fold + 1) * quarter, kc * h + full * LANES:(kc + 1) * h
                ] = rest[:, lane:lane + tail]
        if kc == n - 1:
            buf = chunk % 2
            for part, line in ((0, real), (1, imag)):
                for k in range(wide):
                    image[buf, pl.ds(2 * k * h + part, h, stride=2), :] = line[:, k * LANES:(k + 1) * LANES]
            for k in range(wide):
                written(chunk, k).start()
    for chunk in range(n // 2):
        for k in range(wide):
            written(chunk, k).wait()


def tiled(mesh, h, p):
    n = mesh.shape["col"]
    half = n // 2
    moves, spreads, rows, cols = route(n)
    slots, tasks, send_pairs, arrives = share_out(n, rows, cols)
    gap = -(-h // LANES) * LANES
    block = 2 * h * h // LANES

    event = lambda slot: min(s for s in slots if s >= slot)
    parts = lambda r, j, kr, kc: ((*rows[r, j][kr], kr), (*cols[r, j][kc], n + kc))
    names = {s: {"own"} for s in slots}
    keeps = {}
    for (r, j, y, s), items in tasks.items():
        for kr, kc, _, _ in items:
            for slot, name, place in parts(r, j, kr, kc):
                names[event(slot)].add(name)
                if event(slot) < s and name != "own":
                    keeps.setdefault((r, j, y, event(slot)), set()).add((name, place))
    names = {s: sorted(v) for s, v in names.items()}
    most = {s: max(len(v) for k, v in tasks.items() if k[3] == s) for s in slots}
    kept_most = {s: max([len(v) for k, v in keeps.items() if k[3] == s], default=0) for s in slots}
    bases, kept_bases, size = {}, {}, 3
    for s in slots:
        bases[s] = size
        kept_bases[s] = size + 1 + most[s]
        size += 2 + most[s] + kept_most[s]
    final = size
    size += half * n
    table = np.zeros((n, n, 2, size), np.int32)
    for r in range(n):
        for j in range(n):
            for y in range(2):
                line = table[r, j, y]
                line[:3] = r, j, 1 if r <= j else -1
                for s in slots:
                    items = sorted(tasks.get((r, j, y, s), []), key=lambda i: (rows[r, j][i[0]][0], i[0], -i[2], i[3]))
                    line[bases[s]] = len(items)
                    for t, (kr, kc, kind, place) in enumerate(items):
                        code = 0
                        for shift, (slot, name, where) in zip((0, 6), parts(r, j, kr, kc)):
                            near = name == "own" or event(slot) == s
                            code |= (names[s].index(name) if near else len(names[s]) + where) << shift
                        local = 0 if kind == 0 else 1 + [i for i, x in enumerate(SENDS) if x[0] == s].index(kind - 1)
                        line[bases[s] + 1 + t] = code | local << 12 | place << 16
                    moved = sorted(keeps.get((r, j, y, s), ()))
                    line[kept_bases[s]] = len(moved)
                    for t, (name, where) in enumerate(moved):
                        line[kept_bases[s] + 1 + t] = names[s].index(name) | where << 6
                for i in range(half):
                    for kc in range(n):
                        index, place = arrives[r, j, y, y * half + i, kc]
                        line[final + i * n + kc] = index | place << 4

    def permute(x, pairs):
        return lax.ppermute(x, ("row", "col"), [(a[0] * n + a[1], b[0] * n + b[1]) for a, b in pairs])

    def tie(x, *others):
        return lax.optimization_barrier((x, *others))[0] if others else x

    def local(velocity, panel_weight, panel_group, tile_map, group_gain):
        place = lax.axis_index("row"), lax.axis_index("col"), lax.axis_index("panel")
        line = lax.dynamic_slice(jnp.asarray(table), (*place, 0), (1, 1, 1, size)).reshape(size)
        have = {"own": jnp.transpose(velocity, (1, 0, 2))}
        weight, group = panel_weight[None, :], panel_group[None, :]
        own, kept, recvs, sents = None, None, [], {}
        last = max(s for s, _, _ in moves.values())
        for slot in range(0, last + 2):
            held = [have[k] for k, m in moves.items() if m[0] == slot - 1 and k != "own"]
            done = sents.get(slot - 2, [])
            for name, (s, source, pairs) in moves.items():
                if s == slot and source is not None:
                    x = have[source]
                    have[name] = permute(tie(x, *done, *(held if name[0] == "q" else [])), pairs)
            for name, (s, source, pairs) in spreads.items():
                if s == slot:
                    have[name] = permute(tie(have[source], *done), pairs)
            if slot not in slots:
                continue
            caps = [c for s, c in SENDS if s == slot]
            first = own is None
            used = [have[k] for k in names[slot]]
            anywhere = pl.BlockSpec(memory_space=pltpu.HBM)
            flops = 4 * 2 * h * h * 6 * p * max(1, most[slot] // 2)
            made = pl.pallas_call(
                functools.partial(multiply_blocks, first, bases[slot], kept_bases[slot], len(used), caps, h, p, gap),
                out_shape=[
                    jax.ShapeDtypeStruct((half * n, block, LANES), jnp.float32),
                    jax.ShapeDtypeStruct((2 * n, 6, h, p), jnp.bfloat16),
                ]
                + [jax.ShapeDtypeStruct((c, block, LANES), jnp.bfloat16) for c in caps],
                in_specs=[pl.BlockSpec(memory_space=pltpu.SMEM)] * 3
                + [pl.BlockSpec(memory_space=pltpu.VMEM)] * 2
                + [anywhere] * (len(used) + (0 if first else 2)),
                out_specs=[anywhere] * (2 + len(caps)),
                input_output_aliases={} if first else {5 + len(used): 0, 6 + len(used): 1},
                scratch_shapes=[
                    pltpu.VMEM((2 * h, 3 * p), jnp.bfloat16),
                    pltpu.VMEM((2, gap + h, 3 * p), jnp.bfloat16),
                    pltpu.VMEM((block, LANES), jnp.float32),
                    pltpu.VMEM((block, LANES), jnp.bfloat16),
                    pltpu.SemaphoreType.DMA,
                    pltpu.SemaphoreType.DMA((2,)),
                    pltpu.SemaphoreType.DMA,
                    pltpu.SemaphoreType.DMA,
                ],
                compiler_params=pltpu.CompilerParams(vmem_limit_bytes=60 << 20),
                cost_estimate=pl.CostEstimate(flops=flops, bytes_accessed=8 << 20, transcendentals=0),
                name=f"blocks_{slot}",
            )(line, tile_map, group_gain, weight, group, *used, *([] if first else [own, kept]))
            own, kept = made[:2]
            sents[slot] = made[2:3]
            for sent in made[2:]:
                pairs = []
                for r, j, y in send_pairs[len(recvs)]:
                    pairs.append(((r * n + j) * 2 + y, (r * n + j) * 2 + 1 - y))
                recvs.append(lax.ppermute(sent, ("row", "col", "panel"), pairs))
        wide = n * h // LANES
        return pl.pallas_call(
            functools.partial(add_up, final, n, h),
            out_shape=jax.ShapeDtypeStruct((half * h, 2, n * h), jnp.float32),
            in_specs=[pl.BlockSpec(memory_space=pltpu.SMEM)]
            + [pl.BlockSpec(memory_space=pltpu.HBM)] * (1 + len(recvs)),
            out_specs=pl.BlockSpec(memory_space=pltpu.HBM),
            scratch_shapes=[
                pltpu.VMEM((2, block, LANES), jnp.float32),
                pltpu.VMEM((2, block, LANES), jnp.bfloat16),
                pltpu.VMEM((h, n * h), jnp.float32),
                pltpu.VMEM((h, n * h), jnp.float32),
                pltpu.VMEM((2, h * 2 * wide, LANES), jnp.float32),
                pltpu.SemaphoreType.DMA((2,)),
                pltpu.SemaphoreType.DMA((2,)),
                pltpu.SemaphoreType.DMA((2,)),
            ],
            compiler_params=pltpu.CompilerParams(vmem_limit_bytes=60 << 20),
            name="add_up",
        )(line, own, *recvs)

    return local


def contract(left_side, right_side):
    return lax.dot_general(
        left_side, right_side, (((1,), (1,)), ((), ())), preferred_element_type=jnp.float32
    )


def plain(velocity, panel_weight, panel_group, tile_map, group_gain):
    row_index, col_index = lax.axis_index("row"), lax.axis_index("col")
    rows_block = lax.all_gather(velocity, "col", axis=0, tiled=True)
    kept = jnp.where(row_index == col_index, rows_block, 0).astype(rows_block.dtype)
    cols_block = lax.psum(kept, "row")
    gains = lax.dynamic_index_in_dim(group_gain, tile_map[row_index, col_index], 1, keepdims=False)
    scale = panel_weight * gains[panel_group]
    weighted = (rows_block.astype(jnp.float32) * scale[None, None, :]).astype(jnp.bfloat16)
    width, depth = weighted.shape[0], 3 * weighted.shape[2]
    left = weighted.reshape(width, 2 * depth)
    right = cols_block.reshape(width, 2 * depth)
    sign = jnp.where(row_index <= col_index, jnp.float32(1.0), jnp.float32(-1.0))
    real = contract(left[:, :depth], right[:, :depth]) + sign * contract(left[:, depth:], right[:, depth:])
    imag = contract(left[:, depth:], right[:, :depth]) - sign * contract(left[:, :depth], right[:, depth:])
    return lax.psum_scatter(jnp.stack((real, imag), axis=1), "panel", scatter_dimension=0, tiled=True)


def solution(mesh):
    n, panels = mesh.shape["col"], mesh.shape["panel"]

    def whole(velocity, panel_weight, panel_group, tile_map, group_gain):
        h = velocity.shape[0] // (n * n)
        p = velocity.shape[2] // panels
        fits = (
            mesh.shape["row"] == n
            and n == 4
            and panels == 2
            and h % 32 == 0
            and (h % LANES) * 4 == LANES
            and (n * h) % LANES == 0
            and p % LANES == 0
        )
        return jax.shard_map(
            tiled(mesh, h, p) if fits else plain,
            mesh=mesh,
            in_specs=(P(("row", "col"), None, "panel"), P("panel"), P("panel"), P(), P()),
            out_specs=P(("row", "panel"), None, "col"),
            check_vma=False,
        )(velocity, panel_weight, panel_group, tile_map, group_gain)

    return whole
```

time: 460 us -> 629 us (1.37)
  Pallas kernels: 0 us -> 323 us
  waiting for transfers between devices: 379 us -> 245 us
  starting transfers between devices: 0.08 us -> 51.6 us
  matrix products: 28 us -> 0 us
  other arithmetic: 17.6 us -> 0 us
  local copies, waits for them, and re-layouts: 20.2 us -> 4.89 us
  between operations: 13.2 us -> 0.52 us
    pallas_call x0 -> x6, Pallas kernels: none -> 323 us  [the longest x5 314 us: local(): pl.pallas_call(functools.partial(multiply_blocks, first, bases[slot], kep...]
    ppermute x0 -> x32, waiting for transfers between devices: none -> 245 us  [the longest x27 217 us: permute(): lax.ppermute(x, ('row', 'col'), [(a[0] * n + a[1], b[0] * n + b[1]) for a...]
    all_gather x1 -> x0, waiting for transfers between devices: 128 us -> none  [local(): rows_block = lax.all_gather(velocity, 'col', axis=0, tiled=True)]
    psum x1 -> x0, waiting for transfers between devices: 127 us -> none  [spread(): return lax.psum(kept, axis)]
    reduce_scatter x1 -> x0, waiting for transfers between devices: 124 us -> none  [local(): lax.psum_scatter(partial_tile, 'panel', scatter_dimension=0, tiled=True)]
    ppermute x0 -> x32, starting transfers between devices: none -> 51.6 us  [the longest x27 40.8 us: permute(): lax.ppermute(x, ('row', 'col'), [(a[0] * n + a[1], b[0] * n + b[1]) for a...]
    dot_general x4 -> x0, matrix products: 28 us -> none  [contract(): lax.dot_general(left_side, right_side, (((1,), (1,)), ((), ())), preferre...]
    all_gather x1 -> x0, local copies, waits for them, and re-layouts: 10.4 us -> none  [local(): rows_block = lax.all_gather(velocity, 'col', axis=0, tiled=True)]
  transfers between devices with their start and end apart: 3 -> 32, of which waited for: 3 -> 7; matrix products, arithmetic and copies ran while one was open for 2% -> 0% of each run, Pallas kernels for 0% -> 50%
where the time goes in v1:
time: 629 us; the launch traced here: 625 us
  Pallas kernels  323 us (51%)
  waiting for transfers between devices  245 us (39%)
  starting transfers between devices  51.6 us (8%)
    pallas_call x5, Pallas kernels, local(): pl.pallas_call(functools.partial(multiply_blocks, first, bases[slot], kep...  314 us
    ppermute x27, waiting for transfers between devices, permute(): lax.ppermute(x, ('row', 'col'), [(a[0] * n + a[1], b[0] * n + b[1]) for a...  217 us
    ppermute x27, starting transfers between devices, permute(): lax.ppermute(x, ('row', 'col'), [(a[0] * n + a[1], b[0] * n + b[1]) for a...  40.8 us
    ppermute x5, waiting for transfers between devices, local(): recvs.append(lax.ppermute(sent, ('row', 'col', 'panel'), pairs))  28.2 us
  transfers between devices with their start and end apart: 32, of which 7 were waited for; matrix products, arithmetic and copies ran while one was open for 0% of the time, Pallas kernels for 50%

profile of v1, /device:TPU:24, one launch (start us, length us, event | category | flops | bytes accessed | tf_op | source)
XLA Modules:
  0.0 625.1 jit_solution(6219541270659467391)
XLA Ops:
  0.0 2.5 collective-permute-start
  3.2 19.4 %collective-permute-done.refs_4_ = bf16[6,288,512]{2,1,0:T(8,128)(2,1)S(1)} collective-permute-done((bf16[6,288,512]{2,1,0:T(8,128)(2,1)}, bf16[6,288,512]{2,1,0:T(8,128)(2,1)S(1)}, u32[]{:S(2)}, u32[]{:S(2)}) %collective-permute-start) | collective-permute-done | bytes 1769504 | tf_op jit(solution)/shard_map/ppermute | solution.py:326
  25.0 1.9 collective-permute-start.6
  27.7 1.3 collective-permute-start.4
  29.0 1.9 collective-permute-start.11
  31.7 2.0 collective-permute-start.19
  33.7 1.9 collective-permute-start.9
  35.6 14.3 %collective-permute-done.4.refs_3_ = bf16[6,288,512]{2,1,0:T(8,128)(2,1)S(1)} collective-permute-done((bf16[6,288,512]{2,1,0:T(8,128)(2,1)S(1)}, bf16[6,288,512]{2,1,0:T(8,128)(2,1)S(1)}, u32[]{:S(2)}, u32[]{:S(2)}) %collective-permute-start.4) | collective-permute-done | bytes 1769504 | tf_op jit(solution)/shard_map/ppermute | solution.py:326
  51.2 1.9 collective-permute-start.22
  53.1 1.9 collective-permute-start.21
  57.6 2.7 collective-permute-done.7.refs_7_
  60.3 109.2 %blocks_2.1 = (f32[8,1296,128]{2,1,0:T(8,128)}, bf16[8,6,288,512]{3,2,1,0:T(8,128)(2,1)}, bf16[4,1296,128]{2,1,0:T(8,128)(2,1)}) custom-call(s32[67]{0:T(128)} %dynamic-slice_bitcast_fusion.table, s32[4,4]{1,0:T(4,128)} %tile_map.9, f32[4,4]{1,0:T(4,128)} %gain_ref.9, f32[1,512]{1,0:T(1,128)} %bitcast.16, s32[1,512]{1,0:T(1,128)} %bitcast.21, ...), custom_call_target="tpu_custom_call" | custom-call | flops 8153726976 | bytes 8388608 | tf_op jit(solution)/shard_map/blocks_2/pallas_call | solution.py:355
  169.5 1.9 collective-permute-start.12
  171.5 1.9 collective-permute-start.15
  173.3 1.9 collective-permute-start.13
  176.5 55.6 %blocks_3.1 = (f32[8,1296,128]{2,1,0:T(8,128)}, bf16[8,6,288,512]{3,2,1,0:T(8,128)(2,1)}, bf16[4,1296,128]{2,1,0:T(8,128)(2,1)}) custom-call(s32[67]{0:T(128)} %dynamic-slice_bitcast_fusion.table, s32[4,4]{1,0:T(4,128)} %tile_map.9, f32[4,4]{1,0:T(4,128)} %gain_ref.9, f32[1,512]{1,0:T(1,128)} %bitcast.17, ...), custom_call_target="tpu_custom_call", output_to_operand_aliasing={{0}: (12, {}), {1}: (13, {})} | custom-call | flops 8153726976 | bytes 8388608 | tf_op jit(solution)/shard_map/blocks_3/pallas_call | solution.py:355
  232.2 2.0 collective-permute-start.25
  234.1 1.9 collective-permute-start.17
  236.1 1.9 collective-permute-start.16
  239.2 31.7 %collective-permute-done.18.refs_7_ = bf16[6,288,512]{2,1,0:T(8,128)(2,1)} collective-permute-done((bf16[6,288,512]{2,1,0:T(8,128)(2,1)S(1)}, bf16[6,288,512]{2,1,0:T(8,128)(2,1)}, u32[]{:S(2)}, u32[]{:S(2)}) %collective-permute-start.18) | collective-permute-done | bytes 1769504 | tf_op jit(solution)/shard_map/ppermute | solution.py:326
  272.2 1.9 collective-permute-start.26
  274.1 148.9 %collective-permute-done.14.refs_2_ = bf16[6,288,512]{2,1,0:T(8,128)(2,1)S(1)} collective-permute-done((bf16[6,288,512]{2,1,0:T(8,128)(2,1)}, bf16[6,288,512]{2,1,0:T(8,128)(2,1)S(1)}, u32[]{:S(2)}, u32[]{:S(2)}) %collective-permute-start.14) | collective-permute-done | bytes 1769504 | tf_op jit(solution)/shard_map/ppermute | solution.py:326
  424.2 109.2 %blocks_4.1 = (f32[8,1296,128]{2,1,0:T(8,128)}, bf16[8,6,288,512]{3,2,1,0:T(8,128)(2,1)}, bf16[4,1296,128]{2,1,0:T(8,128)(2,1)}) custom-call(s32[67]{0:T(128)} %dynamic-slice_bitcast_fusion.table, s32[4,4]{1,0:T(4,128)} %tile_map.9, f32[4,4]{1,0:T(4,128)} %gain_ref.9, f32[1,512]{1,0:T(1,128)} %bitcast.18, ...), custom_call_target="tpu_custom_call", output_to_operand_aliasing={{0}: (13, {}), {1}: (14, {})} | custom-call | flops 8153726976 | bytes 8388608 | tf_op jit(solution)/shard_map/blocks_4/pallas_call | solution.py:355
  536.7 1.7 collective-permute-start.28
  538.5 2.4 collective-permute-start.29
  540.9 26.6 %blocks_5.1 = (f32[8,1296,128]{2,1,0:T(8,128)}, bf16[8,6,288,512]{3,2,1,0:T(8,128)(2,1)}, bf16[4,1296,128]{2,1,0:T(8,128)(2,1)}) custom-call(s32[67]{0:T(128)} %dynamic-slice_bitcast_fusion.table, s32[4,4]{1,0:T(4,128)} %tile_map.9, f32[4,4]{1,0:T(4,128)} %gain_ref.9, f32[1,512]{1,0:T(1,128)} %bitcast.19, ...), custom_call_target="tpu_custom_call", output_to_operand_aliasing={{0}: (9, {}), {1}: (10, {})} | custom-call | flops 8153726976 | bytes 8388608 | tf_op jit(solution)/shard_map/blocks_5/pallas_call | solution.py:355
  568.7 13.4 %blocks_6.1 = (f32[8,1296,128]{2,1,0:T(8,128)}, bf16[8,6,288,512]{3,2,1,0:T(8,128)(2,1)}, bf16[4,1296,128]{2,1,0:T(8,128)(2,1)}) custom-call(s32[67]{0:T(128)} %dynamic-slice_bitcast_fusion.table, s32[4,4]{1,0:T(4,128)} %tile_map.9, f32[4,4]{1,0:T(4,128)} %gain_ref.9, f32[1,512]{1,0:T(1,128)} %bitcast.20, ...), custom_call_target="tpu_custom_call", output_to_operand_aliasing={{0}: (7, {}), {1}: (8, {})} | custom-call | flops 4076863488 | bytes 8388608 | tf_op jit(solution)/shard_map/blocks_6/pallas_call | solution.py:355
  582.1 1.3 collective-permute-start.31
  583.4 4.6 collective-permute-start.30
  588.0 13.9 %collective-permute-done.31.refs_4_ = bf16[4,1296,128]{2,1,0:T(8,128)(2,1)S(1)} collective-permute-done((bf16[4,1296,128]{2,1,0:T(8,128)(2,1)}, bf16[4,1296,128]{2,1,0:T(8,128)(2,1)S(1)}, u32[]{:S(2)}, u32[]{:S(2)}) %collective-permute-start.31) | collective-permute-done | bytes 1327136 | tf_op jit(solution)/shard_map/ppermute | solution.py:387
  602.0 14.3 %collective-permute-done.30.refs_3_ = bf16[4,1296,128]{2,1,0:T(8,128)(2,1)} collective-permute-done((bf16[4,1296,128]{2,1,0:T(8,128)(2,1)}, bf16[4,1296,128]{2,1,0:T(8,128)(2,1)}, u32[]{:S(2)}, u32[]{:S(2)}) %collective-permute-start.30) | collective-permute-done | bytes 1327136 | tf_op jit(solution)/shard_map/ppermute | solution.py:387
  616.3 8.7 %add_up.1 = f32[576,2,1152]{2,1,0:T(2,128)} custom-call(s32[67]{0:T(128)} %dynamic-slice_bitcast_fusion.table, f32[8,1296,128]{2,1,0:T(8,128)} %get-tuple-element.56.own, bf16[4,1296,128]{2,1,0:T(8,128)(2,1)} %copy-done.4, bf16[4,1296,128]{2,1,0:T(8,128)(2,1)} %collective-permute-done.28.refs_1_, bf16[4,1296,128]{2,1,0:T(8,128)(2,1)} %collective-permute-done.29.refs_2_, ...), custom_call_target="tpu_custom_call" | custom-call | tf_op jit(solution)/shard_map/add_up/pallas_call | solution.py:389
  (67 shorter events, 18.0 us)
Async XLA Ops:
  0.0 22.7 %collective-permute-start = (bf16[6,288,512]{2,1,0:T(8,128)(2,1)}, bf16[6,288,512]{2,1,0:T(8,128)(2,1)S(1)}, u32[]{:S(2)}, u32[]{:S(2)}) collective-permute-start(bf16[6,288,512]{2,1,0:T(8,128)(2,1)} %bitcast.5), channel_id=1, source_target_pairs={{2,0},{4,2},{6,4},{8,10},{10,12},{12,14},{18,16},{20,18},{22,20},{... | collective-permute-start | bytes 5308424 | tf_op jit(solution)/shard_map/ppermute | solution.py:326
  2.5 24.4 %collective-permute-start.3 = (bf16[6,288,512]{2,1,0:T(8,128)(2,1)}, bf16[6,288,512]{2,1,0:T(8,128)(2,1)S(1)}, u32[]{:S(2)}, u32[]{:S(2)}) collective-permute-start(bf16[6,288,512]{2,1,0:T(8,128)(2,1)} %bitcast.6), channel_id=1, source_target_pairs={{0,16},{10,26},{20,4},{30,14},{1,17},{11,27},{21,5},{31,15}} | collective-permute-start | bytes 5308424 | tf_op jit(solution)/shard_map/ppermute | solution.py:326
  22.7 5.0 collective-permute-start.1
  23.5 5.5 collective-permute-start.8
  24.2 6.7 %collective-permute-start.2 = (bf16[6,288,512]{2,1,0:T(8,128)(2,1)}, bf16[6,288,512]{2,1,0:T(8,128)(2,1)S(1)}, u32[]{:S(2)}, u32[]{:S(2)}) collective-permute-start(bf16[6,288,512]{2,1,0:T(8,128)(2,1)} %bitcast.8), channel_id=1, source_target_pairs={{0,8},{10,2},{20,28},{30,22},{1,9},{11,3},{21,29},{31,23}} | collective-permute-start | bytes 5308424 | tf_op jit(solution)/shard_map/ppermute | solution.py:326
  25.0 6.7 %collective-permute-start.6 = (bf16[6,288,512]{2,1,0:T(8,128)(2,1)S(1)}, bf16[6,288,512]{2,1,0:T(8,128)(2,1)}, u32[]{:S(2)}, u32[]{:S(2)}) collective-permute-start(bf16[6,288,512]{2,1,0:T(8,128)(2,1)S(1)} %collective-permute-done.refs_4_), channel_id=1, source_target_pairs={{0,16},{10,26},{20,4},{30,14},{1,17},{11,27},{21,5},{31,15}} | collective-permute-start | bytes 5308424 | tf_op jit(solution)/shard_map/ppermute | solution.py:326
  26.9 6.8 %collective-permute-start.5 = (bf16[6,288,512]{2,1,0:T(8,128)(2,1)S(1)}, bf16[6,288,512]{2,1,0:T(8,128)(2,1)S(1)}, u32[]{:S(2)}, u32[]{:S(2)}) collective-permute-start(bf16[6,288,512]{2,1,0:T(8,128)(2,1)S(1)} %collective-permute-done.refs_4_), channel_id=1, source_target_pairs={{0,8},{10,2},{20,28},{30,22},{1,9},{11,3},{21,29},{31,23}} | collective-permute-start | bytes 5308424 | tf_op jit(solution)/shard_map/ppermute | solution.py:326
  27.7 22.2 %collective-permute-start.4 = (bf16[6,288,512]{2,1,0:T(8,128)(2,1)S(1)}, bf16[6,288,512]{2,1,0:T(8,128)(2,1)S(1)}, u32[]{:S(2)}, u32[]{:S(2)}) collective-permute-start(bf16[6,288,512]{2,1,0:T(8,128)(2,1)S(1)} %collective-permute-done.3.refs_2_), channel_id=1, source_target_pairs={{16,24},{26,18},{4,12},{14,6},{17,25},{27,19},{5,13},{15,7}} | collective-permute-start | bytes 5308424 | tf_op jit(solution)/shard_map/ppermute | solution.py:326
  29.0 22.2 %collective-permute-start.11 = (bf16[6,288,512]{2,1,0:T(8,128)(2,1)}, bf16[6,288,512]{2,1,0:T(8,128)(2,1)}, u32[]{:S(2)}, u32[]{:S(2)}) collective-permute-start(bf16[6,288,512]{2,1,0:T(8,128)(2,1)} %bitcast.9), channel_id=1, source_target_pairs={{2,4},{12,10},{18,20},{28,26},{3,5},{13,11},{19,21},{29,27}} | collective-permute-start | bytes 5308424 | tf_op jit(solution)/shard_map/ppermute | solution.py:326
  30.9 22.2 %collective-permute-start.10 = (bf16[6,288,512]{2,1,0:T(8,128)(2,1)S(1)}, bf16[6,288,512]{2,1,0:T(8,128)(2,1)S(1)}, u32[]{:S(2)}, u32[]{:S(2)}) collective-permute-start(bf16[6,288,512]{2,1,0:T(8,128)(2,1)S(1)} %collective-permute-done.8.refs_8_), channel_id=1, source_target_pairs={{2,0},{12,14},{18,16},{28,30},{3,1},{13,15},{19,17},{29,31}} | collective-permute-start | bytes 5308424 | tf_op jit(solution)/shard_map/ppermute | solution.py:326
  31.7 24.5 %collective-permute-start.19 = (bf16[6,288,512]{2,1,0:T(8,128)(2,1)S(1)}, bf16[6,288,512]{2,1,0:T(8,128)(2,1)}, u32[]{:S(2)}, u32[]{:S(2)}) collective-permute-start(bf16[6,288,512]{2,1,0:T(8,128)(2,1)S(1)} %collective-permute-done.8.refs_8_), channel_id=1, source_target_pairs={{0,16},{30,14},{1,17},{31,15}} | collective-permute-start | bytes 5308424 | tf_op jit(solution)/shard_map/ppermute | solution.py:326
  33.7 23.9 %collective-permute-start.9 = (bf16[6,288,512]{2,1,0:T(8,128)(2,1)S(1)}, bf16[6,288,512]{2,1,0:T(8,128)(2,1)}, u32[]{:S(2)}, u32[]{:S(2)}) collective-permute-start(bf16[6,288,512]{2,1,0:T(8,128)(2,1)S(1)} %collective-permute-done.8.refs_8_), channel_id=1, source_target_pairs={{0,8},{30,22},{1,9},{31,23}} | collective-permute-start | bytes 5308424 | tf_op jit(solution)/shard_map/ppermute | solution.py:326
  49.9 10.4 %collective-permute-start.7 = (bf16[6,288,512]{2,1,0:T(8,128)(2,1)}, bf16[6,288,512]{2,1,0:T(8,128)(2,1)}, u32[]{:S(2)}, u32[]{:S(2)}) collective-permute-start(bf16[6,288,512]{2,1,0:T(8,128)(2,1)} %collective-permute-done.6.refs_6_), channel_id=1, source_target_pairs={{16,24},{26,18},{4,12},{14,6},{17,25},{27,19},{5,13},{15,7}} | collective-permute-start | bytes 5308424 | tf_op jit(solution)/shard_map/ppermute | solution.py:326
  51.2 122.1 %collective-permute-start.22 = (bf16[6,288,512]{2,1,0:T(8,128)(2,1)}, bf16[6,288,512]{2,1,0:T(8,128)(2,1)}, u32[]{:S(2)}, u32[]{:S(2)}) collective-permute-start(bf16[6,288,512]{2,1,0:T(8,128)(2,1)} %collective-permute-done.11.refs_5_), channel_id=1, source_target_pairs={{10,2},{20,28},{11,3},{21,29}} | collective-permute-start | bytes 5308424 | tf_op jit(solution)/shard_map/ppermute | solution.py:326
  53.1 122.1 %collective-permute-start.21 = (bf16[6,288,512]{2,1,0:T(8,128)(2,1)S(1)}, bf16[6,288,512]{2,1,0:T(8,128)(2,1)}, u32[]{:S(2)}, u32[]{:S(2)}) collective-permute-start(bf16[6,288,512]{2,1,0:T(8,128)(2,1)S(1)} %collective-permute-done.10.refs_3_), channel_id=1, source_target_pairs={{0,8},{30,22},{1,9},{31,23}} | collective-permute-start | bytes 5308424 | tf_op jit(solution)/shard_map/ppermute | solution.py:326
  56.3 120.2 %collective-permute-start.20 = (bf16[6,288,512]{2,1,0:T(8,128)(2,1)}, bf16[6,288,512]{2,1,0:T(8,128)(2,1)}, u32[]{:S(2)}, u32[]{:S(2)}) collective-permute-start(bf16[6,288,512]{2,1,0:T(8,128)(2,1)} %collective-permute-done.19.refs_1_), channel_id=1, source_target_pairs={{16,24},{14,6},{17,25},{15,7}} | collective-permute-start | bytes 5308424 | tf_op jit(solution)/shard_map/ppermute | solution.py:326
  169.5 62.6 %collective-permute-start.12 = (bf16[6,288,512]{2,1,0:T(8,128)(2,1)}, bf16[6,288,512]{2,1,0:T(8,128)(2,1)}, u32[]{:S(2)}, u32[]{:S(2)}) collective-permute-start(bf16[6,288,512]{2,1,0:T(8,128)(2,1)} %copy-done.6), channel_id=1, source_target_pairs={{2,4},{12,10},{18,20},{28,26},{3,5},{13,11},{19,21},{29,27}} | collective-permute-start | bytes 5308424 | tf_op jit(solution)/shard_map/ppermute | solution.py:326
  171.5 64.6 %collective-permute-start.15 = (bf16[6,288,512]{2,1,0:T(8,128)(2,1)}, bf16[6,288,512]{2,1,0:T(8,128)(2,1)}, u32[]{:S(2)}, u32[]{:S(2)}) collective-permute-start(bf16[6,288,512]{2,1,0:T(8,128)(2,1)} %collective-permute-done.11.refs_5_), channel_id=1, source_target_pairs={{10,26},{20,4},{11,27},{21,5}} | collective-permute-start | bytes 5308424 | tf_op jit(solution)/shard_map/ppermute | solution.py:326
  173.3 64.6 %collective-permute-start.13 = (bf16[6,288,512]{2,1,0:T(8,128)(2,1)S(1)}, bf16[6,288,512]{2,1,0:T(8,128)(2,1)}, u32[]{:S(2)}, u32[]{:S(2)}) collective-permute-start(bf16[6,288,512]{2,1,0:T(8,128)(2,1)S(1)} %collective-permute-done.10.refs_3_), channel_id=1, source_target_pairs={{0,16},{30,14},{1,17},{31,15}} | collective-permute-start | bytes 5308424 | tf_op jit(solution)/shard_map/ppermute | solution.py:326
  175.2 95.7 %collective-permute-start.18 = (bf16[6,288,512]{2,1,0:T(8,128)(2,1)S(1)}, bf16[6,288,512]{2,1,0:T(8,128)(2,1)}, u32[]{:S(2)}, u32[]{:S(2)}) collective-permute-start(bf16[6,288,512]{2,1,0:T(8,128)(2,1)S(1)} %bitcast.15), channel_id=1, source_target_pairs={{4,6},{10,8},{20,22},{26,24},{5,7},{11,9},{21,23},{27,25}} | collective-permute-start | bytes 5308424 | tf_op jit(solution)/shard_map/ppermute | solution.py:326
  232.2 40.0 %collective-permute-start.25 = (bf16[6,288,512]{2,1,0:T(8,128)(2,1)}, bf16[6,288,512]{2,1,0:T(8,128)(2,1)}, u32[]{:S(2)}, u32[]{:S(2)}) collective-permute-start(bf16[6,288,512]{2,1,0:T(8,128)(2,1)} %collective-permute-done.12.refs_5_), channel_id=1, source_target_pairs={{10,26},{20,4},{11,27},{21,5}} | collective-permute-start | bytes 5308424 | tf_op jit(solution)/shard_map/ppermute | solution.py:326
  234.1 40.0 %collective-permute-start.17 = (bf16[6,288,512]{2,1,0:T(8,128)(2,1)}, bf16[6,288,512]{2,1,0:T(8,128)(2,1)}, u32[]{:S(2)}, u32[]{:S(2)}) collective-permute-start(bf16[6,288,512]{2,1,0:T(8,128)(2,1)} %collective-permute-done.12.refs_5_), channel_id=1, source_target_pairs={{10,2},{20,28},{11,3},{21,29}} | collective-permute-start | bytes 5308424 | tf_op jit(solution)/shard_map/ppermute | solution.py:326
  236.1 38.0 %collective-permute-start.16 = (bf16[6,288,512]{2,1,0:T(8,128)(2,1)}, bf16[6,288,512]{2,1,0:T(8,128)(2,1)}, u32[]{:S(2)}, u32[]{:S(2)}) collective-permute-start(bf16[6,288,512]{2,1,0:T(8,128)(2,1)} %collective-permute-done.15.refs_3_), channel_id=1, source_target_pairs={{26,18},{4,12},{27,19},{5,13}} | collective-permute-start | bytes 5308424 | tf_op jit(solution)/shard_map/ppermute | solution.py:326
  237.9 185.1 %collective-permute-start.14 = (bf16[6,288,512]{2,1,0:T(8,128)(2,1)}, bf16[6,288,512]{2,1,0:T(8,128)(2,1)S(1)}, u32[]{:S(2)}, u32[]{:S(2)}) collective-permute-start(bf16[6,288,512]{2,1,0:T(8,128)(2,1)} %collective-permute-done.13.refs_1_), channel_id=1, source_target_pairs={{16,24},{14,6},{17,25},{15,7}} | collective-permute-start | bytes 5308424 | tf_op jit(solution)/shard_map/ppermute | solution.py:326
  270.9 262.6 %collective-permute-start.23 = (bf16[6,288,512]{2,1,0:T(8,128)(2,1)}, bf16[6,288,512]{2,1,0:T(8,128)(2,1)S(1)}, u32[]{:S(2)}, u32[]{:S(2)}) collective-permute-start(bf16[6,288,512]{2,1,0:T(8,128)(2,1)} %collective-permute-done.11.refs_5_), channel_id=1, source_target_pairs={{4,6},{10,8},{20,22},{26,24},{5,7},{11,9},{21,23},{27,25}} | collective-permute-start | bytes 5308424 | tf_op jit(solution)/shard_map/ppermute | solution.py:326
  272.2 268.7 %collective-permute-start.26 = (bf16[6,288,512]{2,1,0:T(8,128)(2,1)}, bf16[6,288,512]{2,1,0:T(8,128)(2,1)}, u32[]{:S(2)}, u32[]{:S(2)}) collective-permute-start(bf16[6,288,512]{2,1,0:T(8,128)(2,1)} %collective-permute-done.25.refs_1_), channel_id=1, source_target_pairs={{26,18},{4,12},{27,19},{5,13}} | collective-permute-start | bytes 5308424 | tf_op jit(solution)/shard_map/ppermute | solution.py:326
  534.7 32.8 %collective-permute-start.24 = (bf16[6,288,512]{2,1,0:T(8,128)(2,1)}, bf16[6,288,512]{2,1,0:T(8,128)(2,1)S(1)}, u32[]{:S(2)}, u32[]{:S(2)}) collective-permute-start(bf16[6,288,512]{2,1,0:T(8,128)(2,1)} %collective-permute-done.12.refs_5_), channel_id=1, source_target_pairs={{4,6},{10,8},{20,22},{26,24},{5,7},{11,9},{21,23},{27,25}} | collective-permute-start | bytes 5308424 | tf_op jit(solution)/shard_map/ppermute | solution.py:326
  536.0 52.0 %collective-permute-start.27 = (bf16[4,1296,128]{2,1,0:T(8,128)(2,1)}, bf16[4,1296,128]{2,1,0:T(8,128)(2,1)S(1)}, u32[]{:S(2)}, u32[]{:S(2)}) collective-permute-start(bf16[4,1296,128]{2,1,0:T(8,128)(2,1)} %get-tuple-element.33), channel_id=1, source_target_pairs={{1,0},{2,3},{3,2},{4,5},{11,10},{12,13},{13,12},{14,15},{17,16},{1... | collective-permute-start | bytes 3981320 | tf_op jit(solution)/shard_map/ppermute | solution.py:387
  536.7 51.3 %collective-permute-start.28 = (bf16[4,1296,128]{2,1,0:T(8,128)(2,1)}, bf16[4,1296,128]{2,1,0:T(8,128)(2,1)}, u32[]{:S(2)}, u32[]{:S(2)}) collective-permute-start(bf16[4,1296,128]{2,1,0:T(8,128)(2,1)} %get-tuple-element.47), channel_id=1, source_target_pairs={{0,1},{1,0},{9,8},{15,14},{16,17},{22,23},{30,31},{31,30}} | collective-permute-start | bytes 3981320 | tf_op jit(solution)/shard_map/ppermute | solution.py:387
  538.5 49.5 %collective-permute-start.29 = (bf16[4,1296,128]{2,1,0:T(8,128)(2,1)}, bf16[4,1296,128]{2,1,0:T(8,128)(2,1)}, u32[]{:S(2)}, u32[]{:S(2)}) collective-permute-start(bf16[4,1296,128]{2,1,0:T(8,128)(2,1)} %get-tuple-element.46), channel_id=1, source_target_pairs={{0,1},{2,3},{3,2},{5,4},{6,7},{9,8},{10,11},{11,10},{14,15},{15,14... | collective-permute-start | bytes 3981320 | tf_op jit(solution)/shard_map/ppermute | solution.py:387
  582.1 19.9 %collective-permute-start.31 = (bf16[4,1296,128]{2,1,0:T(8,128)(2,1)}, bf16[4,1296,128]{2,1,0:T(8,128)(2,1)S(1)}, u32[]{:S(2)}, u32[]{:S(2)}) collective-permute-start(bf16[4,1296,128]{2,1,0:T(8,128)(2,1)} %get-tuple-element.58), channel_id=1, source_target_pairs={{7,6},{8,9},{23,22},{24,25}} | collective-permute-start | bytes 3981320 | tf_op jit(solution)/shard_map/ppermute | solution.py:387
  583.4 32.9 %collective-permute-start.30 = (bf16[4,1296,128]{2,1,0:T(8,128)(2,1)}, bf16[4,1296,128]{2,1,0:T(8,128)(2,1)}, u32[]{:S(2)}, u32[]{:S(2)}) collective-permute-start(bf16[4,1296,128]{2,1,0:T(8,128)(2,1)} %get-tuple-element.57), channel_id=1, source_target_pairs={{4,5},{5,4},{6,7},{7,6},{8,9},{10,11},{12,13},{13,12},{18,19},{19,... | collective-permute-start | bytes 3981320 | tf_op jit(solution)/shard_map/ppermute | solution.py:387
  (14 other events, 449.0 us)

commit v2 on v1

v2 whole, which is shorter than its diff:
```python
import functools

import jax
import jax.numpy as jnp
import numpy as np
from jax import lax
from jax.experimental import pallas as pl
from jax.experimental.pallas import tpu as pltpu
from jax.sharding import PartitionSpec as P

LANES = 128
ARRIVALS = (
    (("own", "a", "b", "x0", "c0", "ca", "cb", "d0"), 5),
    (("xb",), 5),
    (("t", "xa", "da", "db"), 5),
    (("ct",), 4),
    (("e", "xt"), 3),
    (("dt",), 3),
    ((), 16),
)
SENDS = ((0, 3), (1, 3), (2, 2), (3, 2), (4, 2), (5, 3))


def route(n):
    devices = [(r, j) for r in range(n) for j in range(n)]
    holds = {"own": {d: d[1] for d in devices}}
    pairs, source = {}, {}

    def add(name, operand, moves):
        pairs[name], source[name] = moves, operand
        holds[name] = {t: holds[operand][f] for f, t in moves}

    ends = [(r, j) for r, j in devices if j in (0, n - 1)]
    inner = [d for d in devices if d not in ends]
    early = [(r, j) for r, j in ends if (r + j) % 2 == 0]
    add("a", "own", [((r, j ^ 1), (r, j)) for r, j in devices])
    add("b", "own", [((r, j ^ 3), (r, j)) for r, j in inner + early])
    holds["z"] = {(r, j): j ^ 3 if (r, j) in inner else j for r, j in devices}
    add("t", "z", [((r, j ^ (1 if (r, j) in ends else 2)), (r, j)) for r, j in devices])
    del holds["z"]
    add("e", "t", [((r, j ^ 1), (r, j)) for r, j in ends if (r, j) not in early])
    rows = {d: {} for d in devices}
    cols = {d: {} for d in devices}
    for name, held in holds.items():
        for device, plane in held.items():
            assert plane not in rows[device]
            rows[device][plane] = name
    for e, name in (("0", "own"), ("a", "a"), ("b", "b"), ("t", "t")):
        for v, kind in ((0, ""), (2, "x"), (1, "c"), (3, "d")):
            parent = 2 if v == 3 else 0
            if v:
                pairs[kind + e] = [((c ^ parent, c), (c ^ v, c)) for c in range(n)]
                source[kind + e] = "x" + e if parent else name
            for c in range(n):
                cols[c ^ v, c][holds[name][c, c]] = kind + e if v else name
    assert all(len(x) == n for d in devices for x in (rows[d], cols[d]))
    return pairs, source, rows, cols


def share_out(n, rows, cols):
    half = n // 2
    event = {name: e for e, (names, _) in enumerate(ARRIVALS) for name in names}
    window = [min((i for i, x in enumerate(SENDS) if x[0] >= e), default=None) for e in range(len(ARRIVALS))]
    tasks, senders, arrives = {}, [[] for _ in SENDS], {}

    def attempt(blocks, chosen):
        wait, plan = list(blocks), []
        room = [x[1] if i in chosen else 0 for i, x in enumerate(SENDS)]
        for e, (_, most) in enumerate(ARRIVALS):
            i = window[e]
            now = [b for b in wait if b[0] <= e]
            leave = [] if i is None else [b for b in now if not b[1]][:min(most, room[i])]
            if leave:
                room[i] -= len(leave)
            stay = [b for b in now if b[1]][:most - len(leave)]
            for b in leave + stay:
                wait.remove(b)
                plan.append((e, i if b in leave else None, b[2], b[3]))
        return None if wait else plan

    for r in range(n):
        for j in range(n):
            for y in range(2):
                blocks = sorted(
                    (max(event[rows[r, j][kr]], event[cols[r, j][kc]]), kr // half == y, kr, kc)
                    for kr in range(n)
                    for kc in range(n)
                )
                best = None
                for mask in range(1 << len(SENDS)):
                    chosen = [i for i in range(len(SENDS)) if mask >> i & 1]
                    plan = attempt(blocks, chosen)
                    if plan is None:
                        continue
                    cost = sum(SENDS[i][1] * (1 + i) ** 2 for i in chosen), sum(e for e, i, _, _ in plan if i is not None)
                    if best is None or cost < best[0]:
                        best = cost, plan
                used = {}
                for e, i, kr, kc in best[1]:
                    if i is None:
                        place = (kr - y * half) * n + kc
                    else:
                        place = used[i] = used.get(i, -1) + 1
                        arrives[r, j, 1 - y, kr, kc] = i, place
                    tasks.setdefault((r, j, y, e), []).append((kr, kc, int(i is not None), place))
                for i in used:
                    senders[i].append((r, j, y))
    return tasks, senders, arrives


def rate(w_ref, group_ref, gain_ref, region):
    groups = group_ref[...]
    gain = jnp.zeros(groups.shape, jnp.float32)
    for g in range(gain_ref.shape[0]):
        gain = gain + jnp.where(groups == g, gain_ref[g, region], jnp.float32(0.0))
    return w_ref[...] * gain


def fetch(index, sources, target, sem, h, p, gap):
    for i, source in enumerate(sources):

        @pl.when(index == i)
        def _():
            for c in range(6):
                pltpu.make_async_copy(
                    source.at[c], target.at[pl.ds((c // 3) * gap, h), pl.ds((c % 3) * p, p)], sem
                ).start()


def landed(sources, target, sem, h, p, gap):
    for c in range(6):
        pltpu.make_async_copy(
            sources[0].at[c], target.at[pl.ds((c // 3) * gap, h), pl.ds((c % 3) * p, p)], sem
        ).wait()


def pack(stage, real, imag, h):
    tail, quarter = h % LANES, h // 2
    full = h // LANES
    for part, value in ((0, real), (1, imag)):
        for k in range(full):
            stage[pl.ds((part * full + k) * h, h), :] = value[:, k * LANES:(k + 1) * LANES].astype(stage.dtype)
        for fold in range(2):
            lane = (2 * fold + part) * tail
            stage[pl.ds(2 * full * h, quarter), lane:lane + tail] = value[
                fold * quarter:(fold + 1) * quarter, full * LANES:
            ].astype(stage.dtype)


def pick(second, first_ref, second_ref, out, held, sem):
    for k, source in enumerate((first_ref, second_ref)):

        @pl.when(second[0] == k)
        def _():
            pltpu.make_async_copy(source, held, sem).start()

    pltpu.make_async_copy(first_ref, held, sem).wait()
    copy = pltpu.make_async_copy(held, out, sem)
    copy.start()
    copy.wait()


def multiply_blocks(passed, results, base, sources, h, p, gap, table, tile_map, gain_ref, w_ref, group_ref, *refs):
    srcs = refs[:sources]
    refs = refs[sources + passed:]
    own, out = refs[0], refs[results - 1]
    raw, left, right, stage_own, stage_out, l_sem, r_sem, own_sem, out_sem = refs[results:]
    count = table[base]
    sign = table[2].astype(jnp.float32)
    scale = rate(w_ref, group_ref, gain_ref, tile_map[table[0], table[1]])

    def entry(t):
        code = table[base + 1 + t]
        return code & 63, (code >> 6) & 63, (code >> 12) & 15, code >> 16

    def stored(stage, target, sem, slot, place):
        return pltpu.make_async_copy(stage.at[slot], target.at[place], sem.at[slot])

    def store(stage, target, sem, done, place, real, imag):
        slot = lax.rem(done, 2)

        @pl.when(done > 1)
        def _():
            stored(stage, target, sem, slot, 0).wait()

        pack(stage.at[slot], real, imag, h)
        stored(stage, target, sem, slot, place).start()

    def settle(stage, target, sem, done):
        for back in (1, 2):

            @pl.when(done >= back)
            def _():
                stored(stage, target, sem, lax.rem(done - back, 2), 0).wait()

    def ask_row(t):
        fetch(entry(t)[0], srcs, raw.at[lax.rem(t, 2)], l_sem.at[lax.rem(t, 2)], h, p, h)

    def ask_column(t):
        fetch(entry(t)[1], srcs, right.at[lax.rem(t, 2)], r_sem.at[lax.rem(t, 2)], h, p, gap)

    def weigh(slot):
        for c in range(3):
            part = raw[slot, :, c * p:(c + 1) * p].astype(jnp.float32)
            left[slot, :, c * p:(c + 1) * p] = (part * scale).astype(jnp.bfloat16)

    @pl.when(count > 0)
    def _():
        ask_row(0)
        ask_column(0)

        @pl.when(count > 1)
        def _():
            ask_row(1)

        landed(srcs, raw.at[0], l_sem.at[0], h, p, h)
        weigh(0)

    def task(t, carry):
        owns, outs = carry
        _, _, kind, place = entry(t)
        slot = lax.rem(t, 2)
        other = 1 - slot

        @pl.when(t + 1 < count)
        def _():
            landed(srcs, raw.at[other], l_sem.at[other], h, p, h)
            ask_column(t + 1)

        @pl.when(t + 2 < count)
        def _():
            ask_row(t + 2)

        landed(srcs, right.at[slot], r_sem.at[slot], h, p, gap)
        weigh(other)
        product = lax.dot_general(
            left[slot], right[slot], (((1,), (1,)), ((), ())), preferred_element_type=jnp.float32
        )
        real = product[:h, :h] + sign * product[h:, gap:gap + h]
        imag = product[h:, :h] - sign * product[:h, gap:gap + h]

        @pl.when(kind == 0)
        def _():
            store(stage_own, own, own_sem, owns, place, real, imag)

        if results > 1:

            @pl.when(kind == 1)
            def _():
                store(stage_out, out, out_sem, outs, place, real, imag)

        return owns + (kind == 0).astype(jnp.int32), outs + (kind == 1).astype(jnp.int32)

    zero = jnp.int32(0)
    owns, outs = lax.fori_loop(0, count, task, (zero, zero))
    settle(stage_own, own, own_sem, owns)
    if results > 1:
        settle(stage_out, out, out_sem, outs)


def add_up(base, n, h, table, own, *refs):
    recvs = refs[:len(SENDS)]
    out, mine, theirs, real, imag, image, m_sem, t_sem, o_sem = refs[len(SENDS):]
    blocks = (n // 2) * n
    full, tail, quarter = h // LANES, h % LANES, h // 2
    wide = n * h // LANES

    def load(b, slot):
        pltpu.make_async_copy(own.at[b], mine.at[slot], m_sem.at[slot]).start()
        code = table[base + b]
        for k, recv in enumerate(recvs):

            @pl.when((code & 15) == k)
            def _():
                pltpu.make_async_copy(recv.at[code >> 4], theirs.at[slot], t_sem.at[slot]).start()

    def written(chunk, k):
        return pltpu.make_async_copy(
            image.at[chunk % 2, pl.ds(2 * k * h, 2 * h)].reshape(h, 2, LANES),
            out.at[pl.ds(chunk * h, h), :, pl.ds(k * LANES, LANES)],
            o_sem.at[chunk % 2],
        )

    load(0, 0)
    for b in range(blocks):
        slot, chunk, kc = b % 2, b // n, b % n
        if b + 1 < blocks:
            load(b + 1, 1 - slot)
        pltpu.make_async_copy(own.at[0], mine.at[slot], m_sem.at[slot]).wait()
        pltpu.make_async_copy(recvs[0].at[0], theirs.at[slot], t_sem.at[slot]).wait()
        for part, line in ((0, real), (1, imag)):
            for k in range(full):
                at = pl.ds((part * full + k) * h, h)
                line[:, kc * h + k * LANES:kc * h + (k + 1) * LANES] = mine[slot, at, :] + theirs[
                    slot, at, :
                ].astype(jnp.float32)
            at = pl.ds(2 * full * h, quarter)
            rest = mine[slot, at, :] + theirs[slot, at, :].astype(jnp.float32)
            for fold in range(2):
                lane = (2 * fold + part) * tail
                line[
                    fold * quarter:(fold + 1) * quarter, kc * h + full * LANES:(kc + 1) * h
                ] = rest[:, lane:lane + tail]
        if kc == n - 1:
            buf = chunk % 2
            for part, line in ((0, real), (1, imag)):
                for k in range(wide):
                    image[buf, pl.ds(2 * k * h + part, h, stride=2), :] = line[:, k * LANES:(k + 1) * LANES]
            for k in range(wide):
                written(chunk, k).start()
    for chunk in range(n // 2):
        for k in range(wide):
            written(chunk, k).wait()


def tiled(mesh, h, p):
    n = mesh.shape["col"]
    half = n // 2
    pairs, source, rows, cols = route(n)
    tasks, senders, arrives = share_out(n, rows, cols)
    gap = -(-h // LANES) * LANES
    block = 2 * h * h // LANES
    events = range(len(ARRIVALS))

    names = {e: set() for e in events}
    for (r, j, _, e), items in tasks.items():
        for kr, kc, _, _ in items:
            names[e] |= {rows[r, j][kr], cols[r, j][kc]}
    names = {e: sorted(v) for e, v in names.items()}
    bases, size = {}, 3
    for e in events:
        bases[e] = size
        size += 1 + max(len(v) for k, v in tasks.items() if k[3] == e)
    final = size
    size += half * n
    table = np.zeros((n, n, 2, size), np.int32)
    for r in range(n):
        for j in range(n):
            for y in range(2):
                line = table[r, j, y]
                line[:3] = r, j, 1 if r <= j else -1
                for e in events:
                    items = sorted(tasks.get((r, j, y, e), []), key=lambda i: (names[e].index(rows[r, j][i[0]]), -i[2], i[3]))
                    line[bases[e]] = len(items)
                    for t, (kr, kc, kind, place) in enumerate(items):
                        parts = names[e].index(rows[r, j][kr]) | names[e].index(cols[r, j][kc]) << 6
                        line[bases[e] + 1 + t] = parts | kind << 12 | place << 16
                for i in range(half):
                    for kc in range(n):
                        index, place = arrives[r, j, y, y * half + i, kc]
                        line[final + i * n + kc] = index | place << 4

    def local(velocity, panel_weight, panel_group, tile_map, group_gain):
        here = lax.axis_index("row"), lax.axis_index("col"), lax.axis_index("panel")
        line = lax.dynamic_slice(jnp.asarray(table), (*here, 0), (1, 1, 1, size)).reshape(size)
        weight, group = panel_weight[None, :], panel_group[None, :]
        have = {"own": jnp.transpose(velocity, (1, 0, 2))}
        anywhere = pl.BlockSpec(memory_space=pl.ANY)

        def move(*given):
            for name in given:
                with jax.named_scope("move_" + name):
                    ids = [(a[0] * n + a[1], b[0] * n + b[1]) for a, b in pairs[name]]
                    have[name] = lax.ppermute(have[source[name]], ("row", "col"), ids)

        def choose(name, first, second):
            inner = jnp.logical_and(here[1] > 0, here[1] < n - 1).astype(jnp.int32)[None]
            have[name] = pl.pallas_call(
                pick,
                out_shape=jax.ShapeDtypeStruct((6, h, p), jnp.bfloat16),
                in_specs=[pl.BlockSpec(memory_space=pltpu.SMEM)] + [anywhere] * 2,
                out_specs=anywhere,
                scratch_shapes=[pltpu.VMEM((6, h, p), jnp.bfloat16), pltpu.SemaphoreType.DMA],
                compiler_params=pltpu.CompilerParams(vmem_limit_bytes=60 << 20),
                cost_estimate=pl.CostEstimate(flops=1 << 10, bytes_accessed=1 << 10, transcendentals=0),
                name="pick",
            )(inner, have[first], have[second])

        def fence(*wanted):
            keys = list(dict.fromkeys(wanted))
            have.update(zip(keys, lax.optimization_barrier(tuple(have[k] for k in keys))))

        def blocks(e):
            boxes = [i for i, x in enumerate(SENDS) if x[0] >= e][:1]
            results = ["sums"] + [f"sent{i}" for i in boxes]
            used = [have[k] for k in names[e]]
            carried = [(k, i) for i, k in enumerate(results) if k in have]
            made = pl.pallas_call(
                functools.partial(multiply_blocks, len(carried), len(results), bases[e], len(used), h, p, gap),
                out_shape=[jax.ShapeDtypeStruct((half * n, block, LANES), jnp.float32)]
                + [jax.ShapeDtypeStruct((SENDS[i][1], block, LANES), jnp.bfloat16) for i in boxes],
                in_specs=[pl.BlockSpec(memory_space=pltpu.SMEM)] * 3
                + [pl.BlockSpec(memory_space=pltpu.VMEM)] * 2
                + [anywhere] * (len(used) + len(carried)),
                out_specs=[anywhere] * len(results),
                input_output_aliases={5 + len(used) + at: i for at, (_, i) in enumerate(carried)},
                scratch_shapes=[
                    pltpu.VMEM((2, 2 * h, 3 * p), jnp.bfloat16),
                    pltpu.VMEM((2, 2 * h, 3 * p), jnp.bfloat16),
                    pltpu.VMEM((2, gap + h, 3 * p), jnp.bfloat16),
                    pltpu.VMEM((2, block, LANES), jnp.float32),
                    pltpu.VMEM((2, block, LANES), jnp.bfloat16),
                    pltpu.SemaphoreType.DMA((2,)),
                    pltpu.SemaphoreType.DMA((2,)),
                    pltpu.SemaphoreType.DMA((2,)),
                    pltpu.SemaphoreType.DMA((2,)),
                ],
                compiler_params=pltpu.CompilerParams(vmem_limit_bytes=60 << 20),
                cost_estimate=pl.CostEstimate(flops=1 << 20, bytes_accessed=1 << 16, transcendentals=0),
                name=f"blocks_{e}",
            )(line, tile_map, group_gain, weight, group, *used, *(have[k] for k, _ in carried))
            have.update(zip(results, made))

        def exchange(i):
            ids = [((r * n + j) * 2 + y, (r * n + j) * 2 + 1 - y) for r, j, y in senders[i]]
            with jax.named_scope(f"move_sums{i}"):
                have[f"got{i}"] = lax.ppermute(have[f"sent{i}"], ("row", "col", "panel"), ids)

        move("c0", "x0", "b", "a")
        fence("own", "b", "a", "x0", "c0")
        choose("z", "own", "b")
        move("t", "xa", "xb", "ca", "cb", "d0")
        fence("d0", "ca", "cb")
        blocks(0)
        fence("sums", "sent0", "xb")
        exchange(0)
        blocks(1)
        fence("sums", "sent1", "got0", "xa", "t")
        move("e", "xt", "ct", "da", "db")
        exchange(1)
        fence("da", "db")
        blocks(2)
        fence("sums", "sent2", "ct")
        exchange(2)
        blocks(3)
        fence("sums", "sent3", "got1", "got2", "xt", "e")
        exchange(3)
        move("dt")
        blocks(4)
        fence("dt", "sums", "sent4")
        exchange(4)
        blocks(5)
        fence("sums", "sent5", "got3", "got4")
        exchange(5)
        blocks(6)
        got = [have[f"got{i}"] for i in range(len(SENDS))]
        return pl.pallas_call(
            functools.partial(add_up, final, n, h),
            out_shape=jax.ShapeDtypeStruct((half * h, 2, n * h), jnp.float32),
            in_specs=[pl.BlockSpec(memory_space=pltpu.SMEM)] + [anywhere] * (1 + len(got)),
            out_specs=anywhere,
            scratch_shapes=[
                pltpu.VMEM((2, block, LANES), jnp.float32),
                pltpu.VMEM((2, block, LANES), jnp.bfloat16),
                pltpu.VMEM((h, n * h), jnp.float32),
                pltpu.VMEM((h, n * h), jnp.float32),
                pltpu.VMEM((2, 2 * h * n * h // LANES, LANES), jnp.float32),
                pltpu.SemaphoreType.DMA((2,)),
                pltpu.SemaphoreType.DMA((2,)),
                pltpu.SemaphoreType.DMA((2,)),
            ],
            compiler_params=pltpu.CompilerParams(vmem_limit_bytes=60 << 20),
            name="add_up",
        )(line, have["sums"], *got)

    return local


def contract(left_side, right_side):
    return lax.dot_general(
        left_side, right_side, (((1,), (1,)), ((), ())), preferred_element_type=jnp.float32
    )


def plain(velocity, panel_weight, panel_group, tile_map, group_gain):
    row_index, col_index = lax.axis_index("row"), lax.axis_index("col")
    rows_block = lax.all_gather(velocity, "col", axis=0, tiled=True)
    kept = jnp.where(row_index == col_index, rows_block, 0).astype(rows_block.dtype)
    cols_block = lax.psum(kept, "row")
    gains = lax.dynamic_index_in_dim(group_gain, tile_map[row_index, col_index], 1, keepdims=False)
    scale = panel_weight * gains[panel_group]
    weighted = (rows_block.astype(jnp.float32) * scale[None, None, :]).astype(jnp.bfloat16)
    width, depth = weighted.shape[0], 3 * weighted.shape[2]
    left = weighted.reshape(width, 2 * depth)
    right = cols_block.reshape(width, 2 * depth)
    sign = jnp.where(row_index <= col_index, jnp.float32(1.0), jnp.float32(-1.0))
    real = contract(left[:, :depth], right[:, :depth]) + sign * contract(left[:, depth:], right[:, depth:])
    imag = contract(left[:, depth:], right[:, :depth]) - sign * contract(left[:, :depth], right[:, depth:])
    return lax.psum_scatter(jnp.stack((real, imag), axis=1), "panel", scatter_dimension=0, tiled=True)


def solution(mesh):
    n, panels = mesh.shape["col"], mesh.shape["panel"]

    def whole(velocity, panel_weight, panel_group, tile_map, group_gain):
        h = velocity.shape[0] // (n * n)
        p = velocity.shape[2] // panels
        fits = (
            mesh.shape["row"] == n
            and n == 4
            and panels == 2
            and h % 32 == 0
            and (h % LANES) * 4 == LANES
            and (n * h) % LANES == 0
            and p % LANES == 0
        )
        return jax.shard_map(
            tiled(mesh, h, p) if fits else plain,
            mesh=mesh,
            in_specs=(P(("row", "col"), None, "panel"), P("panel"), P("panel"), P(), P()),
            out_specs=P(("row", "panel"), None, "col"),
            check_vma=False,
        )(velocity, panel_weight, panel_group, tile_map, group_gain)

    return whole
```

time: 629 us -> 217 us (0.34)
  Pallas kernels: 323 us -> 67.9 us
  waiting for transfers between devices: 245 us -> 103 us
  starting transfers between devices: 51.6 us -> 40.9 us
    pallas_call x5 -> x8, Pallas kernels: 314 us -> 59.2 us  [the longest x7 56.5 us: blocks(): pl.pallas_call(functools.partial(multiply_blocks, len(carried), len(resul...]
    ppermute x32 -> x22, waiting for transfers between devices: 245 us -> 103 us  [the longest x16 78.7 us: move(): have[name] = lax.ppermute(have[source[name]], ('row', 'col'), ids)]
    ppermute x32 -> x22, starting transfers between devices: 51.6 us -> 40.9 us  [the longest x16 23.9 us: move(): have[name] = lax.ppermute(have[source[name]], ('row', 'col'), ids)]
  transfers between devices with their start and end apart: 32 -> 22, of which waited for: 7 -> 6; matrix products, arithmetic and copies ran while one was open for 0% -> 1% of each run, Pallas kernels for 50% -> 27%
where the time goes in v2:
time: 217 us; the launch traced here: 216 us
  waiting for transfers between devices  103 us (47%)
  Pallas kernels  67.9 us (31%)
  starting transfers between devices  40.9 us (19%)
  local copies, waits for them, and re-layouts  3.4 us (2%)
    ppermute x16, waiting for transfers between devices, move(): have[name] = lax.ppermute(have[source[name]], ('row', 'col'), ids)  78.7 us
    pallas_call x7, Pallas kernels, blocks(): pl.pallas_call(functools.partial(multiply_blocks, len(carried), len(resul...  56.5 us
    ppermute x6, waiting for transfers between devices, exchange(): lax.ppermute(have[f'sent{i}'], ('row', 'col', 'panel'), ids)  24.4 us
    ppermute x16, starting transfers between devices, move(): have[name] = lax.ppermute(have[source[name]], ('row', 'col'), ids)  23.9 us
    ppermute x6, starting transfers between devices, exchange(): lax.ppermute(have[f'sent{i}'], ('row', 'col', 'panel'), ids)  17 us
    pallas_call x1, Pallas kernels, local(): pl.pallas_call(functools.partial(add_up, final, n, h), out_shape=jax.Shap...  8.64 us
  transfers between devices with their start and end apart: 22, of which 6 were waited for; matrix products, arithmetic and copies ran while one was open for 1% of the time, Pallas kernels for 27%

profile of v2, /device:TPU:24, one launch (start us, length us, event | category | flops | bytes accessed | tf_op | source)
XLA Modules:
  0.0 215.7 jit_solution(8460432431985158824)
XLA Ops:
  0.0 1.4 collective-permute-start
  1.4 1.5 collective-permute-start.1
  2.9 1.9 collective-permute-start.2
  5.5 34.9 %collective-permute-done.refs_1_.second_ref = bf16[6,288,512]{2,1,0:T(8,128)(2,1)S(1)} collective-permute-done((bf16[6,288,512]{2,1,0:T(8,128)(2,1)}, bf16[6,288,512]{2,1,0:T(8,128)(2,1)S(1)}, u32[]{:S(2)}, u32[]{:S(2)}) %collective-permute-start) | collective-permute-done | bytes 1769504 | tf_op jit(solution)/shard_map/move_b/ppermute | solution.py:364
  40.4 20.5 %collective-permute-done.1.refs_0_ = bf16[6,288,512]{2,1,0:T(8,128)(2,1)S(1)} collective-permute-done((bf16[6,288,512]{2,1,0:T(8,128)(2,1)}, bf16[6,288,512]{2,1,0:T(8,128)(2,1)S(1)}, u32[]{:S(2)}, u32[]{:S(2)}) %collective-permute-start.1) | collective-permute-done | bytes 1769504 | tf_op jit(solution)/shard_map/move_a/ppermute | solution.py:364
  60.9 2.3 %collective-permute-start.6 = (bf16[6,288,512]{2,1,0:T(8,128)(2,1)S(1)}, bf16[6,288,512]{2,1,0:T(8,128)(2,1)}, u32[]{:S(2)}, u32[]{:S(2)}) collective-permute-start(bf16[6,288,512]{2,1,0:T(8,128)(2,1)S(1)} %collective-permute-done.refs_1_.second_ref), channel_id=1, source_target_pairs={{0,8},{10,2},{20,28},{30,22},{1,9},{11,3},{21,29},{31,23}} | collective-permute-start | bytes 5308424 | tf_op jit(solution)/shard_map/move_cb/ppermute | solution.py:364
  63.2 1.9 collective-permute-start.5
  65.1 1.3 collective-permute-start.4
  66.4 1.9 collective-permute-start.7
  68.3 2.7 %pick.1 = bf16[6,288,512]{2,1,0:T(8,128)(2,1)} custom-call(s32[1]{0:T(128)} %bitcast.4.second, bf16[6,288,512]{2,1,0:T(8,128)(2,1)} %bitcast.10, bf16[6,288,512]{2,1,0:T(8,128)(2,1)} %copy-done), custom_call_target="tpu_custom_call" | custom-call | flops 1024 | bytes 1024 | tf_op jit(solution)/shard_map/pick/pallas_call | solution.py:368
  71.1 2.0 collective-permute-start.9
  74.3 7.8 %blocks_0.1 = (f32[8,1296,128]{2,1,0:T(8,128)}, bf16[3,1296,128]{2,1,0:T(8,128)(2,1)}) custom-call(s32[44]{0:T(128)} %dynamic-slice_bitcast_fusion.table, s32[4,4]{1,0:T(4,128)} %tile_map.13, f32[4,4]{1,0:T(4,128)} %gain_ref.13, f32[1,512]{1,0:T(1,128)} %bitcast.18, s32[1,512]{1,0:T(1,128)} %bitcast.25, bf16[6,288,512]{2,1,0:T(8,128)(2,1)} %copy-done.1, ...), custom_call_target="tpu_custom_call" | custom-call | flops 1048576 | bytes 65536 | tf_op jit(solution)/shard_map/blocks_0/pallas_call | solution.py:388
  82.0 4.6 %collective-permute-start.8 = (bf16[3,1296,128]{2,1,0:T(8,128)(2,1)}, bf16[3,1296,128]{2,1,0:T(8,128)(2,1)}, u32[]{:S(2)}, u32[]{:S(2)}) collective-permute-start(bf16[3,1296,128]{2,1,0:T(8,128)(2,1)} %get-tuple-element.65), channel_id=1, source_target_pairs={{0,1},{1,0},{2,3},{3,2},{4,5},{6,7},{9,8},{10,11},{11,10},{12,13},... | collective-permute-start | bytes 2985992 | tf_op jit(solution)/shard_map/move_sums0/ppermute | solution.py:417
  86.6 1.3 collective-permute-start.12
  88.8 23.3 %collective-permute-done.10.refs_9_.refs_10_.refs_11_.refs_12_.refs_5_ = bf16[6,288,512]{2,1,0:T(8,128)(2,1)} collective-permute-done((bf16[6,288,512]{2,1,0:T(8,128)(2,1)}, bf16[6,288,512]{2,1,0:T(8,128)(2,1)}, u32[]{:S(2)}, u32[]{:S(2)}) %collective-permute-start.10) | collective-permute-done | bytes 1769504 | tf_op jit(solution)/shard_map/move_t/ppermute | solution.py:364
  112.1 1.3 collective-permute-start.11
  113.4 2.0 collective-permute-start.13
  115.3 1.9 collective-permute-start.16
  118.5 1.6 collective-permute-start.14
  121.4 14.1 %blocks_2.1 = (f32[8,1296,128]{2,1,0:T(8,128)}, bf16[2,1296,128]{2,1,0:T(8,128)(2,1)}) custom-call(s32[44]{0:T(128)} %dynamic-slice_bitcast_fusion.table, s32[4,4]{1,0:T(4,128)} %tile_map.13, f32[4,4]{1,0:T(4,128)} %gain_ref.13, f32[1,512]{1,0:T(1,128)} %bitcast.20, s32[1,512]{1,0:T(1,128)} %bitcast.27, ...), custom_call_target="tpu_custom_call", output_to_operand_aliasing={{0}: (18, {})} | custom-call | flops 1048576 | bytes 65536 | tf_op jit(solution)/shard_map/blocks_2/pallas_call | solution.py:388
  135.5 3.3 %collective-permute-start.15 = (bf16[2,1296,128]{2,1,0:T(8,128)(2,1)}, bf16[2,1296,128]{2,1,0:T(8,128)(2,1)S(1)}, u32[]{:S(2)}, u32[]{:S(2)}) collective-permute-start(bf16[2,1296,128]{2,1,0:T(8,128)(2,1)} %get-tuple-element.78), channel_id=1, source_target_pairs={{0,1},{1,0},{2,3},{4,5},{5,4},{6,7},{7,6},{8,9},{10,11},{11,10},{1... | collective-permute-start | bytes 1990664 | tf_op jit(solution)/shard_map/move_sums2/ppermute | solution.py:417
  138.9 8.0 %blocks_3.1 = (f32[8,1296,128]{2,1,0:T(8,128)}, bf16[2,1296,128]{2,1,0:T(8,128)(2,1)}) custom-call(s32[44]{0:T(128)} %dynamic-slice_bitcast_fusion.table, s32[4,4]{1,0:T(4,128)} %tile_map.13, f32[4,4]{1,0:T(4,128)} %gain_ref.13, f32[1,512]{1,0:T(1,128)} %bitcast.21, s32[1,512]{1,0:T(1,128)} %bitcast.28, ...), custom_call_target="tpu_custom_call", output_to_operand_aliasing={{0}: (19, {})} | custom-call | flops 1048576 | bytes 65536 | tf_op jit(solution)/shard_map/blocks_3/pallas_call | solution.py:388
  146.8 7.0 %collective-permute-done.15.refs_2_ = bf16[2,1296,128]{2,1,0:T(8,128)(2,1)S(1)} collective-permute-done((bf16[2,1296,128]{2,1,0:T(8,128)(2,1)}, bf16[2,1296,128]{2,1,0:T(8,128)(2,1)S(1)}, u32[]{:S(2)}, u32[]{:S(2)}) %collective-permute-start.15) | collective-permute-done | bytes 663584 | tf_op jit(solution)/shard_map/move_sums2/ppermute | solution.py:417
  155.2 4.3 %collective-permute-start.19 = (bf16[2,1296,128]{2,1,0:T(8,128)(2,1)}, bf16[2,1296,128]{2,1,0:T(8,128)(2,1)S(1)}, u32[]{:S(2)}, u32[]{:S(2)}) collective-permute-start(bf16[2,1296,128]{2,1,0:T(8,128)(2,1)} %get-tuple-element.88), channel_id=1, source_target_pairs={{0,1},{2,3},{3,2},{5,4},{6,7},{7,6},{8,9},{9,8},{10,11},{12,13},{1... | collective-permute-start | bytes 1990664 | tf_op jit(solution)/shard_map/move_sums3/ppermute | solution.py:417
  159.5 10.2 %blocks_4.1 = (f32[8,1296,128]{2,1,0:T(8,128)}, bf16[2,1296,128]{2,1,0:T(8,128)(2,1)}) custom-call(s32[44]{0:T(128)} %dynamic-slice_bitcast_fusion.table, s32[4,4]{1,0:T(4,128)} %tile_map.13, f32[4,4]{1,0:T(4,128)} %gain_ref.13, f32[1,512]{1,0:T(1,128)} %bitcast.22, s32[1,512]{1,0:T(1,128)} %bitcast.29, ...), custom_call_target="tpu_custom_call", output_to_operand_aliasing={{0}: (18, {})} | custom-call | flops 1048576 | bytes 65536 | tf_op jit(solution)/shard_map/blocks_4/pallas_call | solution.py:388
  169.7 1.3 collective-permute-start.20
  171.0 9.8 %blocks_5.1 = (f32[8,1296,128]{2,1,0:T(8,128)}, bf16[3,1296,128]{2,1,0:T(8,128)(2,1)}) custom-call(s32[44]{0:T(128)} %dynamic-slice_bitcast_fusion.table, s32[4,4]{1,0:T(4,128)} %tile_map.13, f32[4,4]{1,0:T(4,128)} %gain_ref.13, f32[1,512]{1,0:T(1,128)} %bitcast.23, s32[1,512]{1,0:T(1,128)} %bitcast.30, ...), custom_call_target="tpu_custom_call", output_to_operand_aliasing={{0}: (19, {})} | custom-call | flops 1048576 | bytes 65536 | tf_op jit(solution)/shard_map/blocks_5/pallas_call | solution.py:388
  180.8 8.8 %collective-permute-done.20.refs_4_ = bf16[2,1296,128]{2,1,0:T(8,128)(2,1)S(1)} collective-permute-done((bf16[2,1296,128]{2,1,0:T(8,128)(2,1)}, bf16[2,1296,128]{2,1,0:T(8,128)(2,1)S(1)}, u32[]{:S(2)}, u32[]{:S(2)}) %collective-permute-start.20) | collective-permute-done | bytes 663584 | tf_op jit(solution)/shard_map/move_sums4/ppermute | solution.py:417
  189.6 1.9 collective-permute-start.21
  191.5 5.8 %blocks_6.1.own = f32[8,1296,128]{2,1,0:T(8,128)} custom-call(s32[44]{0:T(128)} %dynamic-slice_bitcast_fusion.table, s32[4,4]{1,0:T(4,128)} %tile_map.13, f32[4,4]{1,0:T(4,128)} %gain_ref.13, f32[1,512]{1,0:T(1,128)} %bitcast.24, s32[1,512]{1,0:T(1,128)} %bitcast.31, bf16[6,288,512]{2,1,0:T(8,128)(2,1)} %copy-done.1, ...), custom_call_target="tpu_custom_call", output_to_operand_aliasing={{}: (11, {})} | custom-call | flops 1048576 | bytes 65536 | tf_op jit(solution)/shard_map/blocks_6/pallas_call | solution.py:388
  197.4 8.5 %collective-permute-done.21.refs_5_ = bf16[3,1296,128]{2,1,0:T(8,128)(2,1)S(1)} collective-permute-done((bf16[3,1296,128]{2,1,0:T(8,128)(2,1)}, bf16[3,1296,128]{2,1,0:T(8,128)(2,1)S(1)}, u32[]{:S(2)}, u32[]{:S(2)}) %collective-permute-start.21) | collective-permute-done | bytes 995360 | tf_op jit(solution)/shard_map/move_sums5/ppermute | solution.py:417
  206.9 8.6 %add_up.1 = f32[576,2,1152]{2,1,0:T(2,128)} custom-call(s32[44]{0:T(128)} %dynamic-slice_bitcast_fusion.table, f32[8,1296,128]{2,1,0:T(8,128)} %blocks_6.1.own, bf16[3,1296,128]{2,1,0:T(8,128)(2,1)} %collective-permute-done.8.refs_0_, bf16[3,1296,128]{2,1,0:T(8,128)(2,1)} %collective-permute-done.14.refs_1_, bf16[2,1296,128]{2,1,0:T(8,128)(2,1)} %copy-done.7, ...), custom_call_target="tpu_custom_call" | custom-call | tf_op jit(solution)/shard_map/add_up/pallas_call | solution.py:447
  (42 shorter events, 7.7 us)
Async XLA Ops:
  0.0 40.4 %collective-permute-start = (bf16[6,288,512]{2,1,0:T(8,128)(2,1)}, bf16[6,288,512]{2,1,0:T(8,128)(2,1)S(1)}, u32[]{:S(2)}, u32[]{:S(2)}) collective-permute-start(bf16[6,288,512]{2,1,0:T(8,128)(2,1)} %bitcast.6), channel_id=1, source_target_pairs={{4,2},{2,4},{12,10},{10,12},{20,18},{18,20},{28,26},{26,28},{6,0},... | collective-permute-start | bytes 5308424 | tf_op jit(solution)/shard_map/move_b/ppermute | solution.py:364
  1.4 59.5 %collective-permute-start.1 = (bf16[6,288,512]{2,1,0:T(8,128)(2,1)}, bf16[6,288,512]{2,1,0:T(8,128)(2,1)S(1)}, u32[]{:S(2)}, u32[]{:S(2)}) collective-permute-start(bf16[6,288,512]{2,1,0:T(8,128)(2,1)} %bitcast.7), channel_id=1, source_target_pairs={{2,0},{0,2},{6,4},{4,6},{10,8},{8,10},{14,12},{12,14},{18,16},{16,... | collective-permute-start | bytes 5308424 | tf_op jit(solution)/shard_map/move_a/ppermute | solution.py:364
  2.9 58.0 %collective-permute-start.2 = (bf16[6,288,512]{2,1,0:T(8,128)(2,1)}, bf16[6,288,512]{2,1,0:T(8,128)(2,1)}, u32[]{:S(2)}, u32[]{:S(2)}) collective-permute-start(bf16[6,288,512]{2,1,0:T(8,128)(2,1)} %bitcast.8), channel_id=1, source_target_pairs={{0,16},{10,26},{20,4},{30,14},{1,17},{11,27},{21,5},{31,15}} | collective-permute-start | bytes 5308424 | tf_op jit(solution)/shard_map/move_x0/ppermute | solution.py:364
  4.7 56.1 %collective-permute-start.3 = (bf16[6,288,512]{2,1,0:T(8,128)(2,1)}, bf16[6,288,512]{2,1,0:T(8,128)(2,1)S(1)}, u32[]{:S(2)}, u32[]{:S(2)}) collective-permute-start(bf16[6,288,512]{2,1,0:T(8,128)(2,1)} %bitcast.9), channel_id=1, source_target_pairs={{0,8},{10,2},{20,28},{30,22},{1,9},{11,3},{21,29},{31,23}} | collective-permute-start | bytes 5308424 | tf_op jit(solution)/shard_map/move_c0/ppermute | solution.py:364
  40.4 27.9 %copy-start = (bf16[6,288,512]{2,1,0:T(8,128)(2,1)}, bf16[6,288,512]{2,1,0:T(8,128)(2,1)S(1)}, u32[]{:S(2)}) copy-start(bf16[6,288,512]{2,1,0:T(8,128)(2,1)S(1)} %collective-permute-done.refs_1_.second_ref) | copy-start | bytes 5308420
  60.9 10.2 %copy-start.1 = (bf16[6,288,512]{2,1,0:T(8,128)(2,1)}, bf16[6,288,512]{2,1,0:T(8,128)(2,1)S(1)}, u32[]{:S(2)}) copy-start(bf16[6,288,512]{2,1,0:T(8,128)(2,1)S(1)} %collective-permute-done.1.refs_0_) | copy-start | bytes 5308420
  60.9 4.2 %copy-start.2 = (bf16[6,288,512]{2,1,0:T(8,128)(2,1)}, bf16[6,288,512]{2,1,0:T(8,128)(2,1)S(1)}, u32[]{:S(2)}) copy-start(bf16[6,288,512]{2,1,0:T(8,128)(2,1)S(1)} %collective-permute-done.3.refs_2_) | copy-start | bytes 5308420
  60.9 10.2 %collective-permute-start.6 = (bf16[6,288,512]{2,1,0:T(8,128)(2,1)S(1)}, bf16[6,288,512]{2,1,0:T(8,128)(2,1)}, u32[]{:S(2)}, u32[]{:S(2)}) collective-permute-start(bf16[6,288,512]{2,1,0:T(8,128)(2,1)S(1)} %collective-permute-done.refs_1_.second_ref), channel_id=1, source_target_pairs={{0,8},{10,2},{20,28},{30,22},{1,9},{11,3},{21,29},{31,23}} | collective-permute-start | bytes 5308424 | tf_op jit(solution)/shard_map/move_cb/ppermute | solution.py:364
  63.2 11.1 %collective-permute-start.5 = (bf16[6,288,512]{2,1,0:T(8,128)(2,1)S(1)}, bf16[6,288,512]{2,1,0:T(8,128)(2,1)}, u32[]{:S(2)}, u32[]{:S(2)}) collective-permute-start(bf16[6,288,512]{2,1,0:T(8,128)(2,1)S(1)} %collective-permute-done.1.refs_0_), channel_id=1, source_target_pairs={{0,8},{10,2},{20,28},{30,22},{1,9},{11,3},{21,29},{31,23}} | collective-permute-start | bytes 5308424 | tf_op jit(solution)/shard_map/move_ca/ppermute | solution.py:364
  65.1 9.2 %collective-permute-start.4 = (bf16[6,288,512]{2,1,0:T(8,128)(2,1)}, bf16[6,288,512]{2,1,0:T(8,128)(2,1)}, u32[]{:S(2)}, u32[]{:S(2)}) collective-permute-start(bf16[6,288,512]{2,1,0:T(8,128)(2,1)} %collective-permute-done.2.refs_7_.refs_6_.refs_10_.refs_11_), channel_id=1, source_target_pairs={{16,24},{26,18},{4,12},{14,6},{17,25},{27,19},{5,13},{15,7}} | collective-permute-start | bytes 5308424 | tf_op jit(solution)/shard_map/move_d0/ppermute | solution.py:364
  66.4 15.6 %collective-permute-start.7 = (bf16[6,288,512]{2,1,0:T(8,128)(2,1)S(1)}, bf16[6,288,512]{2,1,0:T(8,128)(2,1)}, u32[]{:S(2)}, u32[]{:S(2)}) collective-permute-start(bf16[6,288,512]{2,1,0:T(8,128)(2,1)S(1)} %collective-permute-done.refs_1_.second_ref), channel_id=1, source_target_pairs={{0,16},{10,26},{20,4},{30,14},{1,17},{11,27},{21,5},{31,15}} | collective-permute-start | bytes 5308424 | tf_op jit(solution)/shard_map/move_xb/ppermute | solution.py:364
  71.0 41.1 %collective-permute-start.10 = (bf16[6,288,512]{2,1,0:T(8,128)(2,1)}, bf16[6,288,512]{2,1,0:T(8,128)(2,1)}, u32[]{:S(2)}, u32[]{:S(2)}) collective-permute-start(bf16[6,288,512]{2,1,0:T(8,128)(2,1)} %pick.1), channel_id=1, source_target_pairs={{2,0},{6,2},{0,4},{4,6},{10,8},{14,10},{8,12},{12,14},{18,16},{22,... | collective-permute-start | bytes 5308424 | tf_op jit(solution)/shard_map/move_t/ppermute | solution.py:364
  71.1 41.0 %collective-permute-start.9 = (bf16[6,288,512]{2,1,0:T(8,128)(2,1)S(1)}, bf16[6,288,512]{2,1,0:T(8,128)(2,1)}, u32[]{:S(2)}, u32[]{:S(2)}) collective-permute-start(bf16[6,288,512]{2,1,0:T(8,128)(2,1)S(1)} %collective-permute-done.1.refs_0_), channel_id=1, source_target_pairs={{0,16},{10,26},{20,4},{30,14},{1,17},{11,27},{21,5},{31,15}} | collective-permute-start | bytes 5308424 | tf_op jit(solution)/shard_map/move_xa/ppermute | solution.py:364
  82.0 30.1 %collective-permute-start.8 = (bf16[3,1296,128]{2,1,0:T(8,128)(2,1)}, bf16[3,1296,128]{2,1,0:T(8,128)(2,1)}, u32[]{:S(2)}, u32[]{:S(2)}) collective-permute-start(bf16[3,1296,128]{2,1,0:T(8,128)(2,1)} %get-tuple-element.65), channel_id=1, source_target_pairs={{0,1},{1,0},{2,3},{3,2},{4,5},{6,7},{9,8},{10,11},{11,10},{12,13},... | collective-permute-start | bytes 2985992 | tf_op jit(solution)/shard_map/move_sums0/ppermute | solution.py:417
  86.6 31.9 %collective-permute-start.12 = (bf16[6,288,512]{2,1,0:T(8,128)(2,1)}, bf16[6,288,512]{2,1,0:T(8,128)(2,1)S(1)}, u32[]{:S(2)}, u32[]{:S(2)}) collective-permute-start(bf16[6,288,512]{2,1,0:T(8,128)(2,1)} %collective-permute-done.7.refs_7_.refs_12_.refs_13_), channel_id=1, source_target_pairs={{16,24},{26,18},{4,12},{14,6},{17,25},{27,19},{5,13},{15,7}} | collective-permute-start | bytes 5308424 | tf_op jit(solution)/shard_map/move_db/ppermute | solution.py:364
  112.1 8.1 %collective-permute-start.11 = (bf16[6,288,512]{2,1,0:T(8,128)(2,1)}, bf16[6,288,512]{2,1,0:T(8,128)(2,1)S(1)}, u32[]{:S(2)}, u32[]{:S(2)}) collective-permute-start(bf16[6,288,512]{2,1,0:T(8,128)(2,1)} %collective-permute-done.9.refs_11_.refs_12_), channel_id=1, source_target_pairs={{16,24},{26,18},{4,12},{14,6},{17,25},{27,19},{5,13},{15,7}} | collective-permute-start | bytes 5308424 | tf_op jit(solution)/shard_map/move_da/ppermute | solution.py:364
  113.4 22.1 %collective-permute-start.13 = (bf16[6,288,512]{2,1,0:T(8,128)(2,1)}, bf16[6,288,512]{2,1,0:T(8,128)(2,1)}, u32[]{:S(2)}, u32[]{:S(2)}) collective-permute-start(bf16[6,288,512]{2,1,0:T(8,128)(2,1)} %collective-permute-done.10.refs_9_.refs_10_.refs_11_.refs_12_.refs_5_), channel_id=1, source_target_pairs={{0,8},{10,2},{20,28},{30,22},{1,9},{11,3},{21,29},{31,23}} | collective-permute-start | bytes 5308424 | tf_op jit(solution)/shard_map/move_ct/ppermute | solution.py:364
  115.3 31.5 %collective-permute-start.16 = (bf16[6,288,512]{2,1,0:T(8,128)(2,1)}, bf16[6,288,512]{2,1,0:T(8,128)(2,1)}, u32[]{:S(2)}, u32[]{:S(2)}) collective-permute-start(bf16[6,288,512]{2,1,0:T(8,128)(2,1)} %collective-permute-done.10.refs_9_.refs_10_.refs_11_.refs_12_.refs_5_), channel_id=1, source_target_pairs={{0,16},{10,26},{20,4},{30,14},{1,17},{11,27},{21,5},{31,15}} | collective-permute-start | bytes 5308424 | tf_op jit(solution)/shard_map/move_xt/ppermute | solution.py:364
  117.2 29.6 %collective-permute-start.17 = (bf16[6,288,512]{2,1,0:T(8,128)(2,1)}, bf16[6,288,512]{2,1,0:T(8,128)(2,1)}, u32[]{:S(2)}, u32[]{:S(2)}) collective-permute-start(bf16[6,288,512]{2,1,0:T(8,128)(2,1)} %collective-permute-done.10.refs_9_.refs_10_.refs_11_.refs_12_.refs_5_), channel_id=1, source_target_pairs={{4,6},{10,8},{20,22},{26,24},{5,7},{11,9},{21,23},{27,25}} | collective-permute-start | bytes 5308424 | tf_op jit(solution)/shard_map/move_e/ppermute | solution.py:364
  118.5 1.6 copy-start.3
  118.5 28.3 %collective-permute-start.14 = (bf16[3,1296,128]{2,1,0:T(8,128)(2,1)}, bf16[3,1296,128]{2,1,0:T(8,128)(2,1)}, u32[]{:S(2)}, u32[]{:S(2)}) collective-permute-start(bf16[3,1296,128]{2,1,0:T(8,128)(2,1)} %get-tuple-element.77), channel_id=1, source_target_pairs={{1,0},{3,2},{4,5},{5,4},{9,8},{11,10},{14,15},{15,14},{16,17},{17,... | collective-permute-start | bytes 2985992 | tf_op jit(solution)/shard_map/move_sums1/ppermute | solution.py:417
  120.2 1.2 copy-start.4
  135.5 18.3 %collective-permute-start.15 = (bf16[2,1296,128]{2,1,0:T(8,128)(2,1)}, bf16[2,1296,128]{2,1,0:T(8,128)(2,1)S(1)}, u32[]{:S(2)}, u32[]{:S(2)}) collective-permute-start(bf16[2,1296,128]{2,1,0:T(8,128)(2,1)} %get-tuple-element.78), channel_id=1, source_target_pairs={{0,1},{1,0},{2,3},{4,5},{5,4},{6,7},{7,6},{8,9},{10,11},{11,10},{1... | collective-permute-start | bytes 1990664 | tf_op jit(solution)/shard_map/move_sums2/ppermute | solution.py:417
  153.9 15.7 %copy-start.7 = (bf16[2,1296,128]{2,1,0:T(8,128)(2,1)}, bf16[2,1296,128]{2,1,0:T(8,128)(2,1)S(1)}, u32[]{:S(2)}) copy-start(bf16[2,1296,128]{2,1,0:T(8,128)(2,1)S(1)} %collective-permute-done.15.refs_2_) | copy-start | bytes 1990660
  153.9 15.8 %collective-permute-start.18 = (bf16[6,288,512]{2,1,0:T(8,128)(2,1)}, bf16[6,288,512]{2,1,0:T(8,128)(2,1)S(1)}, u32[]{:S(2)}, u32[]{:S(2)}) collective-permute-start(bf16[6,288,512]{2,1,0:T(8,128)(2,1)} %collective-permute-done.16.refs_12_.refs_13_), channel_id=1, source_target_pairs={{16,24},{26,18},{4,12},{14,6},{17,25},{27,19},{5,13},{15,7}} | collective-permute-start | bytes 5308424 | tf_op jit(solution)/shard_map/move_dt/ppermute | solution.py:364
  155.2 25.6 %collective-permute-start.19 = (bf16[2,1296,128]{2,1,0:T(8,128)(2,1)}, bf16[2,1296,128]{2,1,0:T(8,128)(2,1)S(1)}, u32[]{:S(2)}, u32[]{:S(2)}) collective-permute-start(bf16[2,1296,128]{2,1,0:T(8,128)(2,1)} %get-tuple-element.88), channel_id=1, source_target_pairs={{0,1},{2,3},{3,2},{5,4},{6,7},{7,6},{8,9},{9,8},{10,11},{12,13},{1... | collective-permute-start | bytes 1990664 | tf_op jit(solution)/shard_map/move_sums3/ppermute | solution.py:417
  169.6 1.3 copy-start.5
  169.7 20.0 %collective-permute-start.20 = (bf16[2,1296,128]{2,1,0:T(8,128)(2,1)}, bf16[2,1296,128]{2,1,0:T(8,128)(2,1)S(1)}, u32[]{:S(2)}, u32[]{:S(2)}) collective-permute-start(bf16[2,1296,128]{2,1,0:T(8,128)(2,1)} %get-tuple-element.89), channel_id=1, source_target_pairs={{0,1},{2,3},{4,5},{5,4},{7,6},{8,9},{10,11},{14,15},{15,14},{16,17... | collective-permute-start | bytes 1990664 | tf_op jit(solution)/shard_map/move_sums4/ppermute | solution.py:417
  180.8 16.6 %copy-start.8 = (bf16[2,1296,128]{2,1,0:T(8,128)(2,1)}, bf16[2,1296,128]{2,1,0:T(8,128)(2,1)S(1)}, u32[]{:S(2)}) copy-start(bf16[2,1296,128]{2,1,0:T(8,128)(2,1)S(1)} %collective-permute-done.19.refs_3_) | copy-start | bytes 1990660
  189.6 7.8 %copy-start.9 = (bf16[2,1296,128]{2,1,0:T(8,128)(2,1)}, bf16[2,1296,128]{2,1,0:T(8,128)(2,1)S(1)}, u32[]{:S(2)}) copy-start(bf16[2,1296,128]{2,1,0:T(8,128)(2,1)S(1)} %collective-permute-done.20.refs_4_) | copy-start | bytes 1990660
  189.6 16.3 %collective-permute-start.21 = (bf16[3,1296,128]{2,1,0:T(8,128)(2,1)}, bf16[3,1296,128]{2,1,0:T(8,128)(2,1)S(1)}, u32[]{:S(2)}, u32[]{:S(2)}) collective-permute-start(bf16[3,1296,128]{2,1,0:T(8,128)(2,1)} %get-tuple-element.96), channel_id=1, source_target_pairs={{6,7},{7,6},{8,9},{12,13},{13,12},{18,19},{19,18},{23,22},{24,25},... | collective-permute-start | bytes 2985992 | tf_op jit(solution)/shard_map/move_sums5/ppermute | solution.py:417
  205.9 1.0 copy-start.6

commit v3 on v2

--- a/solution.py
+++ b/solution.py
@@ -9,16 +9,17 @@
 from jax.sharding import PartitionSpec as P
 
 LANES = 128
+KNOWN = 32
 ARRIVALS = (
-    (("own", "a", "b", "x0", "c0", "ca", "cb", "d0"), 5),
-    (("xb",), 5),
-    (("t", "xa", "da", "db"), 5),
+    (("own", "a", "b", "x0", "c0", "ca", "cb", "d0", "xa"), 5),
+    (("xb",), 6),
+    (("t", "da", "db"), 3),
     (("ct",), 4),
-    (("e", "xt"), 3),
+    (("e", "xt"), 2),
     (("dt",), 3),
     ((), 16),
 )
-SENDS = ((0, 3), (1, 3), (2, 2), (3, 2), (4, 2), (5, 3))
+SENDS = ((0, 3), (1, 2), (2, 2), (3, 2), (4, 2), (5, 3))
 
 
 def route(n):
@@ -92,7 +93,7 @@
                     plan = attempt(blocks, chosen)
                     if plan is None:
                         continue
-                    cost = sum(SENDS[i][1] * (1 + i) ** 2 for i in chosen), sum(e for e, i, _, _ in plan if i is not None)
+                    cost = sum(SENDS[i][1] * i**2 for i in chosen), sum(e * e for e, _, _, _ in plan)
                     if best is None or cost < best[0]:
                         best = cost, plan
                 used = {}
@@ -163,15 +164,15 @@
 def multiply_blocks(passed, results, base, sources, h, p, gap, table, tile_map, gain_ref, w_ref, group_ref, *refs):
     srcs = refs[:sources]
     refs = refs[sources + passed:]
-    own, out = refs[0], refs[results - 1]
-    raw, left, right, stage_own, stage_out, l_sem, r_sem, own_sem, out_sem = refs[results:]
+    own, weighed, out = refs[0], refs[1], refs[results - 1]
+    raw, left, right, stage_own, stage_out, raw_sem, l_sem, w_sem, r_sem, own_sem, out_sem = refs[results:]
     count = table[base]
     sign = table[2].astype(jnp.float32)
     scale = rate(w_ref, group_ref, gain_ref, tile_map[table[0], table[1]])
 
     def entry(t):
         code = table[base + 1 + t]
-        return code & 63, (code >> 6) & 63, (code >> 12) & 15, code >> 16
+        return code & 63, (code >> 6) & 63, (code >> 12) & 15, (code >> 16) & 255, code >> 24
 
     def stored(stage, target, sem, slot, place):
         return pltpu.make_async_copy(stage.at[slot], target.at[place], sem.at[slot])
@@ -193,68 +194,83 @@
             def _():
                 stored(stage, target, sem, lax.rem(done - back, 2), 0).wait()
 
-    def ask_row(t):
-        fetch(entry(t)[0], srcs, raw.at[lax.rem(t, 2)], l_sem.at[lax.rem(t, 2)], h, p, h)
+    def known(slot, plane):
+        return pltpu.make_async_copy(weighed.at[plane], left.at[slot], l_sem.at[slot])
+
+    def kept(slot, plane):
+        return pltpu.make_async_copy(left.at[slot], weighed.at[plane], w_sem)
+
+    def ask_row(t, slot):
+        row, plane = entry(t)[0], entry(t)[4]
+        fetch(row, srcs, raw, raw_sem, h, p, h)
+
+        @pl.when(row >= KNOWN)
+        def _():
+            known(slot, plane).start()
 
     def ask_column(t):
         fetch(entry(t)[1], srcs, right.at[lax.rem(t, 2)], r_sem.at[lax.rem(t, 2)], h, p, gap)
 
-    def weigh(slot):
-        for c in range(3):
-            part = raw[slot, :, c * p:(c + 1) * p].astype(jnp.float32)
-            left[slot, :, c * p:(c + 1) * p] = (part * scale).astype(jnp.bfloat16)
-
     @pl.when(count > 0)
     def _():
-        ask_row(0)
+        ask_row(0, 0)
         ask_column(0)
 
-        @pl.when(count > 1)
-        def _():
-            ask_row(1)
-
-        landed(srcs, raw.at[0], l_sem.at[0], h, p, h)
-        weigh(0)
-
     def task(t, carry):
-        owns, outs = carry
-        _, _, kind, place = entry(t)
+        before, side, owns, outs = carry
+        row, _, kind, place, plane = entry(t)
         slot = lax.rem(t, 2)
-        other = 1 - slot
+        changed = plane != before
+        side = jnp.where(changed, 1 - side, side)
+        fresh = jnp.logical_and(changed, row < KNOWN)
+
+        @pl.when(jnp.logical_and(changed, row >= KNOWN))
+        def _():
+            known(side, plane).wait()
+
+        @pl.when(fresh)
+        def _():
+            landed(srcs, raw, raw_sem, h, p, h)
+            for c in range(3):
+                part = raw[:, c * p:(c + 1) * p].astype(jnp.float32)
+                left[side, :, c * p:(c + 1) * p] = (part * scale).astype(jnp.bfloat16)
+            kept(side, plane).start()
 
         @pl.when(t + 1 < count)
         def _():
-            landed(srcs, raw.at[other], l_sem.at[other], h, p, h)
             ask_column(t + 1)
 
-        @pl.when(t + 2 < count)
-        def _():
-            ask_row(t + 2)
+            @pl.when(entry(t + 1)[4] != plane)
+            def _():
+                ask_row(t + 1, 1 - side)
 
         landed(srcs, right.at[slot], r_sem.at[slot], h, p, gap)
-        weigh(other)
         product = lax.dot_general(
-            left[slot], right[slot], (((1,), (1,)), ((), ())), preferred_element_type=jnp.float32
+            left[side], right[slot], (((1,), (1,)), ((), ())), preferred_element_type=jnp.float32
         )
         real = product[:h, :h] + sign * product[h:, gap:gap + h]
         imag = product[h:, :h] - sign * product[:h, gap:gap + h]
 
+        @pl.when(fresh)
+        def _():
+            kept(side, plane).wait()
+
         @pl.when(kind == 0)
         def _():
             store(stage_own, own, own_sem, owns, place, real, imag)
 
-        if results > 1:
+        if results > 2:
 
             @pl.when(kind == 1)
             def _():
                 store(stage_out, out, out_sem, outs, place, real, imag)
 
-        return owns + (kind == 0).astype(jnp.int32), outs + (kind == 1).astype(jnp.int32)
+        return plane, side, owns + (kind == 0).astype(jnp.int32), outs + (kind == 1).astype(jnp.int32)
 
     zero = jnp.int32(0)
-    owns, outs = lax.fori_loop(0, count, task, (zero, zero))
+    _, _, owns, outs = lax.fori_loop(0, count, task, (zero - 1, zero + 1, zero, zero))
     settle(stage_own, own, own_sem, owns)
-    if results > 1:
+    if results > 2:
         settle(stage_out, out, out_sem, outs)
 
 
@@ -265,49 +281,44 @@
     full, tail, quarter = h // LANES, h % LANES, h // 2
     wide = n * h // LANES
 
-    def load(b, slot):
-        pltpu.make_async_copy(own.at[b], mine.at[slot], m_sem.at[slot]).start()
+    def written(chunk, k):
+        return pltpu.make_async_copy(
+            image.at[chunk, pl.ds(2 * k * h, 2 * h)].reshape(h, 2, LANES),
+            out.at[pl.ds(chunk * h, h), :, pl.ds(k * LANES, LANES)],
+            o_sem.at[chunk],
+        )
+
+    for b in range(blocks):
+        pltpu.make_async_copy(own.at[b], mine.at[b], m_sem.at[b]).start()
         code = table[base + b]
         for k, recv in enumerate(recvs):
 
             @pl.when((code & 15) == k)
             def _():
-                pltpu.make_async_copy(recv.at[code >> 4], theirs.at[slot], t_sem.at[slot]).start()
-
-    def written(chunk, k):
-        return pltpu.make_async_copy(
-            image.at[chunk % 2, pl.ds(2 * k * h, 2 * h)].reshape(h, 2, LANES),
-            out.at[pl.ds(chunk * h, h), :, pl.ds(k * LANES, LANES)],
-            o_sem.at[chunk % 2],
-        )
-
-    load(0, 0)
+                pltpu.make_async_copy(recv.at[code >> 4], theirs.at[b], t_sem.at[b]).start()
+
     for b in range(blocks):
-        slot, chunk, kc = b % 2, b // n, b % n
-        if b + 1 < blocks:
-            load(b + 1, 1 - slot)
-        pltpu.make_async_copy(own.at[0], mine.at[slot], m_sem.at[slot]).wait()
-        pltpu.make_async_copy(recvs[0].at[0], theirs.at[slot], t_sem.at[slot]).wait()
+        chunk, kc = b // n, b % n
+        pltpu.make_async_copy(own.at[0], mine.at[b], m_sem.at[b]).wait()
+        pltpu.make_async_copy(recvs[0].at[0], theirs.at[b], t_sem.at[b]).wait()
         for part, line in ((0, real), (1, imag)):
             for k in range(full):
                 at = pl.ds((part * full + k) * h, h)
-                line[:, kc * h + k * LANES:kc * h + (k + 1) * LANES] = mine[slot, at, :] + theirs[
-                    slot, at, :
+                line[:, kc * h + k * LANES:kc * h + (k + 1) * LANES] = mine[b, at, :] + theirs[
+                    b, at, :
                 ].astype(jnp.float32)
             at = pl.ds(2 * full * h, quarter)
-            rest = mine[slot, at, :] + theirs[slot, at, :].astype(jnp.float32)
+            rest = mine[b, at, :] + theirs[b, at, :].astype(jnp.float32)
             for fold in range(2):
                 lane = (2 * fold + part) * tail
                 line[
                     fold * quarter:(fold + 1) * quarter, kc * h + full * LANES:(kc + 1) * h
                 ] = rest[:, lane:lane + tail]
-        if kc == n - 1:
-            buf = chunk % 2
+        first, last = kc * h // LANES, (kc + 1) * h // LANES
+        for k in range(first, last):
             for part, line in ((0, real), (1, imag)):
-                for k in range(wide):
-                    image[buf, pl.ds(2 * k * h + part, h, stride=2), :] = line[:, k * LANES:(k + 1) * LANES]
-            for k in range(wide):
-                written(chunk, k).start()
+                image[chunk, pl.ds(2 * k * h + part, h, stride=2), :] = line[:, k * LANES:(k + 1) * LANES]
+            written(chunk, k).start()
     for chunk in range(n // 2):
         for k in range(wide):
             written(chunk, k).wait()
@@ -323,9 +334,13 @@
     events = range(len(ARRIVALS))
 
     names = {e: set() for e in events}
-    for (r, j, _, e), items in tasks.items():
+    met = {}
+    for (r, j, y, e), items in tasks.items():
+        for kr, _, _, _ in items:
+            met[r, j, y, kr] = min(e, met.get((r, j, y, kr), e))
+    for (r, j, y, e), items in tasks.items():
         for kr, kc, _, _ in items:
-            names[e] |= {rows[r, j][kr], cols[r, j][kc]}
+            names[e] |= {cols[r, j][kc]} | ({rows[r, j][kr]} if met[r, j, y, kr] == e else set())
     names = {e: sorted(v) for e, v in names.items()}
     bases, size = {}, 3
     for e in events:
@@ -340,11 +355,14 @@
                 line = table[r, j, y]
                 line[:3] = r, j, 1 if r <= j else -1
                 for e in events:
-                    items = sorted(tasks.get((r, j, y, e), []), key=lambda i: (names[e].index(rows[r, j][i[0]]), -i[2], i[3]))
+                    items = tasks.get((r, j, y, e), [])
+                    leaving = {i[0]: -sum(x[2] for x in items if x[0] == i[0]) for i in items}
+                    items = sorted(items, key=lambda i: (leaving[i[0]], i[0], -i[2], i[3]))
                     line[bases[e]] = len(items)
                     for t, (kr, kc, kind, place) in enumerate(items):
-                        parts = names[e].index(rows[r, j][kr]) | names[e].index(cols[r, j][kc]) << 6
-                        line[bases[e] + 1 + t] = parts | kind << 12 | place << 16
+                        row = names[e].index(rows[r, j][kr]) if met[r, j, y, kr] == e else KNOWN
+                        code = row | names[e].index(cols[r, j][kc]) << 6 | kind << 12 | place << 16 | kr << 24
+                        line[bases[e] + 1 + t] = code
                 for i in range(half):
                     for kc in range(n):
                         index, place = arrives[r, j, y, y * half + i, kc]
@@ -354,7 +372,7 @@
         here = lax.axis_index("row"), lax.axis_index("col"), lax.axis_index("panel")
         line = lax.dynamic_slice(jnp.asarray(table), (*here, 0), (1, 1, 1, size)).reshape(size)
         weight, group = panel_weight[None, :], panel_group[None, :]
-        have = {"own": jnp.transpose(velocity, (1, 0, 2))}
+        have = {"own": jnp.transpose(velocity, (1, 0, 2)), "line": line}
         anywhere = pl.BlockSpec(memory_space=pl.ANY)
 
         def move(*given):
@@ -382,12 +400,15 @@
 
         def blocks(e):
             boxes = [i for i, x in enumerate(SENDS) if x[0] >= e][:1]
-            results = ["sums"] + [f"sent{i}" for i in boxes]
+            results = ["sums", "weighed"] + [f"sent{i}" for i in boxes]
             used = [have[k] for k in names[e]]
             carried = [(k, i) for i, k in enumerate(results) if k in have]
             made = pl.pallas_call(
                 functools.partial(multiply_blocks, len(carried), len(results), bases[e], len(used), h, p, gap),
-                out_shape=[jax.ShapeDtypeStruct((half * n, block, LANES), jnp.float32)]
+                out_shape=[
+                    jax.ShapeDtypeStruct((half * n, block, LANES), jnp.float32),
+                    jax.ShapeDtypeStruct((n, 2 * h, 3 * p), jnp.bfloat16),
+                ]
                 + [jax.ShapeDtypeStruct((SENDS[i][1], block, LANES), jnp.bfloat16) for i in boxes],
                 in_specs=[pl.BlockSpec(memory_space=pltpu.SMEM)] * 3
                 + [pl.BlockSpec(memory_space=pltpu.VMEM)] * 2
@@ -395,12 +416,14 @@
                 out_specs=[anywhere] * len(results),
                 input_output_aliases={5 + len(used) + at: i for at, (_, i) in enumerate(carried)},
                 scratch_shapes=[
-                    pltpu.VMEM((2, 2 * h, 3 * p), jnp.bfloat16),
+                    pltpu.VMEM((2 * h, 3 * p), jnp.bfloat16),
                     pltpu.VMEM((2, 2 * h, 3 * p), jnp.bfloat16),
                     pltpu.VMEM((2, gap + h, 3 * p), jnp.bfloat16),
                     pltpu.VMEM((2, block, LANES), jnp.float32),
                     pltpu.VMEM((2, block, LANES), jnp.bfloat16),
+                    pltpu.SemaphoreType.DMA,
                     pltpu.SemaphoreType.DMA((2,)),
+                    pltpu.SemaphoreType.DMA,
                     pltpu.SemaphoreType.DMA((2,)),
                     pltpu.SemaphoreType.DMA((2,)),
                     pltpu.SemaphoreType.DMA((2,)),
@@ -408,7 +431,7 @@
                 compiler_params=pltpu.CompilerParams(vmem_limit_bytes=60 << 20),
                 cost_estimate=pl.CostEstimate(flops=1 << 20, bytes_accessed=1 << 16, transcendentals=0),
                 name=f"blocks_{e}",
-            )(line, tile_map, group_gain, weight, group, *used, *(have[k] for k, _ in carried))
+            )(have["line"], tile_map, group_gain, weight, group, *used, *(have[k] for k, _ in carried))
             have.update(zip(results, made))
 
         def exchange(i):
@@ -417,15 +440,18 @@
                 have[f"got{i}"] = lax.ppermute(have[f"sent{i}"], ("row", "col", "panel"), ids)
 
         move("c0", "x0", "b", "a")
-        fence("own", "b", "a", "x0", "c0")
+        fence("own", "a", "x0", "c0", "line")
+        move("xa", "ca", "d0")
+        fence("b")
         choose("z", "own", "b")
-        move("t", "xa", "xb", "ca", "cb", "d0")
-        fence("d0", "ca", "cb")
+        fence("b", "z", "xa", "ca", "d0")
+        move("t", "xb", "cb")
+        fence("cb")
         blocks(0)
         fence("sums", "sent0", "xb")
         exchange(0)
         blocks(1)
-        fence("sums", "sent1", "got0", "xa", "t")
+        fence("sums", "sent1", "got0", "t")
         move("e", "xt", "ct", "da", "db")
         exchange(1)
         fence("da", "db")
@@ -450,18 +476,18 @@
             in_specs=[pl.BlockSpec(memory_space=pltpu.SMEM)] + [anywhere] * (1 + len(got)),
             out_specs=anywhere,
             scratch_shapes=[
-                pltpu.VMEM((2, block, LANES), jnp.float32),
-                pltpu.VMEM((2, block, LANES), jnp.bfloat16),
+                pltpu.VMEM((half * n, block, LANES), jnp.float32),
+                pltpu.VMEM((half * n, block, LANES), jnp.bfloat16),
                 pltpu.VMEM((h, n * h), jnp.float32),
                 pltpu.VMEM((h, n * h), jnp.float32),
-                pltpu.VMEM((2, 2 * h * n * h // LANES, LANES), jnp.float32),
-                pltpu.SemaphoreType.DMA((2,)),
-                pltpu.SemaphoreType.DMA((2,)),
-                pltpu.SemaphoreType.DMA((2,)),
+                pltpu.VMEM((half, 2 * h * n * h // LANES, LANES), jnp.float32),
+                pltpu.SemaphoreType.DMA((half * n,)),
+                pltpu.SemaphoreType.DMA((half * n,)),
+                pltpu.SemaphoreType.DMA((half,)),
             ],
             compiler_params=pltpu.CompilerParams(vmem_limit_bytes=60 << 20),
             name="add_up",
-        )(line, have["sums"], *got)
+        )(have["line"], have["sums"], *got)
 
     return local
 

time: 217 us -> 208 us (0.959)
  waiting for transfers between devices: 103 us -> 96.3 us
  Pallas kernels: 67.9 us -> 63.6 us
  local copies, waits for them, and re-layouts: 3.4 us -> 5.93 us
    ppermute x16, waiting for transfers between devices: 78.7 us -> 73.6 us  [move(): have[name] = lax.ppermute(have[source[name]], ('row', 'col'), ids)]
    pallas_call x1, Pallas kernels: 8.64 us -> 6.03 us  [local(): pl.pallas_call(functools.partial(add_up, final, n, h), out_shape=jax.Shap...]
    unnamed x20 -> x22, local copies, waits for them, and re-layouts: 2.22 us -> 4.69 us
    ppermute x6, starting transfers between devices: 17 us -> 14.6 us  [exchange(): lax.ppermute(have[f'sent{i}'], ('row', 'col', 'panel'), ids)]
  transfers between devices with their start and end apart: 22 -> 22, of which waited for: 6 -> 6; matrix products, arithmetic and copies ran while one was open for 1% -> 1% of each run, Pallas kernels for 27% -> 28%
where the time goes in v3:
time: 208 us; the launch traced here: 206 us
  waiting for transfers between devices  96.3 us (46%)
  Pallas kernels  63.6 us (31%)
  starting transfers between devices  40 us (19%)
  local copies, waits for them, and re-layouts  5.93 us (3%)
    ppermute x16, waiting for transfers between devices, move(): have[name] = lax.ppermute(have[source[name]], ('row', 'col'), ids)  73.6 us
    pallas_call x7, Pallas kernels, blocks(): pl.pallas_call(functools.partial(multiply_blocks, len(carried), len(resul...  54.9 us
    ppermute x16, starting transfers between devices, move(): have[name] = lax.ppermute(have[source[name]], ('row', 'col'), ids)  25.4 us
    ppermute x6, waiting for transfers between devices, exchange(): lax.ppermute(have[f'sent{i}'], ('row', 'col', 'panel'), ids)  22.6 us
    ppermute x6, starting transfers between devices, exchange(): lax.ppermute(have[f'sent{i}'], ('row', 'col', 'panel'), ids)  14.6 us
    pallas_call x1, Pallas kernels, local(): pl.pallas_call(functools.partial(add_up, final, n, h), out_shape=jax.Shap...  6.03 us
    unnamed x22, local copies, waits for them, and re-layouts  4.69 us
  transfers between devices with their start and end apart: 22, of which 6 were waited for; matrix products, arithmetic and copies ran while one was open for 1% of the time, Pallas kernels for 28%

profile of v3, /device:TPU:24, one launch (start us, length us, event | category | flops | bytes accessed | tf_op | source)
XLA Modules:
  0.0 206.3 jit_solution(17274073134674904315)
XLA Ops:
  2.0 7.9 %collective-permute-start.3 = (bf16[6,288,512]{2,1,0:T(8,128)(2,1)}, bf16[6,288,512]{2,1,0:T(8,128)(2,1)}, u32[]{:S(2)}, u32[]{:S(2)}) collective-permute-start(bf16[6,288,512]{2,1,0:T(8,128)(2,1)} %bitcast.9), channel_id=1, source_target_pairs={{4,2},{2,4},{12,10},{10,12},{20,18},{18,20},{28,26},{26,28},{6,0},... | collective-permute-start | bytes 5308424 | tf_op jit(solution)/shard_map/move_b/ppermute | solution.py:382
  9.9 1.2 dynamic-slice_bitcast_fusion.table
  11.2 48.5 %collective-permute-done.refs_0_ = bf16[6,288,512]{2,1,0:T(8,128)(2,1)} collective-permute-done((bf16[6,288,512]{2,1,0:T(8,128)(2,1)}, bf16[6,288,512]{2,1,0:T(8,128)(2,1)}, u32[]{:S(2)}, u32[]{:S(2)}) %collective-permute-start) | collective-permute-done | bytes 1769504 | tf_op jit(solution)/shard_map/move_a/ppermute | solution.py:382
  59.6 1.3 copy-done.3
  60.9 1.9 collective-permute-start.4
  63.6 1.3 collective-permute-start.6
  64.9 2.7 %pick.1 = bf16[6,288,512]{2,1,0:T(8,128)(2,1)} custom-call(s32[1]{0:T(128)} %bitcast.4.second, bf16[6,288,512]{2,1,0:T(8,128)(2,1)} %bitcast.10, bf16[6,288,512]{2,1,0:T(8,128)(2,1)} %collective-permute-done.3.second_ref.refs_1_), custom_call_target="tpu_custom_call" | custom-call | flops 1024 | bytes 1024 | tf_op jit(solution)/shard_map/pick/pallas_call | solution.py:386
  67.7 1.9 collective-permute-done.6.refs_5_.refs_6_.refs_4_
  70.3 1.9 collective-permute-start.9
  73.4 8.0 %blocks_0.1 = (f32[8,1296,128]{2,1,0:T(8,128)}, bf16[4,576,1536]{2,1,0:T(8,128)(2,1)}, bf16[3,1296,128]{2,1,0:T(8,128)(2,1)}) custom-call(s32[41]{0:T(128)} %dynamic-slice_bitcast_fusion.table, s32[4,4]{1,0:T(4,128)} %tile_map.13, f32[4,4]{1,0:T(4,128)} %gain_ref.13, f32[1,512]{1,0:T(1,128)} %bitcast.16, s32[1,512]{1,0:T(1,128)} %bitcast.23, ...), custom_call_target="tpu_custom_call" | custom-call | flops 1048576 | bytes 65536 | tf_op jit(solution)/shard_map/blocks_0/pallas_call | solution.py:406
  81.5 4.6 %collective-permute-start.11 = (bf16[3,1296,128]{2,1,0:T(8,128)(2,1)}, bf16[3,1296,128]{2,1,0:T(8,128)(2,1)}, u32[]{:S(2)}, u32[]{:S(2)}) collective-permute-start(bf16[3,1296,128]{2,1,0:T(8,128)(2,1)} %get-tuple-element.77), channel_id=1, source_target_pairs={{0,1},{1,0},{2,3},{3,2},{4,5},{5,4},{6,7},{9,8},{10,11},{11,10},{1... | collective-permute-start | bytes 2985992 | tf_op jit(solution)/shard_map/move_sums0/ppermute | solution.py:440
  86.1 1.3 collective-permute-start.8
  87.4 1.3 collective-permute-start.10
  89.7 23.3 %collective-permute-done.12.refs_9_.refs_10_ = bf16[6,288,512]{2,1,0:T(8,128)(2,1)} collective-permute-done((bf16[6,288,512]{2,1,0:T(8,128)(2,1)}, bf16[6,288,512]{2,1,0:T(8,128)(2,1)}, u32[]{:S(2)}, u32[]{:S(2)}) %collective-permute-start.12) | collective-permute-done | bytes 1769504 | tf_op jit(solution)/shard_map/move_t/ppermute | solution.py:382
  113.0 1.9 collective-permute-start.13
  114.8 1.9 collective-permute-start.16
  116.7 1.3 collective-permute-start.17
  118.0 1.5 collective-permute-start.14
  120.7 9.6 %blocks_2.1 = (f32[8,1296,128]{2,1,0:T(8,128)}, bf16[4,576,1536]{2,1,0:T(8,128)(2,1)}, bf16[2,1296,128]{2,1,0:T(8,128)(2,1)}) custom-call(s32[41]{0:T(128)} %dynamic-slice_bitcast_fusion.table, s32[4,4]{1,0:T(4,128)} %tile_map.13, f32[4,4]{1,0:T(4,128)} %gain_ref.13, f32[1,512]{1,0:T(1,128)} %bitcast.18, ...), custom_call_target="tpu_custom_call", output_to_operand_aliasing={{0}: (18, {}), {1}: (19, {})} | custom-call | flops 1048576 | bytes 65536 | tf_op jit(solution)/shard_map/blocks_2/pallas_call | solution.py:406
  130.4 1.7 collective-permute-start.15
  132.0 11.2 %blocks_3.1 = (f32[8,1296,128]{2,1,0:T(8,128)}, bf16[4,576,1536]{2,1,0:T(8,128)(2,1)}, bf16[2,1296,128]{2,1,0:T(8,128)(2,1)}) custom-call(s32[41]{0:T(128)} %dynamic-slice_bitcast_fusion.table, s32[4,4]{1,0:T(4,128)} %tile_map.13, f32[4,4]{1,0:T(4,128)} %gain_ref.13, f32[1,512]{1,0:T(1,128)} %bitcast.19, ...), custom_call_target="tpu_custom_call", output_to_operand_aliasing={{0}: (19, {}), {1}: (20, {})} | custom-call | flops 1048576 | bytes 65536 | tf_op jit(solution)/shard_map/blocks_3/pallas_call | solution.py:406
  143.3 4.4 %collective-permute-done.15.refs_2_ = bf16[2,1296,128]{2,1,0:T(8,128)(2,1)S(1)} collective-permute-done((bf16[2,1296,128]{2,1,0:T(8,128)(2,1)}, bf16[2,1296,128]{2,1,0:T(8,128)(2,1)S(1)}, u32[]{:S(2)}, u32[]{:S(2)}) %collective-permute-start.15) | collective-permute-done | bytes 663584 | tf_op jit(solution)/shard_map/move_sums2/ppermute | solution.py:440
  147.7 1.3 collective-permute-start.18
  149.0 3.7 %collective-permute-start.19 = (bf16[2,1296,128]{2,1,0:T(8,128)(2,1)}, bf16[2,1296,128]{2,1,0:T(8,128)(2,1)S(1)}, u32[]{:S(2)}, u32[]{:S(2)}) collective-permute-start(bf16[2,1296,128]{2,1,0:T(8,128)(2,1)} %get-tuple-element.102), channel_id=1, source_target_pairs={{0,1},{1,0},{2,3},{3,2},{5,4},{6,7},{7,6},{8,9},{9,8},{10,11},{11,... | collective-permute-start | bytes 1990664 | tf_op jit(solution)/shard_map/move_sums3/ppermute | solution.py:440
  152.7 7.8 %blocks_4.1 = (f32[8,1296,128]{2,1,0:T(8,128)}, bf16[4,576,1536]{2,1,0:T(8,128)(2,1)}, bf16[2,1296,128]{2,1,0:T(8,128)(2,1)}) custom-call(s32[41]{0:T(128)} %dynamic-slice_bitcast_fusion.table, s32[4,4]{1,0:T(4,128)} %tile_map.13, f32[4,4]{1,0:T(4,128)} %gain_ref.13, f32[1,512]{1,0:T(1,128)} %bitcast.20, ...), custom_call_target="tpu_custom_call", output_to_operand_aliasing={{0}: (16, {}), {1}: (17, {})} | custom-call | flops 1048576 | bytes 65536 | tf_op jit(solution)/shard_map/blocks_4/pallas_call | solution.py:406
  160.5 1.3 collective-permute-start.20
  161.9 9.7 %blocks_5.1 = (f32[8,1296,128]{2,1,0:T(8,128)}, bf16[4,576,1536]{2,1,0:T(8,128)(2,1)}, bf16[3,1296,128]{2,1,0:T(8,128)(2,1)}) custom-call(s32[41]{0:T(128)} %dynamic-slice_bitcast_fusion.table, s32[4,4]{1,0:T(4,128)} %tile_map.13, f32[4,4]{1,0:T(4,128)} %gain_ref.13, f32[1,512]{1,0:T(1,128)} %bitcast.21, ...), custom_call_target="tpu_custom_call", output_to_operand_aliasing={{0}: (14, {}), {1}: (15, {})} | custom-call | flops 1048576 | bytes 65536 | tf_op jit(solution)/shard_map/blocks_5/pallas_call | solution.py:406
  171.6 11.2 %collective-permute-done.20.refs_4_ = bf16[2,1296,128]{2,1,0:T(8,128)(2,1)S(1)} collective-permute-done((bf16[2,1296,128]{2,1,0:T(8,128)(2,1)}, bf16[2,1296,128]{2,1,0:T(8,128)(2,1)S(1)}, u32[]{:S(2)}, u32[]{:S(2)}) %collective-permute-start.20) | collective-permute-done | bytes 663584 | tf_op jit(solution)/shard_map/move_sums4/ppermute | solution.py:440
  182.8 1.9 collective-permute-start.21
  184.8 7.4 %blocks_6.1 = (f32[8,1296,128]{2,1,0:T(8,128)}, bf16[4,576,1536]{2,1,0:T(8,128)(2,1)}) custom-call(s32[41]{0:T(128)} %dynamic-slice_bitcast_fusion.table, s32[4,4]{1,0:T(4,128)} %tile_map.13, f32[4,4]{1,0:T(4,128)} %gain_ref.13, f32[1,512]{1,0:T(1,128)} %bitcast.22, s32[1,512]{1,0:T(1,128)} %bitcast.29, ...), custom_call_target="tpu_custom_call", output_to_operand_aliasing={{0}: (6, {}), {1}: (7, {})} | custom-call | flops 1048576 | bytes 65536 | tf_op jit(solution)/shard_map/blocks_6/pallas_call | solution.py:406
  192.2 7.0 %collective-permute-done.21.refs_5_ = bf16[3,1296,128]{2,1,0:T(8,128)(2,1)S(1)} collective-permute-done((bf16[3,1296,128]{2,1,0:T(8,128)(2,1)}, bf16[3,1296,128]{2,1,0:T(8,128)(2,1)S(1)}, u32[]{:S(2)}, u32[]{:S(2)}) %collective-permute-start.21) | collective-permute-done | bytes 995360 | tf_op jit(solution)/shard_map/move_sums5/ppermute | solution.py:440
  200.1 6.0 %add_up.1 = f32[576,2,1152]{2,1,0:T(2,128)} custom-call(s32[41]{0:T(128)} %dynamic-slice_bitcast_fusion.table, f32[8,1296,128]{2,1,0:T(8,128)} %get-tuple-element.106.own, bf16[3,1296,128]{2,1,0:T(8,128)(2,1)} %collective-permute-done.11.refs_0_, bf16[2,1296,128]{2,1,0:T(8,128)(2,1)} %collective-permute-done.14.refs_1_, bf16[2,1296,128]{2,1,0:T(8,128)(2,1)} %copy-done.8, ...), custom_call_target="tpu_custom_call" | custom-call | tf_op jit(solution)/shard_map/add_up/pallas_call | solution.py:473
  (44 shorter events, 8.0 us)
Async XLA Ops:
  0.0 59.6 %collective-permute-start = (bf16[6,288,512]{2,1,0:T(8,128)(2,1)}, bf16[6,288,512]{2,1,0:T(8,128)(2,1)}, u32[]{:S(2)}, u32[]{:S(2)}) collective-permute-start(bf16[6,288,512]{2,1,0:T(8,128)(2,1)} %bitcast.6), channel_id=1, source_target_pairs={{2,0},{0,2},{6,4},{4,6},{10,8},{8,10},{14,12},{12,14},{18,16},{16,... | collective-permute-start | bytes 5308424 | tf_op jit(solution)/shard_map/move_a/ppermute | solution.py:382
  0.5 59.2 %collective-permute-start.1 = (bf16[6,288,512]{2,1,0:T(8,128)(2,1)}, bf16[6,288,512]{2,1,0:T(8,128)(2,1)S(1)}, u32[]{:S(2)}, u32[]{:S(2)}) collective-permute-start(bf16[6,288,512]{2,1,0:T(8,128)(2,1)} %bitcast.7), channel_id=1, source_target_pairs={{0,16},{10,26},{20,4},{30,14},{1,17},{11,27},{21,5},{31,15}} | collective-permute-start | bytes 5308424 | tf_op jit(solution)/shard_map/move_x0/ppermute | solution.py:382
  1.2 58.4 %collective-permute-start.2 = (bf16[6,288,512]{2,1,0:T(8,128)(2,1)}, bf16[6,288,512]{2,1,0:T(8,128)(2,1)S(1)}, u32[]{:S(2)}, u32[]{:S(2)}) collective-permute-start(bf16[6,288,512]{2,1,0:T(8,128)(2,1)} %bitcast.8), channel_id=1, source_target_pairs={{0,8},{10,2},{20,28},{30,22},{1,9},{11,3},{21,29},{31,23}} | collective-permute-start | bytes 5308424 | tf_op jit(solution)/shard_map/move_c0/ppermute | solution.py:382
  2.0 62.9 %collective-permute-start.3 = (bf16[6,288,512]{2,1,0:T(8,128)(2,1)}, bf16[6,288,512]{2,1,0:T(8,128)(2,1)}, u32[]{:S(2)}, u32[]{:S(2)}) collective-permute-start(bf16[6,288,512]{2,1,0:T(8,128)(2,1)} %bitcast.9), channel_id=1, source_target_pairs={{4,2},{2,4},{12,10},{10,12},{20,18},{18,20},{28,26},{26,28},{6,0},... | collective-permute-start | bytes 5308424 | tf_op jit(solution)/shard_map/move_b/ppermute | solution.py:382
  59.6 1.3 copy-start.3
  60.9 6.7 %copy-start = (bf16[6,288,512]{2,1,0:T(8,128)(2,1)}, bf16[6,288,512]{2,1,0:T(8,128)(2,1)S(1)}, u32[]{:S(2)}) copy-start(bf16[6,288,512]{2,1,0:T(8,128)(2,1)S(1)} %collective-permute-done.2.refs_2_.refs_0_) | copy-start | bytes 5308420
  60.9 6.7 %collective-permute-start.4 = (bf16[6,288,512]{2,1,0:T(8,128)(2,1)}, bf16[6,288,512]{2,1,0:T(8,128)(2,1)}, u32[]{:S(2)}, u32[]{:S(2)}) collective-permute-start(bf16[6,288,512]{2,1,0:T(8,128)(2,1)} %collective-permute-done.refs_0_), channel_id=1, source_target_pairs={{0,16},{10,26},{20,4},{30,14},{1,17},{11,27},{21,5},{31,15}} | collective-permute-start | bytes 5308424 | tf_op jit(solution)/shard_map/move_xa/ppermute | solution.py:382
  62.8 4.8 %collective-permute-start.5 = (bf16[6,288,512]{2,1,0:T(8,128)(2,1)}, bf16[6,288,512]{2,1,0:T(8,128)(2,1)S(1)}, u32[]{:S(2)}, u32[]{:S(2)}) collective-permute-start(bf16[6,288,512]{2,1,0:T(8,128)(2,1)} %collective-permute-done.refs_0_), channel_id=1, source_target_pairs={{0,8},{10,2},{20,28},{30,22},{1,9},{11,3},{21,29},{31,23}} | collective-permute-start | bytes 5308424 | tf_op jit(solution)/shard_map/move_ca/ppermute | solution.py:382
  63.6 5.9 %collective-permute-start.6 = (bf16[6,288,512]{2,1,0:T(8,128)(2,1)}, bf16[6,288,512]{2,1,0:T(8,128)(2,1)}, u32[]{:S(2)}, u32[]{:S(2)}) collective-permute-start(bf16[6,288,512]{2,1,0:T(8,128)(2,1)} %copy-done.3), channel_id=1, source_target_pairs={{16,24},{26,18},{4,12},{14,6},{17,25},{27,19},{5,13},{15,7}} | collective-permute-start | bytes 5308424 | tf_op jit(solution)/shard_map/move_d0/ppermute | solution.py:382
  67.6 4.6 %copy-start.1 = (bf16[6,288,512]{2,1,0:T(8,128)(2,1)}, bf16[6,288,512]{2,1,0:T(8,128)(2,1)S(1)}, u32[]{:S(2)}) copy-start(bf16[6,288,512]{2,1,0:T(8,128)(2,1)S(1)} %collective-permute-done.5.refs_3_.refs_1_) | copy-start | bytes 5308420
  69.5 2.7 %collective-permute-start.7 = (bf16[6,288,512]{2,1,0:T(8,128)(2,1)}, bf16[6,288,512]{2,1,0:T(8,128)(2,1)S(1)}, u32[]{:S(2)}, u32[]{:S(2)}) collective-permute-start(bf16[6,288,512]{2,1,0:T(8,128)(2,1)} %collective-permute-done.3.second_ref.refs_1_), channel_id=1, source_target_pairs={{0,8},{10,2},{20,28},{30,22},{1,9},{11,3},{21,29},{31,23}} | collective-permute-start | bytes 5308424 | tf_op jit(solution)/shard_map/move_cb/ppermute | solution.py:382
  70.3 11.2 %collective-permute-start.9 = (bf16[6,288,512]{2,1,0:T(8,128)(2,1)}, bf16[6,288,512]{2,1,0:T(8,128)(2,1)}, u32[]{:S(2)}, u32[]{:S(2)}) collective-permute-start(bf16[6,288,512]{2,1,0:T(8,128)(2,1)} %collective-permute-done.3.second_ref.refs_1_), channel_id=1, source_target_pairs={{0,16},{10,26},{20,4},{30,14},{1,17},{11,27},{21,5},{31,15}} | collective-permute-start | bytes 5308424 | tf_op jit(solution)/shard_map/move_xb/ppermute | solution.py:382
  72.2 40.7 %collective-permute-start.12 = (bf16[6,288,512]{2,1,0:T(8,128)(2,1)}, bf16[6,288,512]{2,1,0:T(8,128)(2,1)}, u32[]{:S(2)}, u32[]{:S(2)}) collective-permute-start(bf16[6,288,512]{2,1,0:T(8,128)(2,1)} %pick.1), channel_id=1, source_target_pairs={{2,0},{6,2},{0,4},{4,6},{10,8},{14,10},{8,12},{12,14},{18,16},{22,... | collective-permute-start | bytes 5308424 | tf_op jit(solution)/shard_map/move_t/ppermute | solution.py:382
  72.2 1.2 copy-start.2
  81.5 31.4 %collective-permute-start.11 = (bf16[3,1296,128]{2,1,0:T(8,128)(2,1)}, bf16[3,1296,128]{2,1,0:T(8,128)(2,1)}, u32[]{:S(2)}, u32[]{:S(2)}) collective-permute-start(bf16[3,1296,128]{2,1,0:T(8,128)(2,1)} %get-tuple-element.77), channel_id=1, source_target_pairs={{0,1},{1,0},{2,3},{3,2},{4,5},{5,4},{6,7},{9,8},{10,11},{11,10},{1... | collective-permute-start | bytes 2985992 | tf_op jit(solution)/shard_map/move_sums0/ppermute | solution.py:440
  86.1 31.9 %collective-permute-start.8 = (bf16[6,288,512]{2,1,0:T(8,128)(2,1)}, bf16[6,288,512]{2,1,0:T(8,128)(2,1)S(1)}, u32[]{:S(2)}, u32[]{:S(2)}) collective-permute-start(bf16[6,288,512]{2,1,0:T(8,128)(2,1)} %collective-permute-done.4.refs_8_.refs_7_.refs_11_.refs_12_), channel_id=1, source_target_pairs={{16,24},{26,18},{4,12},{14,6},{17,25},{27,19},{5,13},{15,7}} | collective-permute-start | bytes 5308424 | tf_op jit(solution)/shard_map/move_da/ppermute | solution.py:382
  87.4 32.2 %collective-permute-start.10 = (bf16[6,288,512]{2,1,0:T(8,128)(2,1)}, bf16[6,288,512]{2,1,0:T(8,128)(2,1)S(1)}, u32[]{:S(2)}, u32[]{:S(2)}) collective-permute-start(bf16[6,288,512]{2,1,0:T(8,128)(2,1)} %collective-permute-done.9.refs_8_.refs_12_.refs_13_), channel_id=1, source_target_pairs={{16,24},{26,18},{4,12},{14,6},{17,25},{27,19},{5,13},{15,7}} | collective-permute-start | bytes 5308424 | tf_op jit(solution)/shard_map/move_db/ppermute | solution.py:382
  113.0 17.4 %collective-permute-start.13 = (bf16[6,288,512]{2,1,0:T(8,128)(2,1)}, bf16[6,288,512]{2,1,0:T(8,128)(2,1)}, u32[]{:S(2)}, u32[]{:S(2)}) collective-permute-start(bf16[6,288,512]{2,1,0:T(8,128)(2,1)} %collective-permute-done.12.refs_9_.refs_10_), channel_id=1, source_target_pairs={{0,8},{10,2},{20,28},{30,22},{1,9},{11,3},{21,29},{31,23}} | collective-permute-start | bytes 5308424 | tf_op jit(solution)/shard_map/move_ct/ppermute | solution.py:382
  114.8 28.5 %collective-permute-start.16 = (bf16[6,288,512]{2,1,0:T(8,128)(2,1)}, bf16[6,288,512]{2,1,0:T(8,128)(2,1)}, u32[]{:S(2)}, u32[]{:S(2)}) collective-permute-start(bf16[6,288,512]{2,1,0:T(8,128)(2,1)} %collective-permute-done.12.refs_9_.refs_10_), channel_id=1, source_target_pairs={{0,16},{10,26},{20,4},{30,14},{1,17},{11,27},{21,5},{31,15}} | collective-permute-start | bytes 5308424 | tf_op jit(solution)/shard_map/move_xt/ppermute | solution.py:382
  116.7 26.6 %collective-permute-start.17 = (bf16[6,288,512]{2,1,0:T(8,128)(2,1)}, bf16[6,288,512]{2,1,0:T(8,128)(2,1)}, u32[]{:S(2)}, u32[]{:S(2)}) collective-permute-start(bf16[6,288,512]{2,1,0:T(8,128)(2,1)} %collective-permute-done.12.refs_9_.refs_10_), channel_id=1, source_target_pairs={{4,6},{10,8},{20,22},{26,24},{5,7},{11,9},{21,23},{27,25}} | collective-permute-start | bytes 5308424 | tf_op jit(solution)/shard_map/move_e/ppermute | solution.py:382
  118.0 1.5 copy-start.4
  118.0 25.3 %collective-permute-start.14 = (bf16[2,1296,128]{2,1,0:T(8,128)(2,1)}, bf16[2,1296,128]{2,1,0:T(8,128)(2,1)}, u32[]{:S(2)}, u32[]{:S(2)}) collective-permute-start(bf16[2,1296,128]{2,1,0:T(8,128)(2,1)} %get-tuple-element.89), channel_id=1, source_target_pairs={{1,0},{3,2},{4,5},{9,8},{11,10},{14,15},{17,16},{20,21},{22,23},{2... | collective-permute-start | bytes 1990664 | tf_op jit(solution)/shard_map/move_sums1/ppermute | solution.py:440
  119.5 1.2 copy-start.5
  130.4 17.3 %collective-permute-start.15 = (bf16[2,1296,128]{2,1,0:T(8,128)(2,1)}, bf16[2,1296,128]{2,1,0:T(8,128)(2,1)S(1)}, u32[]{:S(2)}, u32[]{:S(2)}) collective-permute-start(bf16[2,1296,128]{2,1,0:T(8,128)(2,1)} %get-tuple-element.90), channel_id=1, source_target_pairs={{0,1},{1,0},{2,3},{3,2},{4,5},{5,4},{6,7},{7,6},{8,9},{9,8},{10,11... | collective-permute-start | bytes 1990664 | tf_op jit(solution)/shard_map/move_sums2/ppermute | solution.py:440
  147.7 12.8 %copy-start.8 = (bf16[2,1296,128]{2,1,0:T(8,128)(2,1)}, bf16[2,1296,128]{2,1,0:T(8,128)(2,1)S(1)}, u32[]{:S(2)}) copy-start(bf16[2,1296,128]{2,1,0:T(8,128)(2,1)S(1)} %collective-permute-done.15.refs_2_) | copy-start | bytes 1990660
  147.7 12.8 %collective-permute-start.18 = (bf16[6,288,512]{2,1,0:T(8,128)(2,1)}, bf16[6,288,512]{2,1,0:T(8,128)(2,1)S(1)}, u32[]{:S(2)}, u32[]{:S(2)}) collective-permute-start(bf16[6,288,512]{2,1,0:T(8,128)(2,1)} %collective-permute-done.16.refs_10_.refs_8_), channel_id=1, source_target_pairs={{16,24},{26,18},{4,12},{14,6},{17,25},{27,19},{5,13},{15,7}} | collective-permute-start | bytes 5308424 | tf_op jit(solution)/shard_map/move_dt/ppermute | solution.py:382
  149.0 22.6 %collective-permute-start.19 = (bf16[2,1296,128]{2,1,0:T(8,128)(2,1)}, bf16[2,1296,128]{2,1,0:T(8,128)(2,1)S(1)}, u32[]{:S(2)}, u32[]{:S(2)}) collective-permute-start(bf16[2,1296,128]{2,1,0:T(8,128)(2,1)} %get-tuple-element.102), channel_id=1, source_target_pairs={{0,1},{1,0},{2,3},{3,2},{5,4},{6,7},{7,6},{8,9},{9,8},{10,11},{11,... | collective-permute-start | bytes 1990664 | tf_op jit(solution)/shard_map/move_sums3/ppermute | solution.py:440
  160.5 1.3 copy-start.6
  160.5 22.3 %collective-permute-start.20 = (bf16[2,1296,128]{2,1,0:T(8,128)(2,1)}, bf16[2,1296,128]{2,1,0:T(8,128)(2,1)S(1)}, u32[]{:S(2)}, u32[]{:S(2)}) collective-permute-start(bf16[2,1296,128]{2,1,0:T(8,128)(2,1)} %get-tuple-element.103), channel_id=1, source_target_pairs={{0,1},{2,3},{4,5},{5,4},{7,6},{8,9},{10,11},{14,15},{15,14},{16,17... | collective-permute-start | bytes 1990664 | tf_op jit(solution)/shard_map/move_sums4/ppermute | solution.py:440
  171.6 20.6 %copy-start.9 = (bf16[2,1296,128]{2,1,0:T(8,128)(2,1)}, bf16[2,1296,128]{2,1,0:T(8,128)(2,1)S(1)}, u32[]{:S(2)}) copy-start(bf16[2,1296,128]{2,1,0:T(8,128)(2,1)S(1)} %collective-permute-done.19.refs_3_) | copy-start | bytes 1990660
  182.8 9.3 %copy-start.10 = (bf16[2,1296,128]{2,1,0:T(8,128)(2,1)}, bf16[2,1296,128]{2,1,0:T(8,128)(2,1)S(1)}, u32[]{:S(2)}) copy-start(bf16[2,1296,128]{2,1,0:T(8,128)(2,1)S(1)} %collective-permute-done.20.refs_4_) | copy-start | bytes 1990660
  182.8 16.3 %collective-permute-start.21 = (bf16[3,1296,128]{2,1,0:T(8,128)(2,1)}, bf16[3,1296,128]{2,1,0:T(8,128)(2,1)S(1)}, u32[]{:S(2)}, u32[]{:S(2)}) collective-permute-start(bf16[3,1296,128]{2,1,0:T(8,128)(2,1)} %get-tuple-element.112), channel_id=1, source_target_pairs={{6,7},{7,6},{8,9},{12,13},{13,12},{18,19},{19,18},{23,22},{24,25},... | collective-permute-start | bytes 2985992 | tf_op jit(solution)/shard_map/move_sums5/ppermute | solution.py:440
  (1 other events, 1.0 us)

commit v4 on v3

--- a/solution.py
+++ b/solution.py
@@ -14,12 +14,12 @@
     (("own", "a", "b", "x0", "c0", "ca", "cb", "d0", "xa"), 5),
     (("xb",), 6),
     (("t", "da", "db"), 3),
-    (("ct",), 4),
+    (("ct",), 5),
     (("e", "xt"), 2),
     (("dt",), 3),
     ((), 16),
 )
-SENDS = ((0, 3), (1, 2), (2, 2), (3, 2), (4, 2), (5, 3))
+SENDS = ((0, 3), (2, 2), (3, 2), (4, 2), (5, 3))
 
 
 def route(n):
@@ -389,7 +389,7 @@
                 in_specs=[pl.BlockSpec(memory_space=pltpu.SMEM)] + [anywhere] * 2,
                 out_specs=anywhere,
                 scratch_shapes=[pltpu.VMEM((6, h, p), jnp.bfloat16), pltpu.SemaphoreType.DMA],
-                compiler_params=pltpu.CompilerParams(vmem_limit_bytes=60 << 20),
+                compiler_params=pltpu.CompilerParams(vmem_limit_bytes=64 << 20),
                 cost_estimate=pl.CostEstimate(flops=1 << 10, bytes_accessed=1 << 10, transcendentals=0),
                 name="pick",
             )(inner, have[first], have[second])
@@ -428,7 +428,7 @@
                     pltpu.SemaphoreType.DMA((2,)),
                     pltpu.SemaphoreType.DMA((2,)),
                 ],
-                compiler_params=pltpu.CompilerParams(vmem_limit_bytes=60 << 20),
+                compiler_params=pltpu.CompilerParams(vmem_limit_bytes=64 << 20),
                 cost_estimate=pl.CostEstimate(flops=1 << 20, bytes_accessed=1 << 16, transcendentals=0),
                 name=f"blocks_{e}",
             )(have["line"], tile_map, group_gain, weight, group, *used, *(have[k] for k, _ in carried))
@@ -453,21 +453,20 @@
         blocks(1)
         fence("sums", "sent1", "got0", "t")
         move("e", "xt", "ct", "da", "db")
-        exchange(1)
         fence("da", "db")
         blocks(2)
-        fence("sums", "sent2", "ct")
+        fence("sums", "sent1", "ct")
+        exchange(1)
+        blocks(3)
+        fence("sums", "sent2", "got1", "xt", "e")
         exchange(2)
-        blocks(3)
-        fence("sums", "sent3", "got1", "got2", "xt", "e")
-        exchange(3)
         move("dt")
         blocks(4)
-        fence("dt", "sums", "sent4")
+        fence("dt", "sums", "sent3")
+        exchange(3)
+        blocks(5)
+        fence("sums", "sent4", "got2", "got3")
         exchange(4)
-        blocks(5)
-        fence("sums", "sent5", "got3", "got4")
-        exchange(5)
         blocks(6)
         got = [have[f"got{i}"] for i in range(len(SENDS))]
         return pl.pallas_call(
@@ -485,7 +484,7 @@
                 pltpu.SemaphoreType.DMA((half * n,)),
                 pltpu.SemaphoreType.DMA((half,)),
             ],
-            compiler_params=pltpu.CompilerParams(vmem_limit_bytes=60 << 20),
+            compiler_params=pltpu.CompilerParams(vmem_limit_bytes=64 << 20),
             name="add_up",
         )(have["line"], have["sums"], *got)
 

time: 208 us -> 201 us (0.966)
  local copies, waits for them, and re-layouts: 5.93 us -> 1.2 us
    ppermute x6 -> x5, starting transfers between devices: 14.6 us -> 9.75 us  [exchange(): lax.ppermute(have[f'sent{i}'], ('row', 'col', 'panel'), ids)]
    unnamed x22 -> x0, local copies, waits for them, and re-layouts: 4.69 us -> none
    ppermute x16, starting transfers between devices: 25.4 us -> 29.8 us  [move(): have[name] = lax.ppermute(have[source[name]], ('row', 'col'), ids)]
    ppermute x6 -> x5, waiting for transfers between devices: 22.6 us -> 20.9 us  [exchange(): lax.ppermute(have[f'sent{i}'], ('row', 'col', 'panel'), ids)]
  transfers between devices with their start and end apart: 22 -> 21, of which waited for: 6 -> 7; matrix products, arithmetic and copies ran while one was open for 1% -> 1% of each run, Pallas kernels for 28% -> 29%
where the time goes in v4:
time: 201 us; the launch traced here: 200 us
  waiting for transfers between devices  94.5 us (47%)
  Pallas kernels  63.9 us (32%)
  starting transfers between devices  39.6 us (20%)
    ppermute x16, waiting for transfers between devices, move(): have[name] = lax.ppermute(have[source[name]], ('row', 'col'), ids)  73.6 us
    pallas_call x7, Pallas kernels, blocks(): pl.pallas_call(functools.partial(multiply_blocks, len(carried), len(resul...  55.2 us
    ppermute x16, starting transfers between devices, move(): have[name] = lax.ppermute(have[source[name]], ('row', 'col'), ids)  29.8 us
    ppermute x5, waiting for transfers between devices, exchange(): lax.ppermute(have[f'sent{i}'], ('row', 'col', 'panel'), ids)  20.9 us
    ppermute x5, starting transfers between devices, exchange(): lax.ppermute(have[f'sent{i}'], ('row', 'col', 'panel'), ids)  9.75 us
    pallas_call x1, Pallas kernels, local(): pl.pallas_call(functools.partial(add_up, final, n, h), out_shape=jax.Shap...  6.03 us
  transfers between devices with their start and end apart: 21, of which 7 were waited for; matrix products, arithmetic and copies ran while one was open for 1% of the time, Pallas kernels for 29%

profile of v4, /device:TPU:24, one launch (start us, length us, event | category | flops | bytes accessed | tf_op | source)
XLA Modules:
  0.0 199.6 jit_solution(760765750865424271)
XLA Ops:
  0.5 1.9 collective-permute-start.1
  2.3 1.9 collective-permute-start.2
  4.2 7.8 %collective-permute-start.3 = (bf16[6,288,512]{2,1,0:T(8,128)(2,1)}, bf16[6,288,512]{2,1,0:T(8,128)(2,1)}, u32[]{:S(2)}, u32[]{:S(2)}) collective-permute-start(bf16[6,288,512]{2,1,0:T(8,128)(2,1)} %bitcast.9), channel_id=1, source_target_pairs={{4,2},{2,4},{12,10},{10,12},{20,18},{18,20},{28,26},{26,28},{6,0},... | collective-permute-start | bytes 5308424 | tf_op jit(solution)/shard_map/move_b/ppermute | solution.py:382
  13.2 46.4 %collective-permute-done.refs_0_ = bf16[6,288,512]{2,1,0:T(8,128)(2,1)} collective-permute-done((bf16[6,288,512]{2,1,0:T(8,128)(2,1)}, bf16[6,288,512]{2,1,0:T(8,128)(2,1)}, u32[]{:S(2)}, u32[]{:S(2)}) %collective-permute-start) | collective-permute-done | bytes 1769504 | tf_op jit(solution)/shard_map/move_a/ppermute | solution.py:382
  59.6 1.9 collective-permute-start.4
  61.5 1.9 collective-permute-start.5
  63.4 1.3 collective-permute-start.6
  64.7 2.7 %pick.1 = bf16[6,288,512]{2,1,0:T(8,128)(2,1)} custom-call(s32[1]{0:T(128)} %bitcast.4.second, bf16[6,288,512]{2,1,0:T(8,128)(2,1)} %bitcast.10, bf16[6,288,512]{2,1,0:T(8,128)(2,1)} %collective-permute-done.3.second_ref.refs_1_), custom_call_target="tpu_custom_call" | custom-call | flops 1024 | bytes 1024 | tf_op jit(solution)/shard_map/pick/pallas_call | solution.py:386
  67.4 1.9 collective-permute-done.6.refs_5_.refs_6_.refs_4_
  69.3 1.9 collective-permute-start.7
  71.2 1.9 collective-permute-start.9
  73.1 8.1 %blocks_0.1 = (f32[8,1296,128]{2,1,0:T(8,128)}, bf16[4,576,1536]{2,1,0:T(8,128)(2,1)}, bf16[3,1296,128]{2,1,0:T(8,128)(2,1)}) custom-call(s32[42]{0:T(128)} %dynamic-slice_bitcast_fusion.table, s32[4,4]{1,0:T(4,128)} %tile_map.13, f32[4,4]{1,0:T(4,128)} %gain_ref.13, f32[1,512]{1,0:T(1,128)} %bitcast.16, s32[1,512]{1,0:T(1,128)} %bitcast.23, ...), custom_call_target="tpu_custom_call" | custom-call | flops 1048576 | bytes 65536 | tf_op jit(solution)/shard_map/blocks_0/pallas_call | solution.py:406
  81.2 4.5 %collective-permute-start.11 = (bf16[3,1296,128]{2,1,0:T(8,128)(2,1)}, bf16[3,1296,128]{2,1,0:T(8,128)(2,1)}, u32[]{:S(2)}, u32[]{:S(2)}) collective-permute-start(bf16[3,1296,128]{2,1,0:T(8,128)(2,1)} %get-tuple-element.76), channel_id=1, source_target_pairs={{0,1},{1,0},{2,3},{3,2},{4,5},{5,4},{6,7},{9,8},{10,11},{11,10},{1... | collective-permute-start | bytes 2985992 | tf_op jit(solution)/shard_map/move_sums0/ppermute | solution.py:440
  85.7 1.3 collective-permute-start.8
  87.0 1.3 collective-permute-start.10
  89.3 24.5 %collective-permute-done.12.refs_9_.refs_10_ = bf16[6,288,512]{2,1,0:T(8,128)(2,1)} collective-permute-done((bf16[6,288,512]{2,1,0:T(8,128)(2,1)}, bf16[6,288,512]{2,1,0:T(8,128)(2,1)}, u32[]{:S(2)}, u32[]{:S(2)}) %collective-permute-start.12) | collective-permute-done | bytes 1769504 | tf_op jit(solution)/shard_map/move_t/ppermute | solution.py:382
  113.8 1.9 collective-permute-start.13
  115.7 1.9 collective-permute-start.15
  117.6 1.3 collective-permute-start.16
  118.9 9.7 %blocks_2.1 = (f32[8,1296,128]{2,1,0:T(8,128)}, bf16[4,576,1536]{2,1,0:T(8,128)(2,1)}, bf16[2,1296,128]{2,1,0:T(8,128)(2,1)}) custom-call(s32[42]{0:T(128)} %dynamic-slice_bitcast_fusion.table, s32[4,4]{1,0:T(4,128)} %tile_map.13, f32[4,4]{1,0:T(4,128)} %gain_ref.13, ...), custom_call_target="tpu_custom_call", output_to_operand_aliasing={{0}: (18, {}), {1}: (19, {}), {2}: (20, {})} | custom-call | flops 1048576 | bytes 65536 | tf_op jit(solution)/shard_map/blocks_2/pallas_call | solution.py:406
  128.6 1.7 collective-permute-start.14
  130.2 11.2 %blocks_3.1 = (f32[8,1296,128]{2,1,0:T(8,128)}, bf16[4,576,1536]{2,1,0:T(8,128)(2,1)}, bf16[2,1296,128]{2,1,0:T(8,128)(2,1)}) custom-call(s32[42]{0:T(128)} %dynamic-slice_bitcast_fusion.table, s32[4,4]{1,0:T(4,128)} %tile_map.13, f32[4,4]{1,0:T(4,128)} %gain_ref.13, f32[1,512]{1,0:T(1,128)} %bitcast.19, ...), custom_call_target="tpu_custom_call", output_to_operand_aliasing={{0}: (19, {}), {1}: (20, {})} | custom-call | flops 1048576 | bytes 65536 | tf_op jit(solution)/shard_map/blocks_3/pallas_call | solution.py:406
  142.3 2.4 %collective-permute-done.14.refs_1_ = bf16[2,1296,128]{2,1,0:T(8,128)(2,1)} collective-permute-done((bf16[2,1296,128]{2,1,0:T(8,128)(2,1)}, bf16[2,1296,128]{2,1,0:T(8,128)(2,1)}, u32[]{:S(2)}, u32[]{:S(2)}) %collective-permute-start.14) | collective-permute-done | bytes 663584 | tf_op jit(solution)/shard_map/move_sums1/ppermute | solution.py:440
  144.8 1.3 collective-permute-start.17
  146.4 7.9 %blocks_4.1 = (f32[8,1296,128]{2,1,0:T(8,128)}, bf16[4,576,1536]{2,1,0:T(8,128)(2,1)}, bf16[2,1296,128]{2,1,0:T(8,128)(2,1)}) custom-call(s32[42]{0:T(128)} %dynamic-slice_bitcast_fusion.table, s32[4,4]{1,0:T(4,128)} %tile_map.13, f32[4,4]{1,0:T(4,128)} %gain_ref.13, f32[1,512]{1,0:T(1,128)} %bitcast.20, ...), custom_call_target="tpu_custom_call", output_to_operand_aliasing={{0}: (16, {}), {1}: (17, {})} | custom-call | flops 1048576 | bytes 65536 | tf_op jit(solution)/shard_map/blocks_4/pallas_call | solution.py:406
  154.3 1.3 collective-permute-start.19
  155.6 9.7 %blocks_5.1 = (f32[8,1296,128]{2,1,0:T(8,128)}, bf16[4,576,1536]{2,1,0:T(8,128)(2,1)}, bf16[3,1296,128]{2,1,0:T(8,128)(2,1)}) custom-call(s32[42]{0:T(128)} %dynamic-slice_bitcast_fusion.table, s32[4,4]{1,0:T(4,128)} %tile_map.13, f32[4,4]{1,0:T(4,128)} %gain_ref.13, f32[1,512]{1,0:T(1,128)} %bitcast.21, ...), custom_call_target="tpu_custom_call", output_to_operand_aliasing={{0}: (14, {}), {1}: (15, {})} | custom-call | flops 1048576 | bytes 65536 | tf_op jit(solution)/shard_map/blocks_5/pallas_call | solution.py:406
  165.3 11.7 %collective-permute-done.19.refs_3_ = bf16[2,1296,128]{2,1,0:T(8,128)(2,1)} collective-permute-done((bf16[2,1296,128]{2,1,0:T(8,128)(2,1)}, bf16[2,1296,128]{2,1,0:T(8,128)(2,1)}, u32[]{:S(2)}, u32[]{:S(2)}) %collective-permute-start.19) | collective-permute-done | bytes 663584 | tf_op jit(solution)/shard_map/move_sums3/ppermute | solution.py:440
  177.0 1.9 collective-permute-start.20
  178.9 7.7 %blocks_6.1 = (f32[8,1296,128]{2,1,0:T(8,128)}, bf16[4,576,1536]{2,1,0:T(8,128)(2,1)}) custom-call(s32[42]{0:T(128)} %dynamic-slice_bitcast_fusion.table, s32[4,4]{1,0:T(4,128)} %tile_map.13, f32[4,4]{1,0:T(4,128)} %gain_ref.13, f32[1,512]{1,0:T(1,128)} %bitcast.22, s32[1,512]{1,0:T(1,128)} %bitcast.29, ...), custom_call_target="tpu_custom_call", output_to_operand_aliasing={{0}: (6, {}), {1}: (7, {})} | custom-call | flops 1048576 | bytes 65536 | tf_op jit(solution)/shard_map/blocks_6/pallas_call | solution.py:406
  186.6 6.8 %collective-permute-done.20.refs_4_ = bf16[3,1296,128]{2,1,0:T(8,128)(2,1)} collective-permute-done((bf16[3,1296,128]{2,1,0:T(8,128)(2,1)}, bf16[3,1296,128]{2,1,0:T(8,128)(2,1)}, u32[]{:S(2)}, u32[]{:S(2)}) %collective-permute-start.20) | collective-permute-done | bytes 995360 | tf_op jit(solution)/shard_map/move_sums4/ppermute | solution.py:440
  193.4 6.0 %add_up.1 = f32[576,2,1152]{2,1,0:T(2,128)} custom-call(s32[42]{0:T(128)} %dynamic-slice_bitcast_fusion.table, f32[8,1296,128]{2,1,0:T(8,128)} %get-tuple-element.105.own, bf16[3,1296,128]{2,1,0:T(8,128)(2,1)} %collective-permute-done.11.refs_0_, bf16[2,1296,128]{2,1,0:T(8,128)(2,1)} %collective-permute-done.14.refs_1_, ...), custom_call_target="tpu_custom_call" | custom-call | tf_op jit(solution)/shard_map/add_up/pallas_call | solution.py:472
  (20 shorter events, 3.9 us)
Async XLA Ops:
  0.0 59.6 %collective-permute-start = (bf16[6,288,512]{2,1,0:T(8,128)(2,1)}, bf16[6,288,512]{2,1,0:T(8,128)(2,1)}, u32[]{:S(2)}, u32[]{:S(2)}) collective-permute-start(bf16[6,288,512]{2,1,0:T(8,128)(2,1)} %bitcast.6), channel_id=1, source_target_pairs={{2,0},{0,2},{6,4},{4,6},{10,8},{8,10},{14,12},{12,14},{18,16},{16,... | collective-permute-start | bytes 5308424 | tf_op jit(solution)/shard_map/move_a/ppermute | solution.py:382
  0.5 59.2 %collective-permute-start.1 = (bf16[6,288,512]{2,1,0:T(8,128)(2,1)}, bf16[6,288,512]{2,1,0:T(8,128)(2,1)}, u32[]{:S(2)}, u32[]{:S(2)}) collective-permute-start(bf16[6,288,512]{2,1,0:T(8,128)(2,1)} %bitcast.7), channel_id=1, source_target_pairs={{0,16},{10,26},{20,4},{30,14},{1,17},{11,27},{21,5},{31,15}} | collective-permute-start | bytes 5308424 | tf_op jit(solution)/shard_map/move_x0/ppermute | solution.py:382
  2.3 57.3 %collective-permute-start.2 = (bf16[6,288,512]{2,1,0:T(8,128)(2,1)}, bf16[6,288,512]{2,1,0:T(8,128)(2,1)}, u32[]{:S(2)}, u32[]{:S(2)}) collective-permute-start(bf16[6,288,512]{2,1,0:T(8,128)(2,1)} %bitcast.8), channel_id=1, source_target_pairs={{0,8},{10,2},{20,28},{30,22},{1,9},{11,3},{21,29},{31,23}} | collective-permute-start | bytes 5308424 | tf_op jit(solution)/shard_map/move_c0/ppermute | solution.py:382
  4.2 60.5 %collective-permute-start.3 = (bf16[6,288,512]{2,1,0:T(8,128)(2,1)}, bf16[6,288,512]{2,1,0:T(8,128)(2,1)}, u32[]{:S(2)}, u32[]{:S(2)}) collective-permute-start(bf16[6,288,512]{2,1,0:T(8,128)(2,1)} %bitcast.9), channel_id=1, source_target_pairs={{4,2},{2,4},{12,10},{10,12},{20,18},{18,20},{28,26},{26,28},{6,0},... | collective-permute-start | bytes 5308424 | tf_op jit(solution)/shard_map/move_b/ppermute | solution.py:382
  59.6 7.8 %collective-permute-start.4 = (bf16[6,288,512]{2,1,0:T(8,128)(2,1)}, bf16[6,288,512]{2,1,0:T(8,128)(2,1)}, u32[]{:S(2)}, u32[]{:S(2)}) collective-permute-start(bf16[6,288,512]{2,1,0:T(8,128)(2,1)} %collective-permute-done.refs_0_), channel_id=1, source_target_pairs={{0,16},{10,26},{20,4},{30,14},{1,17},{11,27},{21,5},{31,15}} | collective-permute-start | bytes 5308424 | tf_op jit(solution)/shard_map/move_xa/ppermute | solution.py:382
  61.5 5.9 %collective-permute-start.5 = (bf16[6,288,512]{2,1,0:T(8,128)(2,1)}, bf16[6,288,512]{2,1,0:T(8,128)(2,1)}, u32[]{:S(2)}, u32[]{:S(2)}) collective-permute-start(bf16[6,288,512]{2,1,0:T(8,128)(2,1)} %collective-permute-done.refs_0_), channel_id=1, source_target_pairs={{0,8},{10,2},{20,28},{30,22},{1,9},{11,3},{21,29},{31,23}} | collective-permute-start | bytes 5308424 | tf_op jit(solution)/shard_map/move_ca/ppermute | solution.py:382
  63.4 5.9 %collective-permute-start.6 = (bf16[6,288,512]{2,1,0:T(8,128)(2,1)}, bf16[6,288,512]{2,1,0:T(8,128)(2,1)}, u32[]{:S(2)}, u32[]{:S(2)}) collective-permute-start(bf16[6,288,512]{2,1,0:T(8,128)(2,1)} %collective-permute-done.1.refs_7_.refs_6_.refs_10_.refs_11_), channel_id=1, source_target_pairs={{16,24},{26,18},{4,12},{14,6},{17,25},{27,19},{5,13},{15,7}} | collective-permute-start | bytes 5308424 | tf_op jit(solution)/shard_map/move_d0/ppermute | solution.py:382
  69.3 3.8 %collective-permute-start.7 = (bf16[6,288,512]{2,1,0:T(8,128)(2,1)}, bf16[6,288,512]{2,1,0:T(8,128)(2,1)}, u32[]{:S(2)}, u32[]{:S(2)}) collective-permute-start(bf16[6,288,512]{2,1,0:T(8,128)(2,1)} %collective-permute-done.3.second_ref.refs_1_), channel_id=1, source_target_pairs={{0,8},{10,2},{20,28},{30,22},{1,9},{11,3},{21,29},{31,23}} | collective-permute-start | bytes 5308424 | tf_op jit(solution)/shard_map/move_cb/ppermute | solution.py:382
  71.2 10.0 %collective-permute-start.9 = (bf16[6,288,512]{2,1,0:T(8,128)(2,1)}, bf16[6,288,512]{2,1,0:T(8,128)(2,1)}, u32[]{:S(2)}, u32[]{:S(2)}) collective-permute-start(bf16[6,288,512]{2,1,0:T(8,128)(2,1)} %collective-permute-done.3.second_ref.refs_1_), channel_id=1, source_target_pairs={{0,16},{10,26},{20,4},{30,14},{1,17},{11,27},{21,5},{31,15}} | collective-permute-start | bytes 5308424 | tf_op jit(solution)/shard_map/move_xb/ppermute | solution.py:382
  73.1 40.7 %collective-permute-start.12 = (bf16[6,288,512]{2,1,0:T(8,128)(2,1)}, bf16[6,288,512]{2,1,0:T(8,128)(2,1)}, u32[]{:S(2)}, u32[]{:S(2)}) collective-permute-start(bf16[6,288,512]{2,1,0:T(8,128)(2,1)} %pick.1), channel_id=1, source_target_pairs={{2,0},{6,2},{0,4},{4,6},{10,8},{14,10},{8,12},{12,14},{18,16},{22,... | collective-permute-start | bytes 5308424 | tf_op jit(solution)/shard_map/move_t/ppermute | solution.py:382
  81.2 32.6 %collective-permute-start.11 = (bf16[3,1296,128]{2,1,0:T(8,128)(2,1)}, bf16[3,1296,128]{2,1,0:T(8,128)(2,1)}, u32[]{:S(2)}, u32[]{:S(2)}) collective-permute-start(bf16[3,1296,128]{2,1,0:T(8,128)(2,1)} %get-tuple-element.76), channel_id=1, source_target_pairs={{0,1},{1,0},{2,3},{3,2},{4,5},{5,4},{6,7},{9,8},{10,11},{11,10},{1... | collective-permute-start | bytes 2985992 | tf_op jit(solution)/shard_map/move_sums0/ppermute | solution.py:440
  85.7 33.2 %collective-permute-start.8 = (bf16[6,288,512]{2,1,0:T(8,128)(2,1)}, bf16[6,288,512]{2,1,0:T(8,128)(2,1)}, u32[]{:S(2)}, u32[]{:S(2)}) collective-permute-start(bf16[6,288,512]{2,1,0:T(8,128)(2,1)} %collective-permute-done.4.refs_8_.refs_7_.refs_11_.refs_12_), channel_id=1, source_target_pairs={{16,24},{26,18},{4,12},{14,6},{17,25},{27,19},{5,13},{15,7}} | collective-permute-start | bytes 5308424 | tf_op jit(solution)/shard_map/move_da/ppermute | solution.py:382
  87.0 31.9 %collective-permute-start.10 = (bf16[6,288,512]{2,1,0:T(8,128)(2,1)}, bf16[6,288,512]{2,1,0:T(8,128)(2,1)}, u32[]{:S(2)}, u32[]{:S(2)}) collective-permute-start(bf16[6,288,512]{2,1,0:T(8,128)(2,1)} %collective-permute-done.9.refs_8_.refs_12_.refs_13_), channel_id=1, source_target_pairs={{16,24},{26,18},{4,12},{14,6},{17,25},{27,19},{5,13},{15,7}} | collective-permute-start | bytes 5308424 | tf_op jit(solution)/shard_map/move_db/ppermute | solution.py:382
  113.8 14.8 %collective-permute-start.13 = (bf16[6,288,512]{2,1,0:T(8,128)(2,1)}, bf16[6,288,512]{2,1,0:T(8,128)(2,1)}, u32[]{:S(2)}, u32[]{:S(2)}) collective-permute-start(bf16[6,288,512]{2,1,0:T(8,128)(2,1)} %collective-permute-done.12.refs_9_.refs_10_), channel_id=1, source_target_pairs={{0,8},{10,2},{20,28},{30,22},{1,9},{11,3},{21,29},{31,23}} | collective-permute-start | bytes 5308424 | tf_op jit(solution)/shard_map/move_ct/ppermute | solution.py:382
  115.7 25.8 %collective-permute-start.15 = (bf16[6,288,512]{2,1,0:T(8,128)(2,1)}, bf16[6,288,512]{2,1,0:T(8,128)(2,1)}, u32[]{:S(2)}, u32[]{:S(2)}) collective-permute-start(bf16[6,288,512]{2,1,0:T(8,128)(2,1)} %collective-permute-done.12.refs_9_.refs_10_), channel_id=1, source_target_pairs={{0,16},{10,26},{20,4},{30,14},{1,17},{11,27},{21,5},{31,15}} | collective-permute-start | bytes 5308424 | tf_op jit(solution)/shard_map/move_xt/ppermute | solution.py:382
  117.6 24.7 %collective-permute-start.16 = (bf16[6,288,512]{2,1,0:T(8,128)(2,1)}, bf16[6,288,512]{2,1,0:T(8,128)(2,1)}, u32[]{:S(2)}, u32[]{:S(2)}) collective-permute-start(bf16[6,288,512]{2,1,0:T(8,128)(2,1)} %collective-permute-done.12.refs_9_.refs_10_), channel_id=1, source_target_pairs={{4,6},{10,8},{20,22},{26,24},{5,7},{11,9},{21,23},{27,25}} | collective-permute-start | bytes 5308424 | tf_op jit(solution)/shard_map/move_e/ppermute | solution.py:382
  128.6 16.2 %collective-permute-start.14 = (bf16[2,1296,128]{2,1,0:T(8,128)(2,1)}, bf16[2,1296,128]{2,1,0:T(8,128)(2,1)}, u32[]{:S(2)}, u32[]{:S(2)}) collective-permute-start(bf16[2,1296,128]{2,1,0:T(8,128)(2,1)} %get-tuple-element.89), channel_id=1, source_target_pairs={{0,1},{1,0},{2,3},{3,2},{4,5},{5,4},{6,7},{7,6},{8,9},{9,8},{10,11... | collective-permute-start | bytes 1990664 | tf_op jit(solution)/shard_map/move_sums1/ppermute | solution.py:440
  144.8 9.5 %collective-permute-start.17 = (bf16[6,288,512]{2,1,0:T(8,128)(2,1)}, bf16[6,288,512]{2,1,0:T(8,128)(2,1)}, u32[]{:S(2)}, u32[]{:S(2)}) collective-permute-start(bf16[6,288,512]{2,1,0:T(8,128)(2,1)} %collective-permute-done.15.refs_10_.refs_8_), channel_id=1, source_target_pairs={{16,24},{26,18},{4,12},{14,6},{17,25},{27,19},{5,13},{15,7}} | collective-permute-start | bytes 5308424 | tf_op jit(solution)/shard_map/move_dt/ppermute | solution.py:382
  146.1 19.3 %collective-permute-start.18 = (bf16[2,1296,128]{2,1,0:T(8,128)(2,1)}, bf16[2,1296,128]{2,1,0:T(8,128)(2,1)}, u32[]{:S(2)}, u32[]{:S(2)}) collective-permute-start(bf16[2,1296,128]{2,1,0:T(8,128)(2,1)} %get-tuple-element.101), channel_id=1, source_target_pairs={{0,1},{1,0},{2,3},{3,2},{4,5},{5,4},{6,7},{7,6},{8,9},{9,8},{10,11... | collective-permute-start | bytes 1990664 | tf_op jit(solution)/shard_map/move_sums2/ppermute | solution.py:440
  154.3 22.7 %collective-permute-start.19 = (bf16[2,1296,128]{2,1,0:T(8,128)(2,1)}, bf16[2,1296,128]{2,1,0:T(8,128)(2,1)}, u32[]{:S(2)}, u32[]{:S(2)}) collective-permute-start(bf16[2,1296,128]{2,1,0:T(8,128)(2,1)} %get-tuple-element.102), channel_id=1, source_target_pairs={{0,1},{1,0},{2,3},{3,2},{4,5},{5,4},{7,6},{8,9},{9,8},{10,11},{11,... | collective-permute-start | bytes 1990664 | tf_op jit(solution)/shard_map/move_sums3/ppermute | solution.py:440
  177.0 16.4 %collective-permute-start.20 = (bf16[3,1296,128]{2,1,0:T(8,128)(2,1)}, bf16[3,1296,128]{2,1,0:T(8,128)(2,1)}, u32[]{:S(2)}, u32[]{:S(2)}) collective-permute-start(bf16[3,1296,128]{2,1,0:T(8,128)(2,1)} %get-tuple-element.110), channel_id=1, source_target_pairs={{6,7},{7,6},{8,9},{12,13},{13,12},{18,19},{19,18},{23,22},{24,25},... | collective-permute-start | bytes 2985992 | tf_op jit(solution)/shard_map/move_sums4/ppermute | solution.py:440

commit v5 on v4

--- a/solution.py
+++ b/solution.py
@@ -479,7 +479,7 @@
                 pltpu.VMEM((half * n, block, LANES), jnp.bfloat16),
                 pltpu.VMEM((h, n * h), jnp.float32),
                 pltpu.VMEM((h, n * h), jnp.float32),
-                pltpu.VMEM((half, 2 * h * n * h // LANES, LANES), jnp.float32),
+                pltpu.VMEM((half, 2 * h * n * h // LANES + 8, LANES), jnp.float32),
                 pltpu.SemaphoreType.DMA((half * n,)),
                 pltpu.SemaphoreType.DMA((half * n,)),
                 pltpu.SemaphoreType.DMA((half,)),

time: 201 us -> 201 us (level)
  no operation moved by 1% of the time
where the time goes in v5:
time: 201 us; the launch traced here: 200 us
  waiting for transfers between devices  94.5 us (47%)
  Pallas kernels  63.9 us (32%)
  starting transfers between devices  39.6 us (20%)
    ppermute x16, waiting for transfers between devices, move(): have[name] = lax.ppermute(have[source[name]], ('row', 'col'), ids)  73.6 us
    pallas_call x7, Pallas kernels, blocks(): pl.pallas_call(functools.partial(multiply_blocks, len(carried), len(resul...  55.2 us
    ppermute x16, starting transfers between devices, move(): have[name] = lax.ppermute(have[source[name]], ('row', 'col'), ids)  29.8 us
    ppermute x5, waiting for transfers between devices, exchange(): lax.ppermute(have[f'sent{i}'], ('row', 'col', 'panel'), ids)  20.9 us
    ppermute x5, starting transfers between devices, exchange(): lax.ppermute(have[f'sent{i}'], ('row', 'col', 'panel'), ids)  9.75 us
    pallas_call x1, Pallas kernels, local(): pl.pallas_call(functools.partial(add_up, final, n, h), out_shape=jax.Shap...  6.03 us
  transfers between devices with their start and end apart: 21, of which 7 were waited for; matrix products, arithmetic and copies ran while one was open for 1% of the time, Pallas kernels for 29%

profile of v5, /device:TPU:24, one launch (start us, length us, event | category | flops | bytes accessed | tf_op | source)
XLA Modules:
  0.0 199.6 jit_solution(3635572884401113491)
XLA Ops:
  0.5 1.9 collective-permute-start.1
  2.3 1.9 collective-permute-start.2
  4.2 7.8 %collective-permute-start.3 = (bf16[6,288,512]{2,1,0:T(8,128)(2,1)}, bf16[6,288,512]{2,1,0:T(8,128)(2,1)}, u32[]{:S(2)}, u32[]{:S(2)}) collective-permute-start(bf16[6,288,512]{2,1,0:T(8,128)(2,1)} %bitcast.9), channel_id=1, source_target_pairs={{4,2},{2,4},{12,10},{10,12},{20,18},{18,20},{28,26},{26,28},{6,0},... | collective-permute-start | bytes 5308424 | tf_op jit(solution)/shard_map/move_b/ppermute | solution.py:382
  13.2 46.4 %collective-permute-done.refs_0_ = bf16[6,288,512]{2,1,0:T(8,128)(2,1)} collective-permute-done((bf16[6,288,512]{2,1,0:T(8,128)(2,1)}, bf16[6,288,512]{2,1,0:T(8,128)(2,1)}, u32[]{:S(2)}, u32[]{:S(2)}) %collective-permute-start) | collective-permute-done | bytes 1769504 | tf_op jit(solution)/shard_map/move_a/ppermute | solution.py:382
  59.6 1.9 collective-permute-start.4
  61.5 1.9 collective-permute-start.5
  63.4 1.3 collective-permute-start.6
  64.7 2.7 %pick.1 = bf16[6,288,512]{2,1,0:T(8,128)(2,1)} custom-call(s32[1]{0:T(128)} %bitcast.4.second, bf16[6,288,512]{2,1,0:T(8,128)(2,1)} %bitcast.10, bf16[6,288,512]{2,1,0:T(8,128)(2,1)} %collective-permute-done.3.second_ref.refs_1_), custom_call_target="tpu_custom_call" | custom-call | flops 1024 | bytes 1024 | tf_op jit(solution)/shard_map/pick/pallas_call | solution.py:386
  67.4 1.9 collective-permute-done.6.refs_5_.refs_6_.refs_4_
  69.3 1.9 collective-permute-start.7
  71.2 1.9 collective-permute-start.9
  73.1 8.1 %blocks_0.1 = (f32[8,1296,128]{2,1,0:T(8,128)}, bf16[4,576,1536]{2,1,0:T(8,128)(2,1)}, bf16[3,1296,128]{2,1,0:T(8,128)(2,1)}) custom-call(s32[42]{0:T(128)} %dynamic-slice_bitcast_fusion.table, s32[4,4]{1,0:T(4,128)} %tile_map.13, f32[4,4]{1,0:T(4,128)} %gain_ref.13, f32[1,512]{1,0:T(1,128)} %bitcast.16, s32[1,512]{1,0:T(1,128)} %bitcast.23, ...), custom_call_target="tpu_custom_call" | custom-call | flops 1048576 | bytes 65536 | tf_op jit(solution)/shard_map/blocks_0/pallas_call | solution.py:406
  81.2 4.5 %collective-permute-start.11 = (bf16[3,1296,128]{2,1,0:T(8,128)(2,1)}, bf16[3,1296,128]{2,1,0:T(8,128)(2,1)}, u32[]{:S(2)}, u32[]{:S(2)}) collective-permute-start(bf16[3,1296,128]{2,1,0:T(8,128)(2,1)} %get-tuple-element.76), channel_id=1, source_target_pairs={{0,1},{1,0},{2,3},{3,2},{4,5},{5,4},{6,7},{9,8},{10,11},{11,10},{1... | collective-permute-start | bytes 2985992 | tf_op jit(solution)/shard_map/move_sums0/ppermute | solution.py:440
  85.7 1.3 collective-permute-start.8
  87.0 1.3 collective-permute-start.10
  89.3 24.5 %collective-permute-done.12.refs_9_.refs_10_ = bf16[6,288,512]{2,1,0:T(8,128)(2,1)} collective-permute-done((bf16[6,288,512]{2,1,0:T(8,128)(2,1)}, bf16[6,288,512]{2,1,0:T(8,128)(2,1)}, u32[]{:S(2)}, u32[]{:S(2)}) %collective-permute-start.12) | collective-permute-done | bytes 1769504 | tf_op jit(solution)/shard_map/move_t/ppermute | solution.py:382
  113.8 1.9 collective-permute-start.13
  115.7 1.9 collective-permute-start.15
  117.6 1.3 collective-permute-start.16
  118.9 9.7 %blocks_2.1 = (f32[8,1296,128]{2,1,0:T(8,128)}, bf16[4,576,1536]{2,1,0:T(8,128)(2,1)}, bf16[2,1296,128]{2,1,0:T(8,128)(2,1)}) custom-call(s32[42]{0:T(128)} %dynamic-slice_bitcast_fusion.table, s32[4,4]{1,0:T(4,128)} %tile_map.13, f32[4,4]{1,0:T(4,128)} %gain_ref.13, ...), custom_call_target="tpu_custom_call", output_to_operand_aliasing={{0}: (18, {}), {1}: (19, {}), {2}: (20, {})} | custom-call | flops 1048576 | bytes 65536 | tf_op jit(solution)/shard_map/blocks_2/pallas_call | solution.py:406
  128.6 1.7 collective-permute-start.14
  130.2 11.2 %blocks_3.1 = (f32[8,1296,128]{2,1,0:T(8,128)}, bf16[4,576,1536]{2,1,0:T(8,128)(2,1)}, bf16[2,1296,128]{2,1,0:T(8,128)(2,1)}) custom-call(s32[42]{0:T(128)} %dynamic-slice_bitcast_fusion.table, s32[4,4]{1,0:T(4,128)} %tile_map.13, f32[4,4]{1,0:T(4,128)} %gain_ref.13, f32[1,512]{1,0:T(1,128)} %bitcast.19, ...), custom_call_target="tpu_custom_call", output_to_operand_aliasing={{0}: (19, {}), {1}: (20, {})} | custom-call | flops 1048576 | bytes 65536 | tf_op jit(solution)/shard_map/blocks_3/pallas_call | solution.py:406
  142.3 2.4 %collective-permute-done.14.refs_1_ = bf16[2,1296,128]{2,1,0:T(8,128)(2,1)} collective-permute-done((bf16[2,1296,128]{2,1,0:T(8,128)(2,1)}, bf16[2,1296,128]{2,1,0:T(8,128)(2,1)}, u32[]{:S(2)}, u32[]{:S(2)}) %collective-permute-start.14) | collective-permute-done | bytes 663584 | tf_op jit(solution)/shard_map/move_sums1/ppermute | solution.py:440
  144.8 1.3 collective-permute-start.17
  146.4 7.9 %blocks_4.1 = (f32[8,1296,128]{2,1,0:T(8,128)}, bf16[4,576,1536]{2,1,0:T(8,128)(2,1)}, bf16[2,1296,128]{2,1,0:T(8,128)(2,1)}) custom-call(s32[42]{0:T(128)} %dynamic-slice_bitcast_fusion.table, s32[4,4]{1,0:T(4,128)} %tile_map.13, f32[4,4]{1,0:T(4,128)} %gain_ref.13, f32[1,512]{1,0:T(1,128)} %bitcast.20, ...), custom_call_target="tpu_custom_call", output_to_operand_aliasing={{0}: (16, {}), {1}: (17, {})} | custom-call | flops 1048576 | bytes 65536 | tf_op jit(solution)/shard_map/blocks_4/pallas_call | solution.py:406
  154.3 1.3 collective-permute-start.19
  155.6 9.7 %blocks_5.1 = (f32[8,1296,128]{2,1,0:T(8,128)}, bf16[4,576,1536]{2,1,0:T(8,128)(2,1)}, bf16[3,1296,128]{2,1,0:T(8,128)(2,1)}) custom-call(s32[42]{0:T(128)} %dynamic-slice_bitcast_fusion.table, s32[4,4]{1,0:T(4,128)} %tile_map.13, f32[4,4]{1,0:T(4,128)} %gain_ref.13, f32[1,512]{1,0:T(1,128)} %bitcast.21, ...), custom_call_target="tpu_custom_call", output_to_operand_aliasing={{0}: (14, {}), {1}: (15, {})} | custom-call | flops 1048576 | bytes 65536 | tf_op jit(solution)/shard_map/blocks_5/pallas_call | solution.py:406
  165.3 11.7 %collective-permute-done.19.refs_3_ = bf16[2,1296,128]{2,1,0:T(8,128)(2,1)} collective-permute-done((bf16[2,1296,128]{2,1,0:T(8,128)(2,1)}, bf16[2,1296,128]{2,1,0:T(8,128)(2,1)}, u32[]{:S(2)}, u32[]{:S(2)}) %collective-permute-start.19) | collective-permute-done | bytes 663584 | tf_op jit(solution)/shard_map/move_sums3/ppermute | solution.py:440
  177.0 1.9 collective-permute-start.20
  178.9 7.7 %blocks_6.1 = (f32[8,1296,128]{2,1,0:T(8,128)}, bf16[4,576,1536]{2,1,0:T(8,128)(2,1)}) custom-call(s32[42]{0:T(128)} %dynamic-slice_bitcast_fusion.table, s32[4,4]{1,0:T(4,128)} %tile_map.13, f32[4,4]{1,0:T(4,128)} %gain_ref.13, f32[1,512]{1,0:T(1,128)} %bitcast.22, s32[1,512]{1,0:T(1,128)} %bitcast.29, ...), custom_call_target="tpu_custom_call", output_to_operand_aliasing={{0}: (6, {}), {1}: (7, {})} | custom-call | flops 1048576 | bytes 65536 | tf_op jit(solution)/shard_map/blocks_6/pallas_call | solution.py:406
  186.6 6.8 %collective-permute-done.20.refs_4_ = bf16[3,1296,128]{2,1,0:T(8,128)(2,1)} collective-permute-done((bf16[3,1296,128]{2,1,0:T(8,128)(2,1)}, bf16[3,1296,128]{2,1,0:T(8,128)(2,1)}, u32[]{:S(2)}, u32[]{:S(2)}) %collective-permute-start.20) | collective-permute-done | bytes 995360 | tf_op jit(solution)/shard_map/move_sums4/ppermute | solution.py:440
  193.4 6.0 %add_up.1 = f32[576,2,1152]{2,1,0:T(2,128)} custom-call(s32[42]{0:T(128)} %dynamic-slice_bitcast_fusion.table, f32[8,1296,128]{2,1,0:T(8,128)} %get-tuple-element.105.own, bf16[3,1296,128]{2,1,0:T(8,128)(2,1)} %collective-permute-done.11.refs_0_, bf16[2,1296,128]{2,1,0:T(8,128)(2,1)} %collective-permute-done.14.refs_1_, ...), custom_call_target="tpu_custom_call" | custom-call | tf_op jit(solution)/shard_map/add_up/pallas_call | solution.py:472
  (20 shorter events, 3.9 us)
Async XLA Ops:
  0.0 59.6 %collective-permute-start = (bf16[6,288,512]{2,1,0:T(8,128)(2,1)}, bf16[6,288,512]{2,1,0:T(8,128)(2,1)}, u32[]{:S(2)}, u32[]{:S(2)}) collective-permute-start(bf16[6,288,512]{2,1,0:T(8,128)(2,1)} %bitcast.6), channel_id=1, source_target_pairs={{2,0},{0,2},{6,4},{4,6},{10,8},{8,10},{14,12},{12,14},{18,16},{16,... | collective-permute-start | bytes 5308424 | tf_op jit(solution)/shard_map/move_a/ppermute | solution.py:382
  0.5 59.2 %collective-permute-start.1 = (bf16[6,288,512]{2,1,0:T(8,128)(2,1)}, bf16[6,288,512]{2,1,0:T(8,128)(2,1)}, u32[]{:S(2)}, u32[]{:S(2)}) collective-permute-start(bf16[6,288,512]{2,1,0:T(8,128)(2,1)} %bitcast.7), channel_id=1, source_target_pairs={{0,16},{10,26},{20,4},{30,14},{1,17},{11,27},{21,5},{31,15}} | collective-permute-start | bytes 5308424 | tf_op jit(solution)/shard_map/move_x0/ppermute | solution.py:382
  2.3 57.3 %collective-permute-start.2 = (bf16[6,288,512]{2,1,0:T(8,128)(2,1)}, bf16[6,288,512]{2,1,0:T(8,128)(2,1)}, u32[]{:S(2)}, u32[]{:S(2)}) collective-permute-start(bf16[6,288,512]{2,1,0:T(8,128)(2,1)} %bitcast.8), channel_id=1, source_target_pairs={{0,8},{10,2},{20,28},{30,22},{1,9},{11,3},{21,29},{31,23}} | collective-permute-start | bytes 5308424 | tf_op jit(solution)/shard_map/move_c0/ppermute | solution.py:382
  4.2 60.5 %collective-permute-start.3 = (bf16[6,288,512]{2,1,0:T(8,128)(2,1)}, bf16[6,288,512]{2,1,0:T(8,128)(2,1)}, u32[]{:S(2)}, u32[]{:S(2)}) collective-permute-start(bf16[6,288,512]{2,1,0:T(8,128)(2,1)} %bitcast.9), channel_id=1, source_target_pairs={{4,2},{2,4},{12,10},{10,12},{20,18},{18,20},{28,26},{26,28},{6,0},... | collective-permute-start | bytes 5308424 | tf_op jit(solution)/shard_map/move_b/ppermute | solution.py:382
  59.6 7.8 %collective-permute-start.4 = (bf16[6,288,512]{2,1,0:T(8,128)(2,1)}, bf16[6,288,512]{2,1,0:T(8,128)(2,1)}, u32[]{:S(2)}, u32[]{:S(2)}) collective-permute-start(bf16[6,288,512]{2,1,0:T(8,128)(2,1)} %collective-permute-done.refs_0_), channel_id=1, source_target_pairs={{0,16},{10,26},{20,4},{30,14},{1,17},{11,27},{21,5},{31,15}} | collective-permute-start | bytes 5308424 | tf_op jit(solution)/shard_map/move_xa/ppermute | solution.py:382
  61.5 5.9 %collective-permute-start.5 = (bf16[6,288,512]{2,1,0:T(8,128)(2,1)}, bf16[6,288,512]{2,1,0:T(8,128)(2,1)}, u32[]{:S(2)}, u32[]{:S(2)}) collective-permute-start(bf16[6,288,512]{2,1,0:T(8,128)(2,1)} %collective-permute-done.refs_0_), channel_id=1, source_target_pairs={{0,8},{10,2},{20,28},{30,22},{1,9},{11,3},{21,29},{31,23}} | collective-permute-start | bytes 5308424 | tf_op jit(solution)/shard_map/move_ca/ppermute | solution.py:382
  63.4 5.9 %collective-permute-start.6 = (bf16[6,288,512]{2,1,0:T(8,128)(2,1)}, bf16[6,288,512]{2,1,0:T(8,128)(2,1)}, u32[]{:S(2)}, u32[]{:S(2)}) collective-permute-start(bf16[6,288,512]{2,1,0:T(8,128)(2,1)} %collective-permute-done.1.refs_7_.refs_6_.refs_10_.refs_11_), channel_id=1, source_target_pairs={{16,24},{26,18},{4,12},{14,6},{17,25},{27,19},{5,13},{15,7}} | collective-permute-start | bytes 5308424 | tf_op jit(solution)/shard_map/move_d0/ppermute | solution.py:382
  69.3 3.8 %collective-permute-start.7 = (bf16[6,288,512]{2,1,0:T(8,128)(2,1)}, bf16[6,288,512]{2,1,0:T(8,128)(2,1)}, u32[]{:S(2)}, u32[]{:S(2)}) collective-permute-start(bf16[6,288,512]{2,1,0:T(8,128)(2,1)} %collective-permute-done.3.second_ref.refs_1_), channel_id=1, source_target_pairs={{0,8},{10,2},{20,28},{30,22},{1,9},{11,3},{21,29},{31,23}} | collective-permute-start | bytes 5308424 | tf_op jit(solution)/shard_map/move_cb/ppermute | solution.py:382
  71.2 10.0 %collective-permute-start.9 = (bf16[6,288,512]{2,1,0:T(8,128)(2,1)}, bf16[6,288,512]{2,1,0:T(8,128)(2,1)}, u32[]{:S(2)}, u32[]{:S(2)}) collective-permute-start(bf16[6,288,512]{2,1,0:T(8,128)(2,1)} %collective-permute-done.3.second_ref.refs_1_), channel_id=1, source_target_pairs={{0,16},{10,26},{20,4},{30,14},{1,17},{11,27},{21,5},{31,15}} | collective-permute-start | bytes 5308424 | tf_op jit(solution)/shard_map/move_xb/ppermute | solution.py:382
  73.1 40.7 %collective-permute-start.12 = (bf16[6,288,512]{2,1,0:T(8,128)(2,1)}, bf16[6,288,512]{2,1,0:T(8,128)(2,1)}, u32[]{:S(2)}, u32[]{:S(2)}) collective-permute-start(bf16[6,288,512]{2,1,0:T(8,128)(2,1)} %pick.1), channel_id=1, source_target_pairs={{2,0},{6,2},{0,4},{4,6},{10,8},{14,10},{8,12},{12,14},{18,16},{22,... | collective-permute-start | bytes 5308424 | tf_op jit(solution)/shard_map/move_t/ppermute | solution.py:382
  81.2 32.6 %collective-permute-start.11 = (bf16[3,1296,128]{2,1,0:T(8,128)(2,1)}, bf16[3,1296,128]{2,1,0:T(8,128)(2,1)}, u32[]{:S(2)}, u32[]{:S(2)}) collective-permute-start(bf16[3,1296,128]{2,1,0:T(8,128)(2,1)} %get-tuple-element.76), channel_id=1, source_target_pairs={{0,1},{1,0},{2,3},{3,2},{4,5},{5,4},{6,7},{9,8},{10,11},{11,10},{1... | collective-permute-start | bytes 2985992 | tf_op jit(solution)/shard_map/move_sums0/ppermute | solution.py:440
  85.7 33.2 %collective-permute-start.8 = (bf16[6,288,512]{2,1,0:T(8,128)(2,1)}, bf16[6,288,512]{2,1,0:T(8,128)(2,1)}, u32[]{:S(2)}, u32[]{:S(2)}) collective-permute-start(bf16[6,288,512]{2,1,0:T(8,128)(2,1)} %collective-permute-done.4.refs_8_.refs_7_.refs_11_.refs_12_), channel_id=1, source_target_pairs={{16,24},{26,18},{4,12},{14,6},{17,25},{27,19},{5,13},{15,7}} | collective-permute-start | bytes 5308424 | tf_op jit(solution)/shard_map/move_da/ppermute | solution.py:382
  87.0 31.9 %collective-permute-start.10 = (bf16[6,288,512]{2,1,0:T(8,128)(2,1)}, bf16[6,288,512]{2,1,0:T(8,128)(2,1)}, u32[]{:S(2)}, u32[]{:S(2)}) collective-permute-start(bf16[6,288,512]{2,1,0:T(8,128)(2,1)} %collective-permute-done.9.refs_8_.refs_12_.refs_13_), channel_id=1, source_target_pairs={{16,24},{26,18},{4,12},{14,6},{17,25},{27,19},{5,13},{15,7}} | collective-permute-start | bytes 5308424 | tf_op jit(solution)/shard_map/move_db/ppermute | solution.py:382
  113.8 14.8 %collective-permute-start.13 = (bf16[6,288,512]{2,1,0:T(8,128)(2,1)}, bf16[6,288,512]{2,1,0:T(8,128)(2,1)}, u32[]{:S(2)}, u32[]{:S(2)}) collective-permute-start(bf16[6,288,512]{2,1,0:T(8,128)(2,1)} %collective-permute-done.12.refs_9_.refs_10_), channel_id=1, source_target_pairs={{0,8},{10,2},{20,28},{30,22},{1,9},{11,3},{21,29},{31,23}} | collective-permute-start | bytes 5308424 | tf_op jit(solution)/shard_map/move_ct/ppermute | solution.py:382
  115.7 25.8 %collective-permute-start.15 = (bf16[6,288,512]{2,1,0:T(8,128)(2,1)}, bf16[6,288,512]{2,1,0:T(8,128)(2,1)}, u32[]{:S(2)}, u32[]{:S(2)}) collective-permute-start(bf16[6,288,512]{2,1,0:T(8,128)(2,1)} %collective-permute-done.12.refs_9_.refs_10_), channel_id=1, source_target_pairs={{0,16},{10,26},{20,4},{30,14},{1,17},{11,27},{21,5},{31,15}} | collective-permute-start | bytes 5308424 | tf_op jit(solution)/shard_map/move_xt/ppermute | solution.py:382
  117.6 24.7 %collective-permute-start.16 = (bf16[6,288,512]{2,1,0:T(8,128)(2,1)}, bf16[6,288,512]{2,1,0:T(8,128)(2,1)}, u32[]{:S(2)}, u32[]{:S(2)}) collective-permute-start(bf16[6,288,512]{2,1,0:T(8,128)(2,1)} %collective-permute-done.12.refs_9_.refs_10_), channel_id=1, source_target_pairs={{4,6},{10,8},{20,22},{26,24},{5,7},{11,9},{21,23},{27,25}} | collective-permute-start | bytes 5308424 | tf_op jit(solution)/shard_map/move_e/ppermute | solution.py:382
  128.6 16.2 %collective-permute-start.14 = (bf16[2,1296,128]{2,1,0:T(8,128)(2,1)}, bf16[2,1296,128]{2,1,0:T(8,128)(2,1)}, u32[]{:S(2)}, u32[]{:S(2)}) collective-permute-start(bf16[2,1296,128]{2,1,0:T(8,128)(2,1)} %get-tuple-element.89), channel_id=1, source_target_pairs={{0,1},{1,0},{2,3},{3,2},{4,5},{5,4},{6,7},{7,6},{8,9},{9,8},{10,11... | collective-permute-start | bytes 1990664 | tf_op jit(solution)/shard_map/move_sums1/ppermute | solution.py:440
  144.8 9.5 %collective-permute-start.17 = (bf16[6,288,512]{2,1,0:T(8,128)(2,1)}, bf16[6,288,512]{2,1,0:T(8,128)(2,1)}, u32[]{:S(2)}, u32[]{:S(2)}) collective-permute-start(bf16[6,288,512]{2,1,0:T(8,128)(2,1)} %collective-permute-done.15.refs_10_.refs_8_), channel_id=1, source_target_pairs={{16,24},{26,18},{4,12},{14,6},{17,25},{27,19},{5,13},{15,7}} | collective-permute-start | bytes 5308424 | tf_op jit(solution)/shard_map/move_dt/ppermute | solution.py:382
  146.1 19.3 %collective-permute-start.18 = (bf16[2,1296,128]{2,1,0:T(8,128)(2,1)}, bf16[2,1296,128]{2,1,0:T(8,128)(2,1)}, u32[]{:S(2)}, u32[]{:S(2)}) collective-permute-start(bf16[2,1296,128]{2,1,0:T(8,128)(2,1)} %get-tuple-element.101), channel_id=1, source_target_pairs={{0,1},{1,0},{2,3},{3,2},{4,5},{5,4},{6,7},{7,6},{8,9},{9,8},{10,11... | collective-permute-start | bytes 1990664 | tf_op jit(solution)/shard_map/move_sums2/ppermute | solution.py:440
  154.3 22.7 %collective-permute-start.19 = (bf16[2,1296,128]{2,1,0:T(8,128)(2,1)}, bf16[2,1296,128]{2,1,0:T(8,128)(2,1)}, u32[]{:S(2)}, u32[]{:S(2)}) collective-permute-start(bf16[2,1296,128]{2,1,0:T(8,128)(2,1)} %get-tuple-element.102), channel_id=1, source_target_pairs={{0,1},{1,0},{2,3},{3,2},{4,5},{5,4},{7,6},{8,9},{9,8},{10,11},{11,... | collective-permute-start | bytes 1990664 | tf_op jit(solution)/shard_map/move_sums3/ppermute | solution.py:440
  177.0 16.4 %collective-permute-start.20 = (bf16[3,1296,128]{2,1,0:T(8,128)(2,1)}, bf16[3,1296,128]{2,1,0:T(8,128)(2,1)}, u32[]{:S(2)}, u32[]{:S(2)}) collective-permute-start(bf16[3,1296,128]{2,1,0:T(8,128)(2,1)} %get-tuple-element.110), channel_id=1, source_target_pairs={{6,7},{7,6},{8,9},{12,13},{13,12},{18,19},{19,18},{23,22},{24,25},... | collective-permute-start | bytes 2985992 | tf_op jit(solution)/shard_map/move_sums4/ppermute | solution.py:440

commit v6 on v5

--- a/solution.py
+++ b/solution.py
@@ -124,12 +124,12 @@
         def _():
             for c in range(6):
                 pltpu.make_async_copy(
-                    source.at[c], target.at[pl.ds((c // 3) * gap, h), pl.ds((c % 3) * p, p)], sem
+                    source.at[c], target.at[pl.ds((c // 3) * gap, h), pl.ds((c % 3) * p, p)], sem(c % 3)
                 ).start()
 
 
-def landed(sources, target, sem, h, p, gap):
-    for c in range(6):
+def landed(sources, target, sem, h, p, gap, parts=range(6)):
+    for c in parts:
         pltpu.make_async_copy(
             sources[0].at[c], target.at[pl.ds((c // 3) * gap, h), pl.ds((c % 3) * p, p)], sem
         ).wait()
@@ -202,14 +202,14 @@
 
     def ask_row(t, slot):
         row, plane = entry(t)[0], entry(t)[4]
-        fetch(row, srcs, raw, raw_sem, h, p, h)
+        fetch(row, srcs, raw, lambda part: raw_sem.at[part], h, p, h)
 
         @pl.when(row >= KNOWN)
         def _():
             known(slot, plane).start()
 
     def ask_column(t):
-        fetch(entry(t)[1], srcs, right.at[lax.rem(t, 2)], r_sem.at[lax.rem(t, 2)], h, p, gap)
+        fetch(entry(t)[1], srcs, right.at[lax.rem(t, 2)], lambda _: r_sem.at[lax.rem(t, 2)], h, p, gap)
 
     @pl.when(count > 0)
     def _():
@@ -230,8 +230,8 @@
 
         @pl.when(fresh)
         def _():
-            landed(srcs, raw, raw_sem, h, p, h)
             for c in range(3):
+                landed(srcs, raw, raw_sem.at[c], h, p, h, (c, c + 3))
                 part = raw[:, c * p:(c + 1) * p].astype(jnp.float32)
                 left[side, :, c * p:(c + 1) * p] = (part * scale).astype(jnp.bfloat16)
             kept(side, plane).start()
@@ -421,7 +421,7 @@
                     pltpu.VMEM((2, gap + h, 3 * p), jnp.bfloat16),
                     pltpu.VMEM((2, block, LANES), jnp.float32),
                     pltpu.VMEM((2, block, LANES), jnp.bfloat16),
-                    pltpu.SemaphoreType.DMA,
+                    pltpu.SemaphoreType.DMA((3,)),
                     pltpu.SemaphoreType.DMA((2,)),
                     pltpu.SemaphoreType.DMA,
                     pltpu.SemaphoreType.DMA((2,)),

time: 201 us -> 201 us (level)
  no operation moved by 1% of the time
where the time goes in v6:
time: 201 us; the launch traced here: 200 us
  waiting for transfers between devices  94.9 us (47%)
  Pallas kernels  63.6 us (32%)
  starting transfers between devices  39.6 us (20%)
    ppermute x16, waiting for transfers between devices, move(): have[name] = lax.ppermute(have[source[name]], ('row', 'col'), ids)  73.9 us
    pallas_call x7, Pallas kernels, blocks(): pl.pallas_call(functools.partial(multiply_blocks, len(carried), len(resul...  54.8 us
    ppermute x16, starting transfers between devices, move(): have[name] = lax.ppermute(have[source[name]], ('row', 'col'), ids)  29.8 us
    ppermute x5, waiting for transfers between devices, exchange(): lax.ppermute(have[f'sent{i}'], ('row', 'col', 'panel'), ids)  21.1 us
    ppermute x5, starting transfers between devices, exchange(): lax.ppermute(have[f'sent{i}'], ('row', 'col', 'panel'), ids)  9.78 us
    pallas_call x1, Pallas kernels, local(): pl.pallas_call(functools.partial(add_up, final, n, h), out_shape=jax.Shap...  6.03 us
  transfers between devices with their start and end apart: 21, of which 7 were waited for; matrix products, arithmetic and copies ran while one was open for 1% of the time, Pallas kernels for 29%

profile of v6, /device:TPU:24, one launch (start us, length us, event | category | flops | bytes accessed | tf_op | source)
XLA Modules:
  0.0 199.7 jit_solution(7579641153351220977)
XLA Ops:
  0.5 1.9 collective-permute-start.1
  2.3 1.9 collective-permute-start.2
  4.2 7.8 %collective-permute-start.3 = (bf16[6,288,512]{2,1,0:T(8,128)(2,1)}, bf16[6,288,512]{2,1,0:T(8,128)(2,1)}, u32[]{:S(2)}, u32[]{:S(2)}) collective-permute-start(bf16[6,288,512]{2,1,0:T(8,128)(2,1)} %bitcast.9), channel_id=1, source_target_pairs={{4,2},{2,4},{12,10},{10,12},{20,18},{18,20},{28,26},{26,28},{6,0},... | collective-permute-start | bytes 5308424 | tf_op jit(solution)/shard_map/move_b/ppermute | solution.py:382
  13.2 46.4 %collective-permute-done.refs_0_ = bf16[6,288,512]{2,1,0:T(8,128)(2,1)} collective-permute-done((bf16[6,288,512]{2,1,0:T(8,128)(2,1)}, bf16[6,288,512]{2,1,0:T(8,128)(2,1)}, u32[]{:S(2)}, u32[]{:S(2)}) %collective-permute-start) | collective-permute-done | bytes 1769504 | tf_op jit(solution)/shard_map/move_a/ppermute | solution.py:382
  59.6 1.9 collective-permute-start.4
  61.5 1.9 collective-permute-start.5
  63.4 1.3 collective-permute-start.6
  64.7 2.7 %pick.1 = bf16[6,288,512]{2,1,0:T(8,128)(2,1)} custom-call(s32[1]{0:T(128)} %bitcast.4.second, bf16[6,288,512]{2,1,0:T(8,128)(2,1)} %bitcast.10, bf16[6,288,512]{2,1,0:T(8,128)(2,1)} %collective-permute-done.3.second_ref.refs_1_), custom_call_target="tpu_custom_call" | custom-call | flops 1024 | bytes 1024 | tf_op jit(solution)/shard_map/pick/pallas_call | solution.py:386
  67.4 1.9 collective-permute-done.6.refs_5_.refs_6_.refs_4_
  69.3 1.9 collective-permute-start.7
  71.2 1.9 collective-permute-start.9
  73.1 7.9 %blocks_0.1 = (f32[8,1296,128]{2,1,0:T(8,128)}, bf16[4,576,1536]{2,1,0:T(8,128)(2,1)}, bf16[3,1296,128]{2,1,0:T(8,128)(2,1)}) custom-call(s32[42]{0:T(128)} %dynamic-slice_bitcast_fusion.table, s32[4,4]{1,0:T(4,128)} %tile_map.13, f32[4,4]{1,0:T(4,128)} %gain_ref.13, f32[1,512]{1,0:T(1,128)} %bitcast.16, s32[1,512]{1,0:T(1,128)} %bitcast.23, ...), custom_call_target="tpu_custom_call" | custom-call | flops 1048576 | bytes 65536 | tf_op jit(solution)/shard_map/blocks_0/pallas_call | solution.py:406
  81.0 4.6 %collective-permute-start.11 = (bf16[3,1296,128]{2,1,0:T(8,128)(2,1)}, bf16[3,1296,128]{2,1,0:T(8,128)(2,1)}, u32[]{:S(2)}, u32[]{:S(2)}) collective-permute-start(bf16[3,1296,128]{2,1,0:T(8,128)(2,1)} %get-tuple-element.76), channel_id=1, source_target_pairs={{0,1},{1,0},{2,3},{3,2},{4,5},{5,4},{6,7},{9,8},{10,11},{11,10},{1... | collective-permute-start | bytes 2985992 | tf_op jit(solution)/shard_map/move_sums0/ppermute | solution.py:440
  85.6 1.3 collective-permute-start.8
  86.9 1.3 collective-permute-start.10
  89.2 24.6 %collective-permute-done.12.refs_9_.refs_10_ = bf16[6,288,512]{2,1,0:T(8,128)(2,1)} collective-permute-done((bf16[6,288,512]{2,1,0:T(8,128)(2,1)}, bf16[6,288,512]{2,1,0:T(8,128)(2,1)}, u32[]{:S(2)}, u32[]{:S(2)}) %collective-permute-start.12) | collective-permute-done | bytes 1769504 | tf_op jit(solution)/shard_map/move_t/ppermute | solution.py:382
  113.8 1.9 collective-permute-start.13
  115.7 1.9 collective-permute-start.15
  117.6 1.3 collective-permute-start.16
  118.9 9.5 %blocks_2.1 = (f32[8,1296,128]{2,1,0:T(8,128)}, bf16[4,576,1536]{2,1,0:T(8,128)(2,1)}, bf16[2,1296,128]{2,1,0:T(8,128)(2,1)}) custom-call(s32[42]{0:T(128)} %dynamic-slice_bitcast_fusion.table, s32[4,4]{1,0:T(4,128)} %tile_map.13, f32[4,4]{1,0:T(4,128)} %gain_ref.13, ...), custom_call_target="tpu_custom_call", output_to_operand_aliasing={{0}: (18, {}), {1}: (19, {}), {2}: (20, {})} | custom-call | flops 1048576 | bytes 65536 | tf_op jit(solution)/shard_map/blocks_2/pallas_call | solution.py:406
  128.4 1.7 collective-permute-start.14
  130.1 11.2 %blocks_3.1 = (f32[8,1296,128]{2,1,0:T(8,128)}, bf16[4,576,1536]{2,1,0:T(8,128)(2,1)}, bf16[2,1296,128]{2,1,0:T(8,128)(2,1)}) custom-call(s32[42]{0:T(128)} %dynamic-slice_bitcast_fusion.table, s32[4,4]{1,0:T(4,128)} %tile_map.13, f32[4,4]{1,0:T(4,128)} %gain_ref.13, f32[1,512]{1,0:T(1,128)} %bitcast.19, ...), custom_call_target="tpu_custom_call", output_to_operand_aliasing={{0}: (19, {}), {1}: (20, {})} | custom-call | flops 1048576 | bytes 65536 | tf_op jit(solution)/shard_map/blocks_3/pallas_call | solution.py:406
  142.3 2.5 %collective-permute-done.14.refs_1_ = bf16[2,1296,128]{2,1,0:T(8,128)(2,1)} collective-permute-done((bf16[2,1296,128]{2,1,0:T(8,128)(2,1)}, bf16[2,1296,128]{2,1,0:T(8,128)(2,1)}, u32[]{:S(2)}, u32[]{:S(2)}) %collective-permute-start.14) | collective-permute-done | bytes 663584 | tf_op jit(solution)/shard_map/move_sums1/ppermute | solution.py:440
  144.8 1.3 collective-permute-start.17
  146.4 7.7 %blocks_4.1 = (f32[8,1296,128]{2,1,0:T(8,128)}, bf16[4,576,1536]{2,1,0:T(8,128)(2,1)}, bf16[2,1296,128]{2,1,0:T(8,128)(2,1)}) custom-call(s32[42]{0:T(128)} %dynamic-slice_bitcast_fusion.table, s32[4,4]{1,0:T(4,128)} %tile_map.13, f32[4,4]{1,0:T(4,128)} %gain_ref.13, f32[1,512]{1,0:T(1,128)} %bitcast.20, ...), custom_call_target="tpu_custom_call", output_to_operand_aliasing={{0}: (16, {}), {1}: (17, {})} | custom-call | flops 1048576 | bytes 65536 | tf_op jit(solution)/shard_map/blocks_4/pallas_call | solution.py:406
  154.2 1.3 collective-permute-start.19
  155.5 9.7 %blocks_5.1 = (f32[8,1296,128]{2,1,0:T(8,128)}, bf16[4,576,1536]{2,1,0:T(8,128)(2,1)}, bf16[3,1296,128]{2,1,0:T(8,128)(2,1)}) custom-call(s32[42]{0:T(128)} %dynamic-slice_bitcast_fusion.table, s32[4,4]{1,0:T(4,128)} %tile_map.13, f32[4,4]{1,0:T(4,128)} %gain_ref.13, f32[1,512]{1,0:T(1,128)} %bitcast.21, ...), custom_call_target="tpu_custom_call", output_to_operand_aliasing={{0}: (14, {}), {1}: (15, {})} | custom-call | flops 1048576 | bytes 65536 | tf_op jit(solution)/shard_map/blocks_5/pallas_call | solution.py:406
  165.2 11.8 %collective-permute-done.19.refs_3_ = bf16[2,1296,128]{2,1,0:T(8,128)(2,1)} collective-permute-done((bf16[2,1296,128]{2,1,0:T(8,128)(2,1)}, bf16[2,1296,128]{2,1,0:T(8,128)(2,1)}, u32[]{:S(2)}, u32[]{:S(2)}) %collective-permute-start.19) | collective-permute-done | bytes 663584 | tf_op jit(solution)/shard_map/move_sums3/ppermute | solution.py:440
  177.0 1.9 collective-permute-start.20
  179.0 7.7 %blocks_6.1 = (f32[8,1296,128]{2,1,0:T(8,128)}, bf16[4,576,1536]{2,1,0:T(8,128)(2,1)}) custom-call(s32[42]{0:T(128)} %dynamic-slice_bitcast_fusion.table, s32[4,4]{1,0:T(4,128)} %tile_map.13, f32[4,4]{1,0:T(4,128)} %gain_ref.13, f32[1,512]{1,0:T(1,128)} %bitcast.22, s32[1,512]{1,0:T(1,128)} %bitcast.29, ...), custom_call_target="tpu_custom_call", output_to_operand_aliasing={{0}: (6, {}), {1}: (7, {})} | custom-call | flops 1048576 | bytes 65536 | tf_op jit(solution)/shard_map/blocks_6/pallas_call | solution.py:406
  186.7 6.8 %collective-permute-done.20.refs_4_ = bf16[3,1296,128]{2,1,0:T(8,128)(2,1)} collective-permute-done((bf16[3,1296,128]{2,1,0:T(8,128)(2,1)}, bf16[3,1296,128]{2,1,0:T(8,128)(2,1)}, u32[]{:S(2)}, u32[]{:S(2)}) %collective-permute-start.20) | collective-permute-done | bytes 995360 | tf_op jit(solution)/shard_map/move_sums4/ppermute | solution.py:440
  193.5 6.0 %add_up.1 = f32[576,2,1152]{2,1,0:T(2,128)} custom-call(s32[42]{0:T(128)} %dynamic-slice_bitcast_fusion.table, f32[8,1296,128]{2,1,0:T(8,128)} %get-tuple-element.105.own, bf16[3,1296,128]{2,1,0:T(8,128)(2,1)} %collective-permute-done.11.refs_0_, bf16[2,1296,128]{2,1,0:T(8,128)(2,1)} %collective-permute-done.14.refs_1_, ...), custom_call_target="tpu_custom_call" | custom-call | tf_op jit(solution)/shard_map/add_up/pallas_call | solution.py:472
  (20 shorter events, 4.1 us)
Async XLA Ops:
  0.0 59.6 %collective-permute-start = (bf16[6,288,512]{2,1,0:T(8,128)(2,1)}, bf16[6,288,512]{2,1,0:T(8,128)(2,1)}, u32[]{:S(2)}, u32[]{:S(2)}) collective-permute-start(bf16[6,288,512]{2,1,0:T(8,128)(2,1)} %bitcast.6), channel_id=1, source_target_pairs={{2,0},{0,2},{6,4},{4,6},{10,8},{8,10},{14,12},{12,14},{18,16},{16,... | collective-permute-start | bytes 5308424 | tf_op jit(solution)/shard_map/move_a/ppermute | solution.py:382
  0.5 59.2 %collective-permute-start.1 = (bf16[6,288,512]{2,1,0:T(8,128)(2,1)}, bf16[6,288,512]{2,1,0:T(8,128)(2,1)}, u32[]{:S(2)}, u32[]{:S(2)}) collective-permute-start(bf16[6,288,512]{2,1,0:T(8,128)(2,1)} %bitcast.7), channel_id=1, source_target_pairs={{0,16},{10,26},{20,4},{30,14},{1,17},{11,27},{21,5},{31,15}} | collective-permute-start | bytes 5308424 | tf_op jit(solution)/shard_map/move_x0/ppermute | solution.py:382
  2.3 57.3 %collective-permute-start.2 = (bf16[6,288,512]{2,1,0:T(8,128)(2,1)}, bf16[6,288,512]{2,1,0:T(8,128)(2,1)}, u32[]{:S(2)}, u32[]{:S(2)}) collective-permute-start(bf16[6,288,512]{2,1,0:T(8,128)(2,1)} %bitcast.8), channel_id=1, source_target_pairs={{0,8},{10,2},{20,28},{30,22},{1,9},{11,3},{21,29},{31,23}} | collective-permute-start | bytes 5308424 | tf_op jit(solution)/shard_map/move_c0/ppermute | solution.py:382
  4.2 60.5 %collective-permute-start.3 = (bf16[6,288,512]{2,1,0:T(8,128)(2,1)}, bf16[6,288,512]{2,1,0:T(8,128)(2,1)}, u32[]{:S(2)}, u32[]{:S(2)}) collective-permute-start(bf16[6,288,512]{2,1,0:T(8,128)(2,1)} %bitcast.9), channel_id=1, source_target_pairs={{4,2},{2,4},{12,10},{10,12},{20,18},{18,20},{28,26},{26,28},{6,0},... | collective-permute-start | bytes 5308424 | tf_op jit(solution)/shard_map/move_b/ppermute | solution.py:382
  59.6 7.8 %collective-permute-start.4 = (bf16[6,288,512]{2,1,0:T(8,128)(2,1)}, bf16[6,288,512]{2,1,0:T(8,128)(2,1)}, u32[]{:S(2)}, u32[]{:S(2)}) collective-permute-start(bf16[6,288,512]{2,1,0:T(8,128)(2,1)} %collective-permute-done.refs_0_), channel_id=1, source_target_pairs={{0,16},{10,26},{20,4},{30,14},{1,17},{11,27},{21,5},{31,15}} | collective-permute-start | bytes 5308424 | tf_op jit(solution)/shard_map/move_xa/ppermute | solution.py:382
  61.5 5.9 %collective-permute-start.5 = (bf16[6,288,512]{2,1,0:T(8,128)(2,1)}, bf16[6,288,512]{2,1,0:T(8,128)(2,1)}, u32[]{:S(2)}, u32[]{:S(2)}) collective-permute-start(bf16[6,288,512]{2,1,0:T(8,128)(2,1)} %collective-permute-done.refs_0_), channel_id=1, source_target_pairs={{0,8},{10,2},{20,28},{30,22},{1,9},{11,3},{21,29},{31,23}} | collective-permute-start | bytes 5308424 | tf_op jit(solution)/shard_map/move_ca/ppermute | solution.py:382
  63.4 5.9 %collective-permute-start.6 = (bf16[6,288,512]{2,1,0:T(8,128)(2,1)}, bf16[6,288,512]{2,1,0:T(8,128)(2,1)}, u32[]{:S(2)}, u32[]{:S(2)}) collective-permute-start(bf16[6,288,512]{2,1,0:T(8,128)(2,1)} %collective-permute-done.1.refs_7_.refs_6_.refs_10_.refs_11_), channel_id=1, source_target_pairs={{16,24},{26,18},{4,12},{14,6},{17,25},{27,19},{5,13},{15,7}} | collective-permute-start | bytes 5308424 | tf_op jit(solution)/shard_map/move_d0/ppermute | solution.py:382
  69.3 3.8 %collective-permute-start.7 = (bf16[6,288,512]{2,1,0:T(8,128)(2,1)}, bf16[6,288,512]{2,1,0:T(8,128)(2,1)}, u32[]{:S(2)}, u32[]{:S(2)}) collective-permute-start(bf16[6,288,512]{2,1,0:T(8,128)(2,1)} %collective-permute-done.3.second_ref.refs_1_), channel_id=1, source_target_pairs={{0,8},{10,2},{20,28},{30,22},{1,9},{11,3},{21,29},{31,23}} | collective-permute-start | bytes 5308424 | tf_op jit(solution)/shard_map/move_cb/ppermute | solution.py:382
  71.2 9.8 %collective-permute-start.9 = (bf16[6,288,512]{2,1,0:T(8,128)(2,1)}, bf16[6,288,512]{2,1,0:T(8,128)(2,1)}, u32[]{:S(2)}, u32[]{:S(2)}) collective-permute-start(bf16[6,288,512]{2,1,0:T(8,128)(2,1)} %collective-permute-done.3.second_ref.refs_1_), channel_id=1, source_target_pairs={{0,16},{10,26},{20,4},{30,14},{1,17},{11,27},{21,5},{31,15}} | collective-permute-start | bytes 5308424 | tf_op jit(solution)/shard_map/move_xb/ppermute | solution.py:382
  73.1 40.7 %collective-permute-start.12 = (bf16[6,288,512]{2,1,0:T(8,128)(2,1)}, bf16[6,288,512]{2,1,0:T(8,128)(2,1)}, u32[]{:S(2)}, u32[]{:S(2)}) collective-permute-start(bf16[6,288,512]{2,1,0:T(8,128)(2,1)} %pick.1), channel_id=1, source_target_pairs={{2,0},{6,2},{0,4},{4,6},{10,8},{14,10},{8,12},{12,14},{18,16},{22,... | collective-permute-start | bytes 5308424 | tf_op jit(solution)/shard_map/move_t/ppermute | solution.py:382
  81.0 32.8 %collective-permute-start.11 = (bf16[3,1296,128]{2,1,0:T(8,128)(2,1)}, bf16[3,1296,128]{2,1,0:T(8,128)(2,1)}, u32[]{:S(2)}, u32[]{:S(2)}) collective-permute-start(bf16[3,1296,128]{2,1,0:T(8,128)(2,1)} %get-tuple-element.76), channel_id=1, source_target_pairs={{0,1},{1,0},{2,3},{3,2},{4,5},{5,4},{6,7},{9,8},{10,11},{11,10},{1... | collective-permute-start | bytes 2985992 | tf_op jit(solution)/shard_map/move_sums0/ppermute | solution.py:440
  85.6 33.3 %collective-permute-start.8 = (bf16[6,288,512]{2,1,0:T(8,128)(2,1)}, bf16[6,288,512]{2,1,0:T(8,128)(2,1)}, u32[]{:S(2)}, u32[]{:S(2)}) collective-permute-start(bf16[6,288,512]{2,1,0:T(8,128)(2,1)} %collective-permute-done.4.refs_8_.refs_7_.refs_11_.refs_12_), channel_id=1, source_target_pairs={{16,24},{26,18},{4,12},{14,6},{17,25},{27,19},{5,13},{15,7}} | collective-permute-start | bytes 5308424 | tf_op jit(solution)/shard_map/move_da/ppermute | solution.py:382
  86.9 32.0 %collective-permute-start.10 = (bf16[6,288,512]{2,1,0:T(8,128)(2,1)}, bf16[6,288,512]{2,1,0:T(8,128)(2,1)}, u32[]{:S(2)}, u32[]{:S(2)}) collective-permute-start(bf16[6,288,512]{2,1,0:T(8,128)(2,1)} %collective-permute-done.9.refs_8_.refs_12_.refs_13_), channel_id=1, source_target_pairs={{16,24},{26,18},{4,12},{14,6},{17,25},{27,19},{5,13},{15,7}} | collective-permute-start | bytes 5308424 | tf_op jit(solution)/shard_map/move_db/ppermute | solution.py:382
  113.8 14.6 %collective-permute-start.13 = (bf16[6,288,512]{2,1,0:T(8,128)(2,1)}, bf16[6,288,512]{2,1,0:T(8,128)(2,1)}, u32[]{:S(2)}, u32[]{:S(2)}) collective-permute-start(bf16[6,288,512]{2,1,0:T(8,128)(2,1)} %collective-permute-done.12.refs_9_.refs_10_), channel_id=1, source_target_pairs={{0,8},{10,2},{20,28},{30,22},{1,9},{11,3},{21,29},{31,23}} | collective-permute-start | bytes 5308424 | tf_op jit(solution)/shard_map/move_ct/ppermute | solution.py:382
  115.7 25.7 %collective-permute-start.15 = (bf16[6,288,512]{2,1,0:T(8,128)(2,1)}, bf16[6,288,512]{2,1,0:T(8,128)(2,1)}, u32[]{:S(2)}, u32[]{:S(2)}) collective-permute-start(bf16[6,288,512]{2,1,0:T(8,128)(2,1)} %collective-permute-done.12.refs_9_.refs_10_), channel_id=1, source_target_pairs={{0,16},{10,26},{20,4},{30,14},{1,17},{11,27},{21,5},{31,15}} | collective-permute-start | bytes 5308424 | tf_op jit(solution)/shard_map/move_xt/ppermute | solution.py:382
  117.6 24.7 %collective-permute-start.16 = (bf16[6,288,512]{2,1,0:T(8,128)(2,1)}, bf16[6,288,512]{2,1,0:T(8,128)(2,1)}, u32[]{:S(2)}, u32[]{:S(2)}) collective-permute-start(bf16[6,288,512]{2,1,0:T(8,128)(2,1)} %collective-permute-done.12.refs_9_.refs_10_), channel_id=1, source_target_pairs={{4,6},{10,8},{20,22},{26,24},{5,7},{11,9},{21,23},{27,25}} | collective-permute-start | bytes 5308424 | tf_op jit(solution)/shard_map/move_e/ppermute | solution.py:382
  128.4 16.4 %collective-permute-start.14 = (bf16[2,1296,128]{2,1,0:T(8,128)(2,1)}, bf16[2,1296,128]{2,1,0:T(8,128)(2,1)}, u32[]{:S(2)}, u32[]{:S(2)}) collective-permute-start(bf16[2,1296,128]{2,1,0:T(8,128)(2,1)} %get-tuple-element.89), channel_id=1, source_target_pairs={{0,1},{1,0},{2,3},{3,2},{4,5},{5,4},{6,7},{7,6},{8,9},{9,8},{10,11... | collective-permute-start | bytes 1990664 | tf_op jit(solution)/shard_map/move_sums1/ppermute | solution.py:440
  144.8 9.4 %collective-permute-start.17 = (bf16[6,288,512]{2,1,0:T(8,128)(2,1)}, bf16[6,288,512]{2,1,0:T(8,128)(2,1)}, u32[]{:S(2)}, u32[]{:S(2)}) collective-permute-start(bf16[6,288,512]{2,1,0:T(8,128)(2,1)} %collective-permute-done.15.refs_10_.refs_8_), channel_id=1, source_target_pairs={{16,24},{26,18},{4,12},{14,6},{17,25},{27,19},{5,13},{15,7}} | collective-permute-start | bytes 5308424 | tf_op jit(solution)/shard_map/move_dt/ppermute | solution.py:382
  146.1 19.1 %collective-permute-start.18 = (bf16[2,1296,128]{2,1,0:T(8,128)(2,1)}, bf16[2,1296,128]{2,1,0:T(8,128)(2,1)}, u32[]{:S(2)}, u32[]{:S(2)}) collective-permute-start(bf16[2,1296,128]{2,1,0:T(8,128)(2,1)} %get-tuple-element.101), channel_id=1, source_target_pairs={{0,1},{1,0},{2,3},{3,2},{4,5},{5,4},{6,7},{7,6},{8,9},{9,8},{10,11... | collective-permute-start | bytes 1990664 | tf_op jit(solution)/shard_map/move_sums2/ppermute | solution.py:440
  154.2 22.9 %collective-permute-start.19 = (bf16[2,1296,128]{2,1,0:T(8,128)(2,1)}, bf16[2,1296,128]{2,1,0:T(8,128)(2,1)}, u32[]{:S(2)}, u32[]{:S(2)}) collective-permute-start(bf16[2,1296,128]{2,1,0:T(8,128)(2,1)} %get-tuple-element.102), channel_id=1, source_target_pairs={{0,1},{1,0},{2,3},{3,2},{4,5},{5,4},{7,6},{8,9},{9,8},{10,11},{11,... | collective-permute-start | bytes 1990664 | tf_op jit(solution)/shard_map/move_sums3/ppermute | solution.py:440
  177.0 16.4 %collective-permute-start.20 = (bf16[3,1296,128]{2,1,0:T(8,128)(2,1)}, bf16[3,1296,128]{2,1,0:T(8,128)(2,1)}, u32[]{:S(2)}, u32[]{:S(2)}) collective-permute-start(bf16[3,1296,128]{2,1,0:T(8,128)(2,1)} %get-tuple-element.110), channel_id=1, source_target_pairs={{6,7},{7,6},{8,9},{12,13},{13,12},{18,19},{19,18},{23,22},{24,25},... | collective-permute-start | bytes 2985992 | tf_op jit(solution)/shard_map/move_sums4/ppermute | solution.py:440
